TPU v7x, 256 devices: a whole 4x4x8 slice. The times are simulated.
256 devices in a mesh: ctx: 32 (over z, y_lo, core), grp: 8 (over y_hi, x).
Axes of the slice: x: 4, y: 4 (y_hi: 2, y_lo: 2; y = y_hi * 2 + y_lo), z: 8, core: 2. Of those that a mesh axis runs over, the one named last changes fastest.
Arguments:
- queries: bfloat16 [16384, 4096], P('ctx', 'grp'), may hold values from -6 to 6
- key_rows: bfloat16 [16384, 1024], P('ctx', 'grp'), may hold values from -6 to 6
- value_rows: bfloat16 [16384, 1024], P('ctx', 'grp'), may hold values from -6 to 6
- output_rows: bfloat16 [16384, 4096], P('ctx', 'grp'), may hold values from -6 to 6
- output_grad: bfloat16 [16384, 4096], P('ctx', 'grp'), may hold values from -6 to 6
- log_normalizer: float32 [16384, 32], P('ctx', 'grp'), may hold values from 4 to 6
- selection: int32 [32, 3], replicated, may hold values from 0 to 30, as said below
- query_weight: bfloat16 [4096, 4096], P(None, 'grp'), may hold values from -0.09375 to 0.09375
- key_weight: bfloat16 [4096, 1024], P(None, 'grp'), may hold values from -0.09375 to 0.09375
- value_weight: bfloat16 [4096, 1024], P(None, 'grp'), may hold values from -0.09375 to 0.09375
Outputs:
- input_grad: bfloat16 [16384, 4096], P('ctx', 'grp')
Inputs may be any that keep to these rules, and one draw needn't show every extreme that they name: `selection`: row b names the 3 blocks chosen for query block b: distinct blocks below b, among them always block b - 1; a row with fewer than 3 blocks below it names all of them and repeats b itself in the remaining places.
All inputs are finite; a program needn't handle non-finite values.
Results may differ from a plain program's by a relative error of at most 0.019.
Values may be sent and summed in bfloat16 or wider, within the bound.
No kernel may reach another device: no remote copies, remote signals or barrier semaphores. Data moves between devices by JAX's collectives and lax.ppermute only.
A program may use at most 128 MiB of HBM per device.

v0:
```python
import jax
import jax.numpy as jnp
from jax import lax
from jax.sharding import PartitionSpec as P

HD = 128
BLOCK = 512
TOPK = 3


def shifted(block, axis, distance):
    devices = range(lax.axis_size(axis))
    route = [(i - distance, i) for i in devices if i - distance in devices]
    return lax.ppermute(block, axis, route)


def shifted_2(value, axis, steps):
    count = lax.axis_size(axis)
    pairs = [(source, (source + steps) % count) for source in range(count)]
    return lax.ppermute(value, axis, pairs)


def pair_mask(query_anchor, key_anchor, row_count, picked):
    offsets = jnp.arange(row_count, dtype=jnp.int32)
    query_pos = query_anchor * row_count + offsets
    key_pos = key_anchor * row_count + offsets
    query_block = query_pos // BLOCK
    key_block = key_pos // BLOCK
    causal = (query_block[:, None] == key_block[None, :]) & (key_pos[None, :] <= query_pos[:, None])
    block_ids = jnp.arange(picked.shape[0], dtype=jnp.int32)
    query_onehot = (query_block[:, None] == block_ids[None, :]).astype(jnp.float32)
    key_onehot = (key_block[:, None] == block_ids[None, :]).astype(jnp.float32)
    chosen = jnp.dot(jnp.dot(query_onehot, picked), key_onehot.T) > 0.5
    return causal | chosen


def gradients(query_side, key_side, allowed):
    query_in, grad_in, norm_in, delta_in = query_side
    key_in, value_in = key_side
    query_count = query_in.shape[0]
    key_count = key_in.shape[0]
    groups = key_in.shape[1] // HD
    per_group = query_in.shape[1] // (HD * groups)
    scaling = float(HD) ** (-0.5)
    query_heads = query_in.reshape(query_count, groups, per_group, HD)
    grad_heads = grad_in.reshape(query_count, groups, per_group, HD)
    key_heads = key_in.reshape(key_count, groups, HD)
    value_heads = value_in.reshape(key_count, groups, HD)
    norm_heads = norm_in.reshape(query_count, groups, per_group).transpose(1, 2, 0)[:, :, :, None]
    delta_heads = delta_in.reshape(query_count, groups, per_group).transpose(1, 2, 0)[:, :, :, None]
    scores = (
        jnp.einsum("qgpd,kgd->gpqk", query_heads, key_heads, preferred_element_type=jnp.float32)
        * scaling
    )
    probs = jnp.where(allowed[None, None], jnp.exp(scores - norm_heads), 0.0)
    prob_grad = jnp.einsum(
        "qgpd,kgd->gpqk", grad_heads, value_heads, preferred_element_type=jnp.float32
    )
    score_grad = probs * (prob_grad - delta_heads)
    probs_half = probs.astype(jnp.bfloat16)
    score_half = score_grad.astype(jnp.bfloat16)
    value_part = jnp.einsum(
        "gpqk,qgpd->kgd", probs_half, grad_heads, preferred_element_type=jnp.float32
    ).reshape(key_count, -1)
    key_part = jnp.einsum(
        "gpqk,qgpd->kgd", score_half, query_heads, preferred_element_type=jnp.float32
    ).reshape(key_count, -1)
    query_part = jnp.einsum(
        "gpqk,kgd->qgpd", score_half, key_heads, preferred_element_type=jnp.float32
    ).reshape(query_count, -1)
    return (query_part, key_part, value_part)


def guarded(query_side, key_side, allowed):

    def skipped():
        return (
            jnp.zeros(query_side[0].shape, jnp.float32),
            jnp.zeros(key_side[0].shape, jnp.float32),
            jnp.zeros(key_side[1].shape, jnp.float32),
        )

    return lax.cond(jnp.any(allowed), lambda: gradients(query_side, key_side, allowed), skipped)


def on_device(
    queries,
    key_rows,
    value_rows,
    output_rows,
    output_grad,
    log_normalizer,
    selection,
    query_weight,
    key_weight,
    value_weight,
):
    scaling = float(HD) ** (-0.5)
    row_count = queries.shape[0]
    head_count = queries.shape[1] // HD
    cycle_size = lax.axis_size("ctx")
    position = lax.axis_index("ctx")
    block_count = selection.shape[0]
    row_delta = jnp.sum(
        (output_rows.astype(jnp.float32) * output_grad.astype(jnp.float32)).reshape(
            row_count, head_count, HD
        ),
        axis=-1,
    )
    block_ids = jnp.arange(block_count, dtype=jnp.int32)
    picked = jnp.zeros((block_count, block_count), jnp.float32)
    for column in range(TOPK):
        picked = jnp.maximum(
            picked, (selection[:, column][:, None] == block_ids[None, :]).astype(jnp.float32)
        )
    picked = jnp.where(block_ids[None, :] < block_ids[:, None], picked, 0.0)
    query_side = (queries, output_grad, log_normalizer, row_delta)

    def key_turn(turn_index, state):
        travel_key, travel_value, key_total, value_total, query_total = state
        anchor = position - turn_index
        allowed = pair_mask(position, anchor, row_count, picked)
        query_part, key_part, value_part = guarded(query_side, (travel_key, travel_value), allowed)
        return (
            travel_key,
            travel_value,
            key_total + key_part,
            value_total + value_part,
            query_total + query_part,
        )

    def key_step(turn_index, state):
        state = key_turn(turn_index, state)
        travel_key, travel_value = shifted((state[0], state[1]), "ctx", 1)
        key_total, value_total = (
            shifted_2(state[2].astype(jnp.bfloat16), "ctx", 1).astype(jnp.float32),
            shifted_2(state[3].astype(jnp.bfloat16), "ctx", 1).astype(jnp.float32),
        )
        return (travel_key, travel_value, key_total, value_total, state[4])

    key_zero = jnp.zeros(key_rows.shape, jnp.float32)
    state = (key_rows, value_rows, key_zero, key_zero, jnp.zeros(queries.shape, jnp.float32))
    state = lax.fori_loop(0, cycle_size - 1, key_step, state)
    state = key_turn(cycle_size - 1, state)
    key_total, value_total = (
        shifted_2(state[2].astype(jnp.bfloat16), "ctx", 1).astype(jnp.float32),
        shifted_2(state[3].astype(jnp.bfloat16), "ctx", 1).astype(jnp.float32),
    )
    query_total = state[4]
    grad_query = (query_total * scaling).astype(jnp.bfloat16)
    grad_key = (key_total * scaling).astype(jnp.bfloat16)
    grad_value = value_total.astype(jnp.bfloat16)
    contract = (((1,), (1,)), ((), ()))
    combined = lax.dot_general(
        grad_query, query_weight, contract, preferred_element_type=jnp.float32
    )
    combined = combined + lax.dot_general(
        grad_key, key_weight, contract, preferred_element_type=jnp.float32
    )
    combined = combined + lax.dot_general(
        grad_value, value_weight, contract, preferred_element_type=jnp.float32
    )
    return lax.psum_scatter(combined.astype(jnp.bfloat16), "grp", scatter_dimension=1, tiled=True)


def solution(mesh):
    return jax.shard_map(
        on_device,
        mesh=mesh,
        in_specs=(
            P("ctx", "grp"),
            P("ctx", "grp"),
            P("ctx", "grp"),
            P("ctx", "grp"),
            P("ctx", "grp"),
            P("ctx", "grp"),
            P(),
            P(None, "grp"),
            P(None, "grp"),
            P(None, "grp"),
        ),
        out_specs=P("ctx", "grp"),
        check_vma=False,
    )
```

profile of v0, /device:TPU:24, one launch (start us, length us, event | category | flops | bytes accessed | tf_op | source)
XLA Modules:
  0.0 878.2 jit_solution(10959652391402996775)
XLA Ops:
  17.9 746.2 %while.25 = (s32[]{:T(128)}, bf16[512,128]{0,1:T(8,128)(2,1)S(1)}, bf16[512,128]{1,0:T(8,128)(2,1)}, f32[512,128]{1,0:T(8,128)}, f32[512,128]{1,0:T(8,128)}, /*i...) while((s32[]{:T(128)}, bf16[512,128]{0,1:T(8,128)(2,1)S(1)}, ...), condition=%wide.region_5.6_spmd.clone, body=%wide.region_1.5_spmd.clone.sunk | while | flops 1373170688 | bytes 38478772 | solution.py:143
  29.3 9.6 %conditional.5 = (f32[512,512]{0,1:T(8,128)S(1)}, f32[512,128]{1,0:T(8,128)}, f32[512,128]{1,0:T(8,128)S(1)}) conditional(s32[]{:T(128)} %convert_element_type.224, () %tuple.85, (pred[512,512]{1,0:T(8,128)(4,1)}, bf16[512,512]{1,0:T(8,128)(2,1)}, bf16[512,128]{0,1:T(8,128)(2,1)}, f32[512,4]{0,1:T(4,128)}, bf16[512,512]{1,0:T(8,128)(2,1)}, ...), branch_computations={%region_3.3_spmd, %region_4.4_spmd} | conditional | flops 1352663040 | bytes 30335112 | solution.py:83
  58.2 9.6 %conditional.5 = (f32[512,512]{0,1:T(8,128)S(1)}, f32[512,128]{1,0:T(8,128)}, f32[512,128]{1,0:T(8,128)S(1)}) conditional(s32[]{:T(128)} %convert_element_type.224, () %tuple.85, (pred[512,512]{1,0:T(8,128)(4,1)}, bf16[512,512]{1,0:T(8,128)(2,1)}, bf16[512,128]{0,1:T(8,128)(2,1)}, f32[512,4]{0,1:T(4,128)}, bf16[512,512]{1,0:T(8,128)(2,1)}, ...), branch_computations={%region_3.3_spmd, %region_4.4_spmd} | conditional | flops 1352663040 | bytes 30335112 | solution.py:83
  88.0 9.6 %conditional.5 = (f32[512,512]{0,1:T(8,128)S(1)}, f32[512,128]{1,0:T(8,128)}, f32[512,128]{1,0:T(8,128)S(1)}) conditional(s32[]{:T(128)} %convert_element_type.224, () %tuple.85, (pred[512,512]{1,0:T(8,128)(4,1)}, bf16[512,512]{1,0:T(8,128)(2,1)}, bf16[512,128]{0,1:T(8,128)(2,1)}, f32[512,4]{0,1:T(4,128)}, bf16[512,512]{1,0:T(8,128)(2,1)}, ...), branch_computations={%region_3.3_spmd, %region_4.4_spmd} | conditional | flops 1352663040 | bytes 30335112 | solution.py:83
  120.4 8.8 collective-permute-start.3
  193.3 9.1 %collective-permute-start.2 = (bf16[512,128]{1,0:T(8,128)(2,1)}, bf16[512,128]{1,0:T(8,128)(2,1)S(1)}, u32[]{:S(2)}, u32[]{:S(2)}) collective-permute-start(bf16[512,128]{1,0:T(8,128)(2,1)} %fusion.172), channel_id=1, source_target_pairs={{0,8},{8,16},{16,24},{24,32},{32,40},{40,48},{48,56},{56,64},{64,7... | collective-permute-start | bytes 393224 | tf_op jit(solution)/shard_map/while/body/eval_jaxpr/ppermute | solution.py:20
  211.6 12.8 %collective-permute-start.1 = (bf16[512,128]{1,0:T(8,128)(2,1)}, bf16[512,128]{1,0:T(8,128)(2,1)}, u32[]{:S(2)}, u32[]{:S(2)}) collective-permute-start(bf16[512,128]{1,0:T(8,128)(2,1)} %copy.99), channel_id=1, source_target_pairs={{0,8},{8,16},{16,24},{24,32},{32,40},{40,48},{48,56},{56,64},{64,7... | collective-permute-start | bytes 393224 | tf_op jit(solution)/shard_map/while/body/eval_jaxpr/ppermute | solution.py:14
  242.4 5.1 collective-permute-start.1
  324.5 5.1 collective-permute-start.1
  356.8 6.6 collective-permute-start.2
  372.7 5.1 collective-permute-start.1
  394.7 5.1 collective-permute-start.1
  416.8 5.1 collective-permute-start.1
  438.9 14.5 %collective-permute-start.1 = (bf16[512,128]{1,0:T(8,128)(2,1)}, bf16[512,128]{1,0:T(8,128)(2,1)}, u32[]{:S(2)}, u32[]{:S(2)}) collective-permute-start(bf16[512,128]{1,0:T(8,128)(2,1)} %copy.99), channel_id=1, source_target_pairs={{0,8},{8,16},{16,24},{24,32},{32,40},{40,48},{48,56},{56,64},{64,7... | collective-permute-start | bytes 393224 | tf_op jit(solution)/shard_map/while/body/eval_jaxpr/ppermute | solution.py:14
  474.7 5.1 collective-permute-start.1
  494.5 6.2 collective-permute-start
  502.3 5.1 collective-permute-start.1
  525.6 5.1 collective-permute-start.1
  547.7 5.1 collective-permute-start.1
  569.8 5.1 collective-permute-start.1
  698.5 5.1 collective-permute-start.1
  721.8 5.1 collective-permute-start.1
  744.9 5.1 collective-permute-start.1
  778.3 93.1 %reduce-scatter.2.cloned.1.call-done = bf16[512,512]{1,0:T(8,128)(2,1)} async-done(((bf16[512,4096]{1,0:T(8,128)(2,1)}), bf16[512,512]{1,0:T(8,128)(2,1)}) %reduce-scatter.2.cloned.1.call-update) | async-done | bytes 524304 | tf_op jit(solution)/shard_map/reduce_scatter | solution.py:163
  (733 shorter events, 649.8 us)
Async XLA Ops:
  6.5 864.8 %reduce-scatter.2.cloned.1.call-start = ((), (), s32[]{:S(2)}) async-start(), calls=%async_computation.1 | async-start | bytes 4718592 | tf_op jit(solution)/shard_map/reduce_scatter | solution.py:163
  18.5 28.1 %collective-permute-start = (bf16[512,128]{0,1:T(8,128)(2,1)}, bf16[512,128]{0,1:T(8,128)(2,1)S(1)}, u32[]{:S(2)}, u32[]{:S(2)}) collective-permute-start(bf16[512,128]{0,1:T(8,128)(2,1)} %copy.98), channel_id=1, source_target_pairs={{0,8},{8,16},{16,24},{24,32},{32,40},{40,48},{48,56},{56,64},{64,7... | collective-permute-start | bytes 393224 | tf_op jit(solution)/shard_map/while/body/eval_jaxpr/ppermute | solution.py:14
  22.0 24.7 %collective-permute-start.1 = (bf16[512,128]{1,0:T(8,128)(2,1)}, bf16[512,128]{1,0:T(8,128)(2,1)}, u32[]{:S(2)}, u32[]{:S(2)}) collective-permute-start(bf16[512,128]{1,0:T(8,128)(2,1)} %copy.99), channel_id=1, source_target_pairs={{0,8},{8,16},{16,24},{24,32},{32,40},{40,48},{48,56},{56,64},{64,7... | collective-permute-start | bytes 393224 | tf_op jit(solution)/shard_map/while/body/eval_jaxpr/ppermute | solution.py:14
  47.3 29.2 %collective-permute-start = (bf16[512,128]{0,1:T(8,128)(2,1)}, bf16[512,128]{0,1:T(8,128)(2,1)S(1)}, u32[]{:S(2)}, u32[]{:S(2)}) collective-permute-start(bf16[512,128]{0,1:T(8,128)(2,1)} %copy.98), channel_id=1, source_target_pairs={{0,8},{8,16},{16,24},{24,32},{32,40},{40,48},{48,56},{56,64},{64,7... | collective-permute-start | bytes 393224 | tf_op jit(solution)/shard_map/while/body/eval_jaxpr/ppermute | solution.py:14
  50.8 25.8 %collective-permute-start.1 = (bf16[512,128]{1,0:T(8,128)(2,1)}, bf16[512,128]{1,0:T(8,128)(2,1)}, u32[]{:S(2)}, u32[]{:S(2)}) collective-permute-start(bf16[512,128]{1,0:T(8,128)(2,1)} %copy.99), channel_id=1, source_target_pairs={{0,8},{8,16},{16,24},{24,32},{32,40},{40,48},{48,56},{56,64},{64,7... | collective-permute-start | bytes 393224 | tf_op jit(solution)/shard_map/while/body/eval_jaxpr/ppermute | solution.py:14
  77.2 29.1 %collective-permute-start = (bf16[512,128]{0,1:T(8,128)(2,1)}, bf16[512,128]{0,1:T(8,128)(2,1)S(1)}, u32[]{:S(2)}, u32[]{:S(2)}) collective-permute-start(bf16[512,128]{0,1:T(8,128)(2,1)} %copy.98), channel_id=1, source_target_pairs={{0,8},{8,16},{16,24},{24,32},{32,40},{40,48},{48,56},{56,64},{64,7... | collective-permute-start | bytes 393224 | tf_op jit(solution)/shard_map/while/body/eval_jaxpr/ppermute | solution.py:14
  80.7 25.7 %collective-permute-start.1 = (bf16[512,128]{1,0:T(8,128)(2,1)}, bf16[512,128]{1,0:T(8,128)(2,1)}, u32[]{:S(2)}, u32[]{:S(2)}) collective-permute-start(bf16[512,128]{1,0:T(8,128)(2,1)} %copy.99), channel_id=1, source_target_pairs={{0,8},{8,16},{16,24},{24,32},{32,40},{40,48},{48,56},{56,64},{64,7... | collective-permute-start | bytes 393224 | tf_op jit(solution)/shard_map/while/body/eval_jaxpr/ppermute | solution.py:14
  107.0 29.2 %collective-permute-start = (bf16[512,128]{0,1:T(8,128)(2,1)}, bf16[512,128]{0,1:T(8,128)(2,1)S(1)}, u32[]{:S(2)}, u32[]{:S(2)}) collective-permute-start(bf16[512,128]{0,1:T(8,128)(2,1)} %copy.98), channel_id=1, source_target_pairs={{0,8},{8,16},{16,24},{24,32},{32,40},{40,48},{48,56},{56,64},{64,7... | collective-permute-start | bytes 393224 | tf_op jit(solution)/shard_map/while/body/eval_jaxpr/ppermute | solution.py:14
  110.5 25.8 %collective-permute-start.1 = (bf16[512,128]{1,0:T(8,128)(2,1)}, bf16[512,128]{1,0:T(8,128)(2,1)}, u32[]{:S(2)}, u32[]{:S(2)}) collective-permute-start(bf16[512,128]{1,0:T(8,128)(2,1)} %copy.99), channel_id=1, source_target_pairs={{0,8},{8,16},{16,24},{24,32},{32,40},{40,48},{48,56},{56,64},{64,7... | collective-permute-start | bytes 393224 | tf_op jit(solution)/shard_map/while/body/eval_jaxpr/ppermute | solution.py:14
  179.5 24.7 %collective-permute-start = (bf16[512,128]{0,1:T(8,128)(2,1)}, bf16[512,128]{0,1:T(8,128)(2,1)S(1)}, u32[]{:S(2)}, u32[]{:S(2)}) collective-permute-start(bf16[512,128]{0,1:T(8,128)(2,1)} %copy.98), channel_id=1, source_target_pairs={{0,8},{8,16},{16,24},{24,32},{32,40},{40,48},{48,56},{56,64},{64,7... | collective-permute-start | bytes 393224 | tf_op jit(solution)/shard_map/while/body/eval_jaxpr/ppermute | solution.py:14
  204.9 33.4 %collective-permute-start = (bf16[512,128]{0,1:T(8,128)(2,1)}, bf16[512,128]{0,1:T(8,128)(2,1)S(1)}, u32[]{:S(2)}, u32[]{:S(2)}) collective-permute-start(bf16[512,128]{0,1:T(8,128)(2,1)} %copy.98), channel_id=1, source_target_pairs={{0,8},{8,16},{16,24},{24,32},{32,40},{40,48},{48,56},{56,64},{64,7... | collective-permute-start | bytes 393224 | tf_op jit(solution)/shard_map/while/body/eval_jaxpr/ppermute | solution.py:14
  211.6 26.7 %collective-permute-start.1 = (bf16[512,128]{1,0:T(8,128)(2,1)}, bf16[512,128]{1,0:T(8,128)(2,1)}, u32[]{:S(2)}, u32[]{:S(2)}) collective-permute-start(bf16[512,128]{1,0:T(8,128)(2,1)} %copy.99), channel_id=1, source_target_pairs={{0,8},{8,16},{16,24},{24,32},{32,40},{40,48},{48,56},{56,64},{64,7... | collective-permute-start | bytes 393224 | tf_op jit(solution)/shard_map/while/body/eval_jaxpr/ppermute | solution.py:14
  321.0 21.4 %collective-permute-start = (bf16[512,128]{0,1:T(8,128)(2,1)}, bf16[512,128]{0,1:T(8,128)(2,1)S(1)}, u32[]{:S(2)}, u32[]{:S(2)}) collective-permute-start(bf16[512,128]{0,1:T(8,128)(2,1)} %copy.98), channel_id=1, source_target_pairs={{0,8},{8,16},{16,24},{24,32},{32,40},{40,48},{48,56},{56,64},{64,7... | collective-permute-start | bytes 393224 | tf_op jit(solution)/shard_map/while/body/eval_jaxpr/ppermute | solution.py:14
  343.1 22.2 %collective-permute-start = (bf16[512,128]{0,1:T(8,128)(2,1)}, bf16[512,128]{0,1:T(8,128)(2,1)S(1)}, u32[]{:S(2)}, u32[]{:S(2)}) collective-permute-start(bf16[512,128]{0,1:T(8,128)(2,1)} %copy.98), channel_id=1, source_target_pairs={{0,8},{8,16},{16,24},{24,32},{32,40},{40,48},{48,56},{56,64},{64,7... | collective-permute-start | bytes 393224 | tf_op jit(solution)/shard_map/while/body/eval_jaxpr/ppermute | solution.py:14
  366.0 24.6 %collective-permute-start = (bf16[512,128]{0,1:T(8,128)(2,1)}, bf16[512,128]{0,1:T(8,128)(2,1)S(1)}, u32[]{:S(2)}, u32[]{:S(2)}) collective-permute-start(bf16[512,128]{0,1:T(8,128)(2,1)} %copy.98), channel_id=1, source_target_pairs={{0,8},{8,16},{16,24},{24,32},{32,40},{40,48},{48,56},{56,64},{64,7... | collective-permute-start | bytes 393224 | tf_op jit(solution)/shard_map/while/body/eval_jaxpr/ppermute | solution.py:14
  413.4 21.4 %collective-permute-start = (bf16[512,128]{0,1:T(8,128)(2,1)}, bf16[512,128]{0,1:T(8,128)(2,1)S(1)}, u32[]{:S(2)}, u32[]{:S(2)}) collective-permute-start(bf16[512,128]{0,1:T(8,128)(2,1)} %copy.98), channel_id=1, source_target_pairs={{0,8},{8,16},{16,24},{24,32},{32,40},{40,48},{48,56},{56,64},{64,7... | collective-permute-start | bytes 393224 | tf_op jit(solution)/shard_map/while/body/eval_jaxpr/ppermute | solution.py:14
  435.5 35.1 %collective-permute-start = (bf16[512,128]{0,1:T(8,128)(2,1)}, bf16[512,128]{0,1:T(8,128)(2,1)S(1)}, u32[]{:S(2)}, u32[]{:S(2)}) collective-permute-start(bf16[512,128]{0,1:T(8,128)(2,1)} %copy.98), channel_id=1, source_target_pairs={{0,8},{8,16},{16,24},{24,32},{32,40},{40,48},{48,56},{56,64},{64,7... | collective-permute-start | bytes 393224 | tf_op jit(solution)/shard_map/while/body/eval_jaxpr/ppermute | solution.py:14
  438.9 31.6 %collective-permute-start.1 = (bf16[512,128]{1,0:T(8,128)(2,1)}, bf16[512,128]{1,0:T(8,128)(2,1)}, u32[]{:S(2)}, u32[]{:S(2)}) collective-permute-start(bf16[512,128]{1,0:T(8,128)(2,1)} %copy.99), channel_id=1, source_target_pairs={{0,8},{8,16},{16,24},{24,32},{32,40},{40,48},{48,56},{56,64},{64,7... | collective-permute-start | bytes 393224 | tf_op jit(solution)/shard_map/while/body/eval_jaxpr/ppermute | solution.py:14
  471.2 22.6 %collective-permute-start = (bf16[512,128]{0,1:T(8,128)(2,1)}, bf16[512,128]{0,1:T(8,128)(2,1)S(1)}, u32[]{:S(2)}, u32[]{:S(2)}) collective-permute-start(bf16[512,128]{0,1:T(8,128)(2,1)} %copy.98), channel_id=1, source_target_pairs={{0,8},{8,16},{16,24},{24,32},{32,40},{40,48},{48,56},{56,64},{64,7... | collective-permute-start | bytes 393224 | tf_op jit(solution)/shard_map/while/body/eval_jaxpr/ppermute | solution.py:14
  494.5 26.9 %collective-permute-start = (bf16[512,128]{0,1:T(8,128)(2,1)}, bf16[512,128]{0,1:T(8,128)(2,1)S(1)}, u32[]{:S(2)}, u32[]{:S(2)}) collective-permute-start(bf16[512,128]{0,1:T(8,128)(2,1)} %copy.98), channel_id=1, source_target_pairs={{0,8},{8,16},{16,24},{24,32},{32,40},{40,48},{48,56},{56,64},{64,7... | collective-permute-start | bytes 393224 | tf_op jit(solution)/shard_map/while/body/eval_jaxpr/ppermute | solution.py:14
  522.1 21.4 %collective-permute-start = (bf16[512,128]{0,1:T(8,128)(2,1)}, bf16[512,128]{0,1:T(8,128)(2,1)S(1)}, u32[]{:S(2)}, u32[]{:S(2)}) collective-permute-start(bf16[512,128]{0,1:T(8,128)(2,1)} %copy.98), channel_id=1, source_target_pairs={{0,8},{8,16},{16,24},{24,32},{32,40},{40,48},{48,56},{56,64},{64,7... | collective-permute-start | bytes 393224 | tf_op jit(solution)/shard_map/while/body/eval_jaxpr/ppermute | solution.py:14
  544.2 21.4 %collective-permute-start = (bf16[512,128]{0,1:T(8,128)(2,1)}, bf16[512,128]{0,1:T(8,128)(2,1)S(1)}, u32[]{:S(2)}, u32[]{:S(2)}) collective-permute-start(bf16[512,128]{0,1:T(8,128)(2,1)} %copy.98), channel_id=1, source_target_pairs={{0,8},{8,16},{16,24},{24,32},{32,40},{40,48},{48,56},{56,64},{64,7... | collective-permute-start | bytes 393224 | tf_op jit(solution)/shard_map/while/body/eval_jaxpr/ppermute | solution.py:14
  693.2 24.4 %collective-permute-start = (bf16[512,128]{0,1:T(8,128)(2,1)}, bf16[512,128]{0,1:T(8,128)(2,1)S(1)}, u32[]{:S(2)}, u32[]{:S(2)}) collective-permute-start(bf16[512,128]{0,1:T(8,128)(2,1)} %copy.98), channel_id=1, source_target_pairs={{0,8},{8,16},{16,24},{24,32},{32,40},{40,48},{48,56},{56,64},{64,7... | collective-permute-start | bytes 393224 | tf_op jit(solution)/shard_map/while/body/eval_jaxpr/ppermute | solution.py:14
  740.4 23.7 %collective-permute-start = (bf16[512,128]{0,1:T(8,128)(2,1)}, bf16[512,128]{0,1:T(8,128)(2,1)S(1)}, u32[]{:S(2)}, u32[]{:S(2)}) collective-permute-start(bf16[512,128]{0,1:T(8,128)(2,1)} %copy.98), channel_id=1, source_target_pairs={{0,8},{8,16},{16,24},{24,32},{32,40},{40,48},{48,56},{56,64},{64,7... | collective-permute-start | bytes 393224 | tf_op jit(solution)/shard_map/while/body/eval_jaxpr/ppermute | solution.py:14
  (121 other events, 1875.8 us)
Sparse Core Ops, SparseCore 0:
  778.4 92.9 reduce-scatter.1
where the time goes:
time: 885 us; the launch traced here: 878 us
  starting transfers between devices  308 us (35%)
  other arithmetic  163 us (18%)
  waiting for transfers between devices  152 us (17%)
  matrix products  115 us (13%)
  local copies, waits for them, and re-layouts  104 us (12%)
  loops' own time  22.2 us (3%)
  between operations  14.2 us (2%)
    ppermute x62, starting transfers between devices, shifted(): return lax.ppermute(block, axis, route)  227 us
    reduce_scatter x1, waiting for transfers between devices, on_device(): lax.psum_scatter(combined.astype(jnp.bfloat16), 'grp', scatter_dimension=...  93.1 us
    ppermute x64, starting transfers between devices, shifted_2(): return lax.ppermute(value, axis, pairs)  81.7 us
    dot_general x32, matrix products, pair_mask(): chosen = jnp.dot(jnp.dot(query_onehot, picked), key_onehot.T) > 0.5  81.1 us
    while x62, local copies, waits for them, and re-layouts  68.9 us
    ppermute x64, waiting for transfers between devices, shifted_2(): return lax.ppermute(value, axis, pairs)  58.9 us
    convert_element_type x31, other arithmetic, key_step(): state[2].astype(jnp.bfloat16)  53 us
    convert_element_type x31, other arithmetic, key_step(): state[3].astype(jnp.bfloat16)  50 us
  transfers between devices with their start and end apart: 127, of which 54 were waited for; matrix products, arithmetic and copies ran while one was open for 39% of the time, Pallas kernels for 0%

commit v1 on v0

v1 whole, which is shorter than its diff:
```python
import functools

import jax
import jax.numpy as jnp
from jax import lax
from jax.experimental import pallas as pl
from jax.experimental.pallas import tpu as pltpu
from jax.sharding import PartitionSpec as P

HD = 128
HEADS = 4
BLOCK = 512
BLOCKS = 32
PIECE = BLOCK // BLOCKS
SLOTS = 2
GROUPS = 8
SCALE = float(HD) ** (-0.5)
LOG2E = 1.4426950408889634
BF = jnp.bfloat16
F32 = jnp.float32
VMEM_BYTES = 50 * 1024 * 1024

PORTS = {"a": 1, "b": 3, "y": 4}
CHUNKS = ((0, 176, "aby"), (176, 176, "bya"), (352, 160, "yab"))

NT = (((1,), (1,)), ((), ()))


def others(selection, block):
    before = block - 1
    first, second, third = selection[block, 0], selection[block, 1], selection[block, 2]
    return jnp.where(first == before, second, first), jnp.where(third == before, second, third)


def pick_kernel(selection, pieces, out):
    def step(block, carry):
        for slot, chosen in enumerate(others(selection, block)):
            out[block, slot] = pieces[chosen]
        return carry

    lax.fori_loop(0, BLOCKS, step, 0)


def collect_kernel(selection, parts, out, total):
    total[...] = jnp.zeros_like(total)

    def step(block, carry):
        for slot, chosen in enumerate(others(selection, block)):

            @pl.when(chosen < block)
            def _():
                total[chosen] += parts[block, slot].astype(F32)

        return carry

    lax.fori_loop(0, BLOCKS, step, 0)
    out[...] = total[...].astype(BF)


def attention_kernel(
    place, selection, queries, output_grad, output_rows, norm, own, before, chosen,
    query_out, own_out, before_out, chosen_out,
    keys, values, keys_t, delta, query_total, key_total, value_total,
):
    block = place[0]
    picks = others(selection, block)
    norm_rows = norm[...] * LOG2E
    for head in range(HEADS):
        cols = pl.ds(head * HD, HD)
        product = output_rows[:, cols].astype(F32) * output_grad[:, cols].astype(F32)
        delta[head] = jnp.sum(product.T, axis=0, keepdims=True)
    query_total[...] = jnp.zeros_like(query_total)

    def tile(tile_norm, causal):
        key_total[...] = jnp.zeros_like(key_total)
        value_total[...] = jnp.zeros_like(value_total)
        key, value, key_t = keys[...], values[...], keys_t[...]

        def head_step(head, carry):
            cols = pl.ds(pl.multiple_of(head * HD, HD), HD)
            query, grad = queries[:, cols], output_grad[:, cols]
            scores = lax.dot_general(key, query, NT, preferred_element_type=F32)
            prob_grad = lax.dot_general(value, grad, NT, preferred_element_type=F32)
            probs = jnp.exp2(scores * (SCALE * LOG2E) - tile_norm[head] * LOG2E)
            if causal:
                shape = (BLOCK, BLOCK)
                seen = lax.broadcasted_iota(jnp.int32, shape, 0) <= lax.broadcasted_iota(jnp.int32, shape, 1)
                probs = jnp.where(seen, probs, 0.0)
            score_half = (probs * (prob_grad - delta[head])).astype(BF)
            value_total[...] += jnp.dot(probs.astype(BF), grad, preferred_element_type=F32)
            key_total[...] += jnp.dot(score_half, query, preferred_element_type=F32)
            query_total[head] += jnp.dot(key_t, score_half, preferred_element_type=F32)
            return carry

        lax.fori_loop(0, HEADS, head_step, 0)

    def load(key, value):
        keys[...] = key
        values[...] = value
        keys_t[...] = key.astype(F32).T.astype(BF)

    load(own[:, :HD], own[:, HD:])
    tile(norm, True)
    own_out[:, :HD] = key_total[...]
    own_out[:, HD:] = value_total[...]

    @pl.when(block > 0)
    def _():
        load(before[:, :HD], before[:, HD:])
        tile(norm, False)
        before_out[:, :HD] = key_total[...].astype(BF)
        before_out[:, HD:] = value_total[...].astype(BF)

    @pl.when(block == 0)
    def _():
        before_out[...] = jnp.zeros_like(before_out)

    for slot in range(SLOTS):

        @pl.when(picks[slot] < block)
        def _():
            load(
                chosen[:, slot, :, :HD].reshape(BLOCK, HD),
                chosen[:, slot, :, HD:].reshape(BLOCK, HD),
            )
            tile(norm, False)
            chosen_out[:, slot, :, :HD] = key_total[...].reshape(BLOCKS, PIECE, HD).astype(BF)
            chosen_out[:, slot, :, HD:] = value_total[...].reshape(BLOCKS, PIECE, HD).astype(BF)

        @pl.when(picks[slot] >= block)
        def _():
            chosen_out[:, slot] = jnp.zeros((BLOCKS, PIECE, 2 * HD), BF)

    for head in range(HEADS):
        query_out[:, head * HD : (head + 1) * HD] = (query_total[head].T * SCALE).astype(BF)


def project_kernel(place, query_grad, own, before, chosen, query_weight, key_weight, value_weight, *refs):
    outs, (key_grad, value_grad) = refs[: len(CHUNKS)], refs[len(CHUNKS) :]

    @pl.when(pl.program_id(0) == 0)
    def _():
        total = own[...] + before[...].astype(F32) + chosen[...].reshape(BLOCK, 2 * HD).astype(F32)
        key_grad[...] = (total[:, :HD] * SCALE).astype(BF)
        value_grad[...] = total[:, HD:].astype(BF)

    part = lax.dot_general(query_grad[...], query_weight[...], NT, preferred_element_type=F32)
    part += lax.dot_general(key_grad[...], key_weight[...], NT, preferred_element_type=F32)
    part += lax.dot_general(value_grad[...], value_weight[...], NT, preferred_element_type=F32)
    part = part.astype(BF)
    for (start, rows, _), out in zip(CHUNKS, outs):
        out[0] = part[start : start + rows]


def chunk_index(step, order):
    bits = {"a": step // 4, "b": step // 2 % 2, "y": step % 2}
    return bits[order[0]] * 4 + bits[order[1]] * 2 + bits[order[2]]


def weight_index(step, place):
    target = (step // 4) * PORTS["a"] ^ (step // 2 % 2) * PORTS["b"] ^ (step % 2) * PORTS["y"]
    return (place[0] ^ target, 0)


def project(place, query_grad, own, before, chosen, query_weight, key_weight, value_weight):
    model = query_weight.shape[0] // GROUPS
    whole = lambda array: pl.BlockSpec(array.shape, lambda step, place: (0,) * array.ndim)
    weight = lambda array: pl.BlockSpec((model, array.shape[1]), weight_index)
    return pl.pallas_call(
        project_kernel,
        grid_spec=pltpu.PrefetchScalarGridSpec(
            num_scalar_prefetch=1,
            grid=(GROUPS,),
            in_specs=[
                whole(query_grad), whole(own), whole(before), whole(chosen),
                weight(query_weight), weight(key_weight), weight(value_weight),
            ],
            out_specs=[
                pl.BlockSpec((1, rows, model), lambda step, place, order=order: (chunk_index(step, order), 0, 0))
                for _, rows, order in CHUNKS
            ],
            scratch_shapes=[pltpu.VMEM((BLOCK, HD), BF), pltpu.VMEM((BLOCK, HD), BF)],
        ),
        out_shape=[jax.ShapeDtypeStruct((GROUPS, rows, model), BF) for _, rows, _ in CHUNKS],
        compiler_params=pltpu.CompilerParams(vmem_limit_bytes=VMEM_BYTES),
    )(place, query_grad, own, before, chosen, query_weight, key_weight, value_weight)


def swap(value, port):
    return lax.ppermute(value, "grp", [(source, source ^ PORTS[port]) for source in range(GROUPS)])


def reduce_over_groups(parts):
    parts = list(parts)
    for stage in range(3):
        half = parts[0].shape[0] // 2
        sent = lax.optimization_barrier([part[half:] for part in parts])
        got = [swap(part, order[stage]) for part, (_, _, order) in zip(sent, CHUNKS)]
        got = lax.optimization_barrier(got)
        parts = [part[:half].astype(F32) + other.astype(F32) for part, other in zip(parts, got)]
        parts = [part.astype(BF) for part in parts]
    return jnp.concatenate([part[0] for part in parts], axis=0)


def on_device(
    queries, key_rows, value_rows, output_rows, output_grad, log_normalizer, selection,
    query_weight, key_weight, value_weight,
):
    smem = pl.BlockSpec(memory_space=pltpu.SMEM)
    vmem = pl.BlockSpec(memory_space=pltpu.VMEM)
    params = pltpu.CompilerParams(vmem_limit_bytes=VMEM_BYTES)
    place = lax.axis_index("ctx").astype(jnp.int32).reshape(1)
    group = lax.axis_index("grp").astype(jnp.int32).reshape(1)
    count = lax.axis_size("ctx")
    own = jnp.concatenate([key_rows, value_rows], axis=1)
    norm = log_normalizer.T.reshape(HEADS, 1, BLOCK)

    before = lax.ppermute(own, "ctx", [(i, (i + 1) % count) for i in range(count)])
    pieces = lax.all_to_all(own.reshape(BLOCKS, PIECE, 2 * HD), "ctx", 0, 0)
    picked = pl.pallas_call(
        pick_kernel,
        in_specs=[smem, vmem],
        out_specs=vmem,
        out_shape=jax.ShapeDtypeStruct((BLOCKS, SLOTS, PIECE, 2 * HD), BF),
        compiler_params=params,
    )(selection, pieces)
    chosen = lax.all_to_all(picked, "ctx", 0, 0)

    query_grad, own_grad, before_grad, chosen_grad = pl.pallas_call(
        attention_kernel,
        in_specs=[smem, smem] + [vmem] * 7,
        out_specs=[vmem] * 4,
        out_shape=[
            jax.ShapeDtypeStruct((BLOCK, HEADS * HD), BF),
            jax.ShapeDtypeStruct((BLOCK, 2 * HD), F32),
            jax.ShapeDtypeStruct((BLOCK, 2 * HD), BF),
            jax.ShapeDtypeStruct((BLOCKS, SLOTS, PIECE, 2 * HD), BF),
        ],
        scratch_shapes=[
            pltpu.VMEM((BLOCK, HD), BF),
            pltpu.VMEM((BLOCK, HD), BF),
            pltpu.VMEM((HD, BLOCK), BF),
            pltpu.VMEM((HEADS, 1, BLOCK), F32),
            pltpu.VMEM((HEADS, HD, BLOCK), F32),
            pltpu.VMEM((BLOCK, HD), F32),
            pltpu.VMEM((BLOCK, HD), F32),
        ],
        compiler_params=params,
    )(place, selection, queries, output_grad, output_rows, norm, own, before, chosen)

    before_sum = lax.ppermute(before_grad, "ctx", [(i, (i - 1) % count) for i in range(count)])
    returned = lax.all_to_all(chosen_grad, "ctx", 0, 0)
    collected = pl.pallas_call(
        collect_kernel,
        in_specs=[smem, vmem],
        out_specs=vmem,
        out_shape=jax.ShapeDtypeStruct((BLOCKS, PIECE, 2 * HD), BF),
        scratch_shapes=[pltpu.VMEM((BLOCKS, PIECE, 2 * HD), F32)],
        compiler_params=params,
    )(selection, returned)
    chosen_sum = lax.all_to_all(collected, "ctx", 0, 0)
    parts = project(
        group, query_grad, own_grad, before_sum, chosen_sum, query_weight, key_weight, value_weight
    )
    return reduce_over_groups(parts)


def solution(mesh):
    tokens = P("ctx", "grp")
    return jax.shard_map(
        on_device,
        mesh=mesh,
        in_specs=(tokens,) * 6 + (P(),) + (P(None, "grp"),) * 3,
        out_specs=tokens,
        check_vma=False,
    )
```

time: 885 us -> 163 us (0.18)
  starting transfers between devices: 308 us -> 29.1 us
  other arithmetic: 163 us -> 1.83 us
  matrix products: 115 us -> 0 us
  local copies, waits for them, and re-layouts: 104 us -> 7.57 us
  waiting for transfers between devices: 152 us -> 70 us
  blocking collectives: 0 us -> 27.1 us
  Pallas kernels: 0 us -> 25.4 us
  loops' own time: 22.2 us -> 0 us
  between operations: 14.2 us -> 0.23 us
    ppermute x126 -> x11, starting transfers between devices: 308 us -> 11 us  [the longest x9 10.6 us: swap(): lax.ppermute(value, 'grp', [(source, source ^ PORTS[port]) for source in...]
    convert_element_type x126 -> x5, other arithmetic: 148 us -> 0.87 us  [reduce_over_groups(): parts = [part.astype(BF) for part in parts]]
    dot_general x50 -> x0, matrix products: 115 us -> none  [the longest x32 81.1 us: pair_mask(): chosen = jnp.dot(jnp.dot(query_onehot, picked), key_onehot.T) > 0.5]
    reduce_scatter x1 -> x0, waiting for transfers between devices: 93.1 us -> none  [on_device(): lax.psum_scatter(combined.astype(jnp.bfloat16), 'grp', scatter_dimension=...]
    while x62 -> x0, local copies, waits for them, and re-layouts: 68.9 us -> none
    another operation x90 -> x0, local copies, waits for them, and re-layouts: 29.1 us -> none
    all_to_all x0 -> x3, waiting for transfers between devices: none -> 27.9 us  [the longest x1 11.3 us: on_device(): pieces = lax.all_to_all(own.reshape(BLOCKS, PIECE, 2 * HD), 'ctx', 0, 0)]
    all_to_all x0 -> x1, blocking collectives: none -> 27.1 us  [on_device(): returned = lax.all_to_all(chosen_grad, 'ctx', 0, 0)]
  transfers between devices with their start and end apart: 127 -> 14, of which waited for: 54 -> 9; matrix products, arithmetic and copies ran while one was open for 39% -> 0% of each run, Pallas kernels for 0% -> 0%
where the time goes in v1:
time: 163 us; the launch traced here: 161 us
  waiting for transfers between devices  70 us (43%)
  starting transfers between devices  29.1 us (18%)
  blocking collectives  27.1 us (17%)
  Pallas kernels  25.4 us (16%)
  local copies, waits for them, and re-layouts  7.57 us (5%)
  other arithmetic  1.83 us (1%)
    ppermute x9, waiting for transfers between devices, swap(): lax.ppermute(value, 'grp', [(source, source ^ PORTS[port]) for source in...  29 us
    all_to_all x1, blocking collectives, on_device(): returned = lax.all_to_all(chosen_grad, 'ctx', 0, 0)  27.1 us
    pallas_call x1, Pallas kernels, on_device(): pl.pallas_call(attention_kernel, in_specs=[smem, smem] + [vmem] * 7, out_...  12 us
    all_to_all x1, waiting for transfers between devices, on_device(): pieces = lax.all_to_all(own.reshape(BLOCKS, PIECE, 2 * HD), 'ctx', 0, 0)  11.3 us
    ppermute x9, starting transfers between devices, swap(): lax.ppermute(value, 'grp', [(source, source ^ PORTS[port]) for source in...  10.6 us
    all_to_all x1, starting transfers between devices, on_device(): pieces = lax.all_to_all(own.reshape(BLOCKS, PIECE, 2 * HD), 'ctx', 0, 0)  10.1 us
    all_to_all x1, waiting for transfers between devices, on_device(): chosen = lax.all_to_all(picked, 'ctx', 0, 0)  9.88 us
    pallas_call x1, Pallas kernels, project(): pl.pallas_call(project_kernel, grid_spec=pltpu.PrefetchScalarGridSpec(num...  9.17 us
  transfers between devices with their start and end apart: 14, of which 9 were waited for; matrix products, arithmetic and copies ran while one was open for 0% of the time, Pallas kernels for 0%

profile of v1, /device:TPU:24, one launch (start us, length us, event | category | flops | bytes accessed | tf_op | source)
XLA Modules:
  0.0 161.2 jit_solution(15344193895123663197)
XLA Ops:
  0.0 1.7 %constant_dynamic-update-slice_fusion.1 = bf16[512,256]{1,0:T(8,128)(2,1)} fusion(bf16[512,128]{1,0:T(8,128)(2,1)} %param.11), kind=kLoop, calls=%fused_computation.14 | loop fusion | bytes 262144
  1.7 1.6 constant_dynamic-update-slice_fusion.own
  3.3 10.1 %all-to-all-start = ((bf16[32,16,256]{2,1,0:T(8,128)(2,1)}), bf16[32,16,256]{2,1,0:T(8,128)(2,1)S(1)}, u32[]{:S(2)}, u32[]{:S(2)}) async-start(bf16[32,16,256]{2,1,0:T(8,128)(2,1)} %bitcast.3), calls=%async_computation | async-start | bytes 524288 | tf_op jit(solution)/shard_map/all_to_all | solution.py:219
  14.2 11.3 %all-to-all-done.pieces = bf16[32,16,256]{2,1,0:T(8,128)(2,1)S(1)} async-done(((bf16[32,16,256]{2,1,0:T(8,128)(2,1)}), bf16[32,16,256]{2,1,0:T(8,128)(2,1)S(1)}, u32[]{:S(2)}, u32[]{:S(2)}) %all-to-all-start) | async-done | bytes 262176 | tf_op jit(solution)/shard_map/all_to_all | solution.py:219
  25.5 1.9 %shard_map.100 = bf16[32,2,16,256]{3,2,1,0:T(8,128)(2,1)} custom-call(s32[32,3]{1,0:T(8,128)S(1)} %copy.12.selection, bf16[32,16,256]{2,1,0:T(8,128)(2,1)S(1)} %all-to-all-done.pieces), custom_call_target="tpu_custom_call" | custom-call | tf_op jit(solution)/shard_map/pallas_call | solution.py:220
  27.4 3.9 %all-to-all-start.1 = ((bf16[32,2,16,256]{3,2,1,0:T(8,128)(2,1)}), bf16[32,2,16,256]{3,2,1,0:T(8,128)(2,1)S(1)}, u32[]{:S(2)}, u32[]{:S(2)}) async-start(bf16[32,2,16,256]{3,2,1,0:T(8,128)(2,1)} %shard_map.100), calls=%async_computation.1 | async-start | bytes 1048576 | tf_op jit(solution)/shard_map/all_to_all | solution.py:227
  31.5 7.9 %collective-permute-done.before = bf16[512,256]{1,0:T(8,128)(2,1)S(1)} collective-permute-done((bf16[512,256]{1,0:T(8,128)(2,1)}, bf16[512,256]{1,0:T(8,128)(2,1)S(1)}, u32[]{:S(2)}, u32[]{:S(2)}) %collective-permute-start) | collective-permute-done | bytes 262176 | tf_op jit(solution)/shard_map/ppermute | solution.py:218
  39.4 9.9 %all-to-all-done.1.chosen = bf16[32,2,16,256]{3,2,1,0:T(8,128)(2,1)S(1)} async-done(((bf16[32,2,16,256]{3,2,1,0:T(8,128)(2,1)}), bf16[32,2,16,256]{3,2,1,0:T(8,128)(2,1)S(1)}, u32[]{:S(2)}, u32[]{:S(2)}) %all-to-all-start.1) | async-done | bytes 524320 | tf_op jit(solution)/shard_map/all_to_all | solution.py:227
  50.1 12.0 %shard_map.101 = (bf16[512,512]{1,0:T(8,128)(2,1)S(1)}, f32[512,256]{1,0:T(8,128)S(1)}, bf16[512,256]{1,0:T(8,128)(2,1)S(1)}, bf16[32,2,16,256]{3,2,1,0:T(8,128)(2,1)S(1)}) custom-call(s32[1]{0:T(128)} %bitcast.1.place, s32[32,3]{1,0:T(8,128)S(1)} %copy.12.selection, bf16[512,512]{1,0:T(8,128)(2,1)S(1)} %copy-done.2, bf16[512,512]{1,0:T(8,128)(2,1)S(1)} %copy-done.3, ...), custom_call_target="tpu_custom_call" | custom-call | tf_op jit(solution)/shard_map/pallas_call | solution.py:229
  62.1 27.1 %all_to_all.20.parts = bf16[32,2,16,256]{3,2,1,0:T(8,128)(2,1)S(1)} all-to-all(bf16[32,2,16,256]{3,2,1,0:T(8,128)(2,1)S(1)} %get-tuple-element.33), channel_id=1, replica_groups=mesh['ctx'=32,'grp'=8] {'ctx'}, dimensions={0} | all-to-all | bytes 1048576 | tf_op jit(solution)/shard_map/all_to_all | solution.py:252
  89.2 2.4 %shard_map.102 = bf16[32,16,256]{2,1,0:T(8,128)(2,1)} custom-call(s32[32,3]{1,0:T(8,128)S(1)} %copy.12.selection, bf16[32,2,16,256]{3,2,1,0:T(8,128)(2,1)S(1)} %all_to_all.20.parts), custom_call_target="tpu_custom_call" | custom-call | tf_op jit(solution)/shard_map/pallas_call | solution.py:253
  91.5 4.1 %all-to-all-start.3 = ((bf16[32,16,256]{2,1,0:T(8,128)(2,1)}), bf16[32,16,256]{2,1,0:T(8,128)(2,1)S(1)}, u32[]{:S(2)}, u32[]{:S(2)}) async-start(bf16[32,16,256]{2,1,0:T(8,128)(2,1)} %shard_map.102), calls=%async_computation.3 | async-start | bytes 524288 | tf_op jit(solution)/shard_map/all_to_all | solution.py:261
  95.8 5.3 %collective-permute-done.1.before = bf16[512,256]{1,0:T(8,128)(2,1)} collective-permute-done((bf16[512,256]{1,0:T(8,128)(2,1)}, bf16[512,256]{1,0:T(8,128)(2,1)}, u32[]{:S(2)}, u32[]{:S(2)}) %collective-permute-start.1) | collective-permute-done | bytes 262176 | tf_op jit(solution)/shard_map/ppermute | solution.py:251
  101.1 6.7 %all-to-all-done.3.chosen = bf16[32,16,256]{2,1,0:T(8,128)(2,1)S(1)} async-done(((bf16[32,16,256]{2,1,0:T(8,128)(2,1)}), bf16[32,16,256]{2,1,0:T(8,128)(2,1)S(1)}, u32[]{:S(2)}, u32[]{:S(2)}) %all-to-all-start.3) | async-done | bytes 262176 | tf_op jit(solution)/shard_map/all_to_all | solution.py:261
  107.8 9.2 %shard_map.103 = (bf16[8,176,512]{2,1,0:T(8,128)(2,1)}, bf16[8,176,512]{2,1,0:T(8,128)(2,1)}, bf16[8,160,512]{2,1,0:T(8,128)(2,1)}) custom-call(s32[1]{0:T(128)} %bitcast.place, bf16[512,512]{1,0:T(8,128)(2,1)S(1)} %get-tuple-element.30.query_grad, f32[512,256]{1,0:T(8,128)S(1)} %get-tuple-element.31.own, bf16[512,256]{1,0:T(8,128)(2,1)} %collective-permute-done.1.before, ...), custom_call_target="tpu_custom_call" | custom-call | tf_op jit(solution)/shard_map/pallas_call | solution.py:169
  118.2 1.3 slice.55
  119.5 1.6 collective-permute-start.2
  121.1 2.1 %collective-permute-start.3 = (bf16[4,176,512]{2,1,0:T(8,128)(2,1)S(1)}, bf16[4,176,512]{2,1,0:T(8,128)(2,1)S(1)}, u32[]{:S(2)}, u32[]{:S(2)}) collective-permute-start(bf16[4,176,512]{2,1,0:T(8,128)(2,1)S(1)} %slice.56), channel_id=1, source_target_pairs={{0,3},{1,2},{2,1},{3,0},{4,7},{5,6},{6,5},{7,4},{8,11},{9,10},{10,... | collective-permute-start | bytes 2162696 | tf_op jit(solution)/shard_map/ppermute | solution.py:190
  124.5 15.6 %collective-permute-done.4 = bf16[4,160,512]{2,1,0:T(8,128)(2,1)S(1)} collective-permute-done((bf16[4,160,512]{2,1,0:T(8,128)(2,1)S(1)}, bf16[4,160,512]{2,1,0:T(8,128)(2,1)S(1)}, u32[]{:S(2)}, u32[]{:S(2)}) %collective-permute-start.4) | collective-permute-done | bytes 655392 | tf_op jit(solution)/shard_map/ppermute | solution.py:190
  140.8 1.5 collective-permute-start.5
  143.5 7.1 %collective-permute-done.7 = bf16[2,160,512]{2,1,0:T(8,128)(2,1)S(1)} collective-permute-done((bf16[2,160,512]{2,1,0:T(8,128)(2,1)S(1)}, bf16[2,160,512]{2,1,0:T(8,128)(2,1)S(1)}, u32[]{:S(2)}, u32[]{:S(2)}) %collective-permute-start.7) | collective-permute-done | bytes 327712 | tf_op jit(solution)/shard_map/ppermute | solution.py:190
  152.2 1.3 collective-permute-start.8
  153.7 1.6 collective-permute-start.10
  155.2 5.0 %collective-permute-done.10 = bf16[1,160,512]{2,1,0:T(8,128)(2,1)S(1)} collective-permute-done((bf16[1,160,512]{2,1,0:T(8,128)(2,1)S(1)}, bf16[1,160,512]{2,1,0:T(8,128)(2,1)S(1)}, u32[]{:S(2)}, u32[]{:S(2)}) %collective-permute-start.10) | collective-permute-done | bytes 163872 | tf_op jit(solution)/shard_map/ppermute | solution.py:190
  (53 shorter events, 9.1 us)
Async XLA Ops:
  0.0 31.5 %copy-start.10 = (f32[512,4]{0,1:T(4,128)S(1)}, f32[512,4]{0,1:T(4,128)}, u32[]{:S(2)}) copy-start(f32[512,4]{0,1:T(4,128)} %param.15) | copy-start | bytes 24580
  0.0 50.1 %copy-start.3 = (bf16[512,512]{1,0:T(8,128)(2,1)S(1)}, bf16[512,512]{1,0:T(8,128)(2,1)}, u32[]{:S(2)}) copy-start(bf16[512,512]{1,0:T(8,128)(2,1)} %output_grad.1) | copy-start | bytes 1572868
  0.0 50.1 %copy-start.4 = (bf16[512,512]{1,0:T(8,128)(2,1)S(1)}, bf16[512,512]{1,0:T(8,128)(2,1)}, u32[]{:S(2)}) copy-start(bf16[512,512]{1,0:T(8,128)(2,1)} %output_rows.1) | copy-start | bytes 1572868
  0.0 50.1 %copy-start.2 = (bf16[512,512]{1,0:T(8,128)(2,1)S(1)}, bf16[512,512]{1,0:T(8,128)(2,1)}, u32[]{:S(2)}) copy-start(bf16[512,512]{1,0:T(8,128)(2,1)} %queries.1) | copy-start | bytes 1572868
  3.3 22.2 %all-to-all-start = ((bf16[32,16,256]{2,1,0:T(8,128)(2,1)}), bf16[32,16,256]{2,1,0:T(8,128)(2,1)S(1)}, u32[]{:S(2)}, u32[]{:S(2)}) async-start(bf16[32,16,256]{2,1,0:T(8,128)(2,1)} %bitcast.3), calls=%async_computation | async-start | bytes 524288 | tf_op jit(solution)/shard_map/all_to_all | solution.py:219
  27.4 21.9 %all-to-all-start.1 = ((bf16[32,2,16,256]{3,2,1,0:T(8,128)(2,1)}), bf16[32,2,16,256]{3,2,1,0:T(8,128)(2,1)S(1)}, u32[]{:S(2)}, u32[]{:S(2)}) async-start(bf16[32,2,16,256]{3,2,1,0:T(8,128)(2,1)} %shard_map.100), calls=%async_computation.1 | async-start | bytes 1048576 | tf_op jit(solution)/shard_map/all_to_all | solution.py:227
  31.3 8.1 %collective-permute-start = (bf16[512,256]{1,0:T(8,128)(2,1)}, bf16[512,256]{1,0:T(8,128)(2,1)S(1)}, u32[]{:S(2)}, u32[]{:S(2)}) collective-permute-start(bf16[512,256]{1,0:T(8,128)(2,1)} %constant_dynamic-update-slice_fusion.own), channel_id=1, source_target_pairs={{0,8},{8,16},{16,24},{24,32},{32,40},{40,48},{48,56},{56,64},{64,7... | collective-permute-start | bytes 786440 | tf_op jit(solution)/shard_map/ppermute | solution.py:218
  62.0 27.1 %copy-start.5 = (bf16[512,256]{1,0:T(8,128)(2,1)}, bf16[512,256]{1,0:T(8,128)(2,1)S(1)}, u32[]{:S(2)}) copy-start(bf16[512,256]{1,0:T(8,128)(2,1)S(1)} %get-tuple-element.32) | copy-start | bytes 786436
  62.1 45.7 %copy-start = (bf16[4096,128]{1,0:T(8,128)(2,1)S(1)}, bf16[4096,128]{1,0:T(8,128)(2,1)}, u32[]{:S(2)}) copy-start(bf16[4096,128]{1,0:T(8,128)(2,1)} %key_weight.1) | copy-start | bytes 3145732
  62.1 45.7 %copy-start.1 = (bf16[4096,128]{1,0:T(8,128)(2,1)S(1)}, bf16[4096,128]{1,0:T(8,128)(2,1)}, u32[]{:S(2)}) copy-start(bf16[4096,128]{1,0:T(8,128)(2,1)} %value_weight.1) | copy-start | bytes 3145732
  91.5 16.3 %all-to-all-start.3 = ((bf16[32,16,256]{2,1,0:T(8,128)(2,1)}), bf16[32,16,256]{2,1,0:T(8,128)(2,1)S(1)}, u32[]{:S(2)}, u32[]{:S(2)}) async-start(bf16[32,16,256]{2,1,0:T(8,128)(2,1)} %shard_map.102), calls=%async_computation.3 | async-start | bytes 524288 | tf_op jit(solution)/shard_map/all_to_all | solution.py:261
  95.6 5.5 %collective-permute-start.1 = (bf16[512,256]{1,0:T(8,128)(2,1)}, bf16[512,256]{1,0:T(8,128)(2,1)}, u32[]{:S(2)}, u32[]{:S(2)}) collective-permute-start(bf16[512,256]{1,0:T(8,128)(2,1)} %copy-done.5), channel_id=1, source_target_pairs={{0,248},{8,0},{16,8},{24,16},{32,24},{40,32},{48,40},{56,48},{64,5... | collective-permute-start | bytes 786440 | tf_op jit(solution)/shard_map/ppermute | solution.py:251
  116.9 2.5 %copy-start.8 = (bf16[8,176,512]{2,1,0:T(8,128)(2,1)S(1)}, bf16[8,176,512]{2,1,0:T(8,128)(2,1)}, u32[]{:S(2)}) copy-start(bf16[8,176,512]{2,1,0:T(8,128)(2,1)} %get-tuple-element.35) | copy-start | bytes 4325380
  118.2 21.9 %copy-start.9 = (bf16[8,160,512]{2,1,0:T(8,128)(2,1)S(1)}, bf16[8,160,512]{2,1,0:T(8,128)(2,1)}, u32[]{:S(2)}) copy-start(bf16[8,160,512]{2,1,0:T(8,128)(2,1)} %get-tuple-element.36) | copy-start | bytes 3932164
  119.5 20.8 %copy-start.7 = (bf16[8,176,512]{2,1,0:T(8,128)(2,1)S(1)}, bf16[8,176,512]{2,1,0:T(8,128)(2,1)}, u32[]{:S(2)}) copy-start(bf16[8,176,512]{2,1,0:T(8,128)(2,1)} %get-tuple-element.34) | copy-start | bytes 4325380
  119.5 20.5 %collective-permute-start.2 = (bf16[4,176,512]{2,1,0:T(8,128)(2,1)S(1)}, bf16[4,176,512]{2,1,0:T(8,128)(2,1)S(1)}, u32[]{:S(2)}, u32[]{:S(2)}) collective-permute-start(bf16[4,176,512]{2,1,0:T(8,128)(2,1)S(1)} %slice.55), channel_id=1, source_target_pairs={{0,1},{1,0},{2,3},{3,2},{4,5},{5,4},{6,7},{7,6},{8,9},{9,8},{10,11... | collective-permute-start | bytes 2162696 | tf_op jit(solution)/shard_map/ppermute | solution.py:190
  121.1 19.0 %collective-permute-start.3 = (bf16[4,176,512]{2,1,0:T(8,128)(2,1)S(1)}, bf16[4,176,512]{2,1,0:T(8,128)(2,1)S(1)}, u32[]{:S(2)}, u32[]{:S(2)}) collective-permute-start(bf16[4,176,512]{2,1,0:T(8,128)(2,1)S(1)} %slice.56), channel_id=1, source_target_pairs={{0,3},{1,2},{2,1},{3,0},{4,7},{5,6},{6,5},{7,4},{8,11},{9,10},{10,... | collective-permute-start | bytes 2162696 | tf_op jit(solution)/shard_map/ppermute | solution.py:190
  123.2 16.9 %collective-permute-start.4 = (bf16[4,160,512]{2,1,0:T(8,128)(2,1)S(1)}, bf16[4,160,512]{2,1,0:T(8,128)(2,1)S(1)}, u32[]{:S(2)}, u32[]{:S(2)}) collective-permute-start(bf16[4,160,512]{2,1,0:T(8,128)(2,1)S(1)} %slice.57), channel_id=1, source_target_pairs={{0,4},{1,5},{2,6},{3,7},{4,0},{5,1},{6,2},{7,3},{8,12},{9,13},{10,... | collective-permute-start | bytes 1966088 | tf_op jit(solution)/shard_map/ppermute | solution.py:190
  140.8 9.8 %collective-permute-start.5 = (bf16[2,176,512]{2,1,0:T(8,128)(2,1)S(1)}, bf16[2,176,512]{2,1,0:T(8,128)(2,1)S(1)}, u32[]{:S(2)}, u32[]{:S(2)}) collective-permute-start(bf16[2,176,512]{2,1,0:T(8,128)(2,1)S(1)} %slice.73), channel_id=1, source_target_pairs={{0,3},{1,2},{2,1},{3,0},{4,7},{5,6},{6,5},{7,4},{8,11},{9,10},{10,... | collective-permute-start | bytes 1081352 | tf_op jit(solution)/shard_map/ppermute | solution.py:190
  142.3 9.6 %collective-permute-start.6 = (bf16[2,176,512]{2,1,0:T(8,128)(2,1)S(1)}, bf16[2,176,512]{2,1,0:T(8,128)(2,1)S(1)}, u32[]{:S(2)}, u32[]{:S(2)}) collective-permute-start(bf16[2,176,512]{2,1,0:T(8,128)(2,1)S(1)} %slice.74), channel_id=1, source_target_pairs={{0,4},{1,5},{2,6},{3,7},{4,0},{5,1},{6,2},{7,3},{8,12},{9,13},{10,... | collective-permute-start | bytes 1081352 | tf_op jit(solution)/shard_map/ppermute | solution.py:190
  143.5 7.1 %collective-permute-start.7 = (bf16[2,160,512]{2,1,0:T(8,128)(2,1)S(1)}, bf16[2,160,512]{2,1,0:T(8,128)(2,1)S(1)}, u32[]{:S(2)}, u32[]{:S(2)}) collective-permute-start(bf16[2,160,512]{2,1,0:T(8,128)(2,1)S(1)} %slice.75), channel_id=1, source_target_pairs={{0,1},{1,0},{2,3},{3,2},{4,5},{5,4},{6,7},{7,6},{8,9},{9,8},{10,11... | collective-permute-start | bytes 983048 | tf_op jit(solution)/shard_map/ppermute | solution.py:190
  152.2 8.0 %collective-permute-start.8 = (bf16[1,176,512]{2,1,0:T(8,128)(2,1)S(1)}, bf16[1,176,512]{2,1,0:T(8,128)(2,1)S(1)}, u32[]{:S(2)}, u32[]{:S(2)}) collective-permute-start(bf16[1,176,512]{2,1,0:T(8,128)(2,1)S(1)} %slice.77), channel_id=1, source_target_pairs={{0,4},{1,5},{2,6},{3,7},{4,0},{5,1},{6,2},{7,3},{8,12},{9,13},{10,... | collective-permute-start | bytes 540680 | tf_op jit(solution)/shard_map/ppermute | solution.py:190
  153.5 6.6 %collective-permute-start.9 = (bf16[1,176,512]{2,1,0:T(8,128)(2,1)S(1)}, bf16[1,176,512]{2,1,0:T(8,128)(2,1)S(1)}, u32[]{:S(2)}, u32[]{:S(2)}) collective-permute-start(bf16[1,176,512]{2,1,0:T(8,128)(2,1)S(1)} %slice.79), channel_id=1, source_target_pairs={{0,1},{1,0},{2,3},{3,2},{4,5},{5,4},{6,7},{7,6},{8,9},{9,8},{10,11... | collective-permute-start | bytes 540680 | tf_op jit(solution)/shard_map/ppermute | solution.py:190
  153.7 6.5 %collective-permute-start.10 = (bf16[1,160,512]{2,1,0:T(8,128)(2,1)S(1)}, bf16[1,160,512]{2,1,0:T(8,128)(2,1)S(1)}, u32[]{:S(2)}, u32[]{:S(2)}) collective-permute-start(bf16[1,160,512]{2,1,0:T(8,128)(2,1)S(1)} %slice.81), channel_id=1, source_target_pairs={{0,3},{1,2},{2,1},{3,0},{4,7},{5,6},{6,5},{7,4},{8,11},{9,10},{10,... | collective-permute-start | bytes 491528 | tf_op jit(solution)/shard_map/ppermute | solution.py:190
  (1 other events, 0.8 us)

commit v2 on v1

v2 whole, which is shorter than its diff:
```python
import jax
import jax.numpy as jnp
from jax import lax
from jax.experimental import pallas as pl
from jax.experimental.pallas import tpu as pltpu
from jax.sharding import PartitionSpec as P

HD = 128
HEADS = 4
BLOCK = 512
BLOCKS = 32
PIECE = BLOCK // BLOCKS
SLOTS = 2
GROUPS = 8
SCALE = float(HD) ** (-0.5)
LOG2E = 1.4426950408889634
BF = jnp.bfloat16
F32 = jnp.float32
MIB = 1024 * 1024

PARTNERS = 3
HALVES = 2
OTHER = 4

NT = (((1,), (1,)), ((), ()))


def others(selection, block):
    before = block - 1
    first, second, third = selection[block, 0], selection[block, 1], selection[block, 2]
    return jnp.where(first == before, second, first), jnp.where(third == before, second, third)


def pick_kernel(selection, pieces, *refs):
    out = refs[-1]

    def step(block, carry):
        for slot, chosen in enumerate(others(selection, block)):
            out[block, slot] = pieces[chosen]
        return carry

    lax.fori_loop(0, BLOCKS, step, 0)


def collect_kernel(selection, parts, *refs):
    out, total = refs[-2:]
    total[...] = jnp.zeros_like(total)

    def step(block, carry):
        for slot, chosen in enumerate(others(selection, block)):

            @pl.when(chosen < block)
            def _():
                total[chosen] += parts[block, slot].astype(F32)

        return carry

    lax.fori_loop(0, BLOCKS, step, 0)
    out[...] = total[...].astype(BF)


def attend(queries, output_grad, norm, delta, scratch, causal):
    keys, values, keys_t, query_total, key_total, value_total = scratch
    key_total[...] = jnp.zeros_like(key_total)
    value_total[...] = jnp.zeros_like(value_total)
    key, value, key_t = keys[...], values[...], keys_t[...]

    def head_step(head, carry):
        cols = pl.ds(pl.multiple_of(head * HD, HD), HD)
        query, grad = queries[:, cols], output_grad[:, cols]
        scores = lax.dot_general(key, query, NT, preferred_element_type=F32)
        prob_grad = lax.dot_general(value, grad, NT, preferred_element_type=F32)
        probs = jnp.exp2(scores * (SCALE * LOG2E) - norm[head] * LOG2E)
        if causal:
            shape = (BLOCK, BLOCK)
            seen = lax.broadcasted_iota(jnp.int32, shape, 0) <= lax.broadcasted_iota(jnp.int32, shape, 1)
            probs = jnp.where(seen, probs, 0.0)
        score_half = (probs * (prob_grad - delta[head])).astype(BF)
        value_total[...] += jnp.dot(probs.astype(BF), grad, preferred_element_type=F32)
        key_total[...] += jnp.dot(score_half, query, preferred_element_type=F32)
        query_total[head] += jnp.dot(key_t, score_half, preferred_element_type=F32)
        return carry

    lax.fori_loop(0, HEADS, head_step, 0, unroll=True)


def load(scratch, key, value):
    keys, values, keys_t = scratch[:3]
    keys[...] = key
    values[...] = value
    keys_t[...] = key.astype(F32).T.astype(BF)


def near_kernel(
    place, queries, output_grad, output_rows, norm, own, before,
    delta, query_total, own_out, before_out, keys, values, keys_t, key_total, value_total,
):
    scratch = (keys, values, keys_t, query_total, key_total, value_total)
    for head in range(HEADS):
        cols = pl.ds(head * HD, HD)
        product = output_rows[:, cols].astype(F32) * output_grad[:, cols].astype(F32)
        delta[head] = jnp.sum(product.T, axis=0, keepdims=True)
    query_total[...] = jnp.zeros_like(query_total)
    load(scratch, own[:, :HD], own[:, HD:])
    attend(queries, output_grad, norm, delta, scratch, True)
    own_out[:, :HD] = key_total[...]
    own_out[:, HD:] = value_total[...]

    @pl.when(place[0] > 0)
    def _():
        load(scratch, before[:, :HD], before[:, HD:])
        attend(queries, output_grad, norm, delta, scratch, False)
        before_out[:, :HD] = key_total[...].astype(BF)
        before_out[:, HD:] = value_total[...].astype(BF)

    @pl.when(place[0] == 0)
    def _():
        before_out[...] = jnp.zeros_like(before_out)


def far_kernel(
    place, selection, queries, output_grad, norm, delta, query_near, chosen,
    query_out, chosen_out, keys, values, keys_t, query_total, key_total, value_total,
):
    scratch = (keys, values, keys_t, query_total, key_total, value_total)
    block = place[0]
    query_total[...] = query_near[...]
    for slot, pick in enumerate(others(selection, block)):

        @pl.when(pick < block)
        def _():
            load(
                scratch,
                chosen[:, slot, :, :HD].reshape(BLOCK, HD),
                chosen[:, slot, :, HD:].reshape(BLOCK, HD),
            )
            attend(queries, output_grad, norm, delta, scratch, False)
            chosen_out[:, slot, :, :HD] = key_total[...].reshape(BLOCKS, PIECE, HD).astype(BF)
            chosen_out[:, slot, :, HD:] = value_total[...].reshape(BLOCKS, PIECE, HD).astype(BF)

        @pl.when(pick >= block)
        def _():
            chosen_out[:, slot] = jnp.zeros((BLOCKS, PIECE, 2 * HD), BF)

    for head in range(HEADS):
        query_out[:, head * HD : (head + 1) * HD] = (query_total[head].T * SCALE).astype(BF)


def tile_scratch(with_query):
    shapes = [((BLOCK, HD), BF), ((BLOCK, HD), BF), ((HD, BLOCK), BF)]
    shapes += [((HEADS, HD, BLOCK), F32)] * with_query + [((BLOCK, HD), F32)] * 2
    return [pltpu.VMEM(shape, dtype) for shape, dtype in shapes]


def join_kernel(key_rows, value_rows, out):
    out[:, :HD] = key_rows[...]
    out[:, HD:] = value_rows[...]


def pack_kernel(place, query_weight, key_weight, value_weight, out):
    wide = HEADS * HD
    out[:, :wide] = query_weight[...]
    out[:, wide : wide + HD] = key_weight[...]
    out[:, wide + HD :] = value_weight[...]


def pack_weights(place, partner, *weights):
    rows = lambda step, place: (place[0] ^ (place[1] * OTHER) ^ partner, 0)
    shape = (BLOCK, (HEADS + 2) * HD)
    return pl.pallas_call(
        pack_kernel,
        grid_spec=pltpu.PrefetchScalarGridSpec(
            num_scalar_prefetch=1,
            grid=(1,),
            in_specs=[pl.BlockSpec((BLOCK, weight.shape[1]), rows) for weight in weights],
            out_specs=pl.BlockSpec(shape, lambda step, place: (0, 0)),
        ),
        out_shape=jax.ShapeDtypeStruct(shape, BF),
        cost_estimate=cost(0, 4 * shape[0] * shape[1]),
        compiler_params=pltpu.CompilerParams(vmem_limit_bytes=8 * MIB),
    )(place, *weights)


def unpack_kernel(place, *refs):
    direct, swapped, refs = refs[:PARTNERS], refs[PARTNERS : 2 * PARTNERS], refs[2 * PARTNERS :]
    own, (query_out, kept, sent, done) = (refs[:3], refs[3:6]), refs[6:]
    done[...] = jnp.zeros_like(done)
    wide = HEADS * HD

    def run(first, second):
        for side, (out, parts) in enumerate(((kept, first), (sent, second))):
            rows = slice(side * BLOCK, (side + 1) * BLOCK)
            query, key, value = own[side]
            query_out[rows, :wide] = query[...]
            out[:, :HD] = key[...]
            out[:, HD : 2 * HD] = value[...]
            for index, part in enumerate(parts):
                query_out[rows, (index + 1) * wide : (index + 2) * wide] = part[:, :wide]
                out[:, (index + 1) * 2 * HD : (index + 2) * 2 * HD] = part[:, wide:]

    @pl.when(place[1] == 0)
    def _():
        run(direct, swapped)

    @pl.when(place[1] == 1)
    def _():
        run(swapped, direct)


def unpack_weights(place, weights, direct, swapped):
    part = pl.BlockSpec((BLOCK, (HEADS + 2) * HD), lambda step, place: (0, 0))
    kept = [pl.BlockSpec((BLOCK, weight.shape[1]), lambda step, place: (place[0], 0)) for weight in weights]
    sent = [pl.BlockSpec((BLOCK, weight.shape[1]), lambda step, place: (place[0] ^ OTHER, 0)) for weight in weights]
    near = (BLOCK, (PARTNERS + 1) * 2 * HD)
    shapes = [(2 * BLOCK, (PARTNERS + 1) * HEADS * HD), near, near, (16, HD)]
    return pl.pallas_call(
        unpack_kernel,
        grid_spec=pltpu.PrefetchScalarGridSpec(
            num_scalar_prefetch=1,
            grid=(1,),
            in_specs=[part] * (2 * PARTNERS) + kept + sent,
            out_specs=[pl.BlockSpec(shape, lambda step, place: (0, 0)) for shape in shapes],
        ),
        out_shape=[jax.ShapeDtypeStruct(shape, BF) for shape in shapes],
        cost_estimate=cost(0, 4 * sum(rows * cols for rows, cols in shapes)),
        compiler_params=pltpu.CompilerParams(vmem_limit_bytes=32 * MIB),
    )(place, *direct, *swapped, *weights, *weights)


def join_queries_kernel(*refs):
    out = refs[-1]
    for index, part in enumerate(refs[: PARTNERS + 1]):
        out[:, index * HEADS * HD : (index + 1) * HEADS * HD] = part[...]


def join_queries(parts, after):
    shape = (BLOCK, (PARTNERS + 1) * HEADS * HD)
    whole = lambda shape: pl.BlockSpec(shape, lambda step: (0, 0))
    return pl.pallas_call(
        join_queries_kernel,
        grid=(1,),
        in_specs=[whole(part.shape) for part in parts] + [pl.BlockSpec(memory_space=pl.ANY)],
        out_specs=whole(shape),
        out_shape=jax.ShapeDtypeStruct(shape, BF),
        cost_estimate=cost(0, 4 * shape[0] * shape[1]),
        compiler_params=pltpu.CompilerParams(vmem_limit_bytes=12 * MIB),
    )(*parts, after)


def cost(flops, size):
    return pl.CostEstimate(flops=flops, bytes_accessed=size, transcendentals=0)


def over_x(value, partner):
    return lax.ppermute(value, "grp", [(source, source ^ partner) for source in range(GROUPS)])


def gather_over_x(value):
    return [value] + [over_x(value, partner) for partner in range(1, PARTNERS + 1)]


def product(left, right):
    return lax.dot_general(left, right, NT, preferred_element_type=F32)


def on_device(
    queries, key_rows, value_rows, output_rows, output_grad, log_normalizer, selection,
    query_weight, key_weight, value_weight,
):
    smem = pl.BlockSpec(memory_space=pltpu.SMEM)
    vmem = pl.BlockSpec(memory_space=pltpu.VMEM)
    hbm = pl.BlockSpec(memory_space=pl.ANY)
    small, large = [pltpu.CompilerParams(vmem_limit_bytes=size * MIB) for size in (4, 24)]
    index = lax.axis_index("ctx").astype(jnp.int32)
    place = index.reshape(1)
    group = jnp.stack([lax.axis_index("grp").astype(jnp.int32), index % 2])
    count = lax.axis_size("ctx")
    norm = log_normalizer.T.reshape(HEADS, 1, BLOCK)
    rows, pieces_shape = (BLOCK, 2 * HD), (BLOCKS, SLOTS, PIECE, 2 * HD)
    tile_flops = 10 * HEADS * HD * BLOCK * BLOCK

    own = pl.pallas_call(
        join_kernel,
        in_specs=[vmem, vmem],
        out_specs=vmem,
        out_shape=jax.ShapeDtypeStruct(rows, BF),
        cost_estimate=cost(0, 8 * BLOCK * HD),
        compiler_params=small,
    )(key_rows, value_rows)
    weights = (query_weight, key_weight, value_weight)
    packed = [pack_weights(group, partner, *weights) for partner in range(1, PARTNERS + 1)]
    direct = [over_x(part, index + 1) for index, part in enumerate(packed)]
    before = lax.ppermute(own, "ctx", [(i, (i + 1) % count) for i in range(count)])
    pieces = lax.all_to_all(own.reshape(BLOCKS, PIECE, 2 * HD), "ctx", 0, 0)
    picked = pl.pallas_call(
        pick_kernel,
        in_specs=[smem, vmem] + [hbm] * PARTNERS,
        out_specs=vmem,
        out_shape=jax.ShapeDtypeStruct(pieces_shape, BF),
        cost_estimate=cost(0, 12 * BLOCK * HD),
        compiler_params=small,
    )(selection, pieces, *packed)
    chosen = lax.all_to_all(picked, "ctx", 0, 0)

    whole = lambda shape: pl.BlockSpec(shape, lambda step: (0,) * len(shape))
    near_in = (queries, output_grad, output_rows, norm, own, before)
    delta, query_near, own_grad, before_grad = pl.pallas_call(
        near_kernel,
        grid=(1,),
        in_specs=[smem] + [whole(array.shape) for array in near_in],
        out_specs=[whole((HEADS, 1, BLOCK)), whole((HEADS, HD, BLOCK)), whole(rows), whole(rows)],
        out_shape=[
            jax.ShapeDtypeStruct((HEADS, 1, BLOCK), F32),
            jax.ShapeDtypeStruct((HEADS, HD, BLOCK), F32),
            jax.ShapeDtypeStruct(rows, F32),
            jax.ShapeDtypeStruct(rows, BF),
        ],
        scratch_shapes=tile_scratch(0),
        cost_estimate=cost(6 * tile_flops, 1 << 22),
        compiler_params=large,
    )(place, *near_in)
    before_sum = lax.ppermute(before_grad, "ctx", [(i, (i - 1) % count) for i in range(count)])

    far_in = (queries, output_grad, norm, delta, query_near, chosen)
    query_grad, chosen_grad = pl.pallas_call(
        far_kernel,
        grid=(1,),
        in_specs=[smem, smem] + [whole(array.shape) for array in far_in],
        out_specs=[whole((BLOCK, HEADS * HD)), whole(pieces_shape)],
        out_shape=[
            jax.ShapeDtypeStruct((BLOCK, HEADS * HD), BF),
            jax.ShapeDtypeStruct(pieces_shape, BF),
        ],
        scratch_shapes=tile_scratch(1),
        cost_estimate=cost(6 * tile_flops, 1 << 22),
        compiler_params=large,
    )(place, selection, *far_in)

    returned = lax.all_to_all(chosen_grad, "ctx", 0, 0)
    *direct, query_grad = lax.optimization_barrier((*direct, query_grad))
    swapped = [lax.ppermute(part, "ctx", [(i, i ^ 1) for i in range(count)]) for part in direct]
    query_all_weight, near_kept, near_sent, done = unpack_weights(group, weights, direct, swapped)
    query_parts = gather_over_x(query_grad)
    collected = pl.pallas_call(
        collect_kernel,
        in_specs=[smem, vmem, hbm],
        out_specs=vmem,
        out_shape=jax.ShapeDtypeStruct((BLOCKS, PIECE, 2 * HD), BF),
        scratch_shapes=[pltpu.VMEM((BLOCKS, PIECE, 2 * HD), F32)],
        cost_estimate=cost(0, 12 * BLOCK * HD),
        compiler_params=small,
    )(selection, returned, done)
    part = product(join_queries(query_parts, collected), query_all_weight)
    kept_part, sent_part = part[:, :BLOCK], part[:, BLOCK:]
    chosen_sum = lax.all_to_all(collected, "ctx", 0, 0).reshape(rows)
    factor = jnp.where(lax.broadcasted_iota(jnp.int32, rows, 1) < HD, SCALE, 1.0)
    near_grad = ((own_grad + before_sum.astype(F32) + chosen_sum.astype(F32)) * factor).astype(BF)
    half = BLOCK // HALVES
    pairs = [(source, source ^ OTHER) for source in range(GROUPS)]
    near_parts = [gather_over_x(near_grad[i * half : (i + 1) * half]) for i in range(HALVES)]
    outs = []
    for i, near_all in enumerate(near_parts):
        some = slice(i * half, (i + 1) * half)
        near_all = jnp.concatenate(near_all, axis=1)
        sent = (sent_part[some] + product(near_all, near_sent)).astype(BF)
        got = lax.ppermute(sent, "grp", pairs)
        outs.append((kept_part[some] + product(near_all, near_kept) + got.astype(F32)).astype(BF))
    return jnp.concatenate(outs, axis=0)


def solution(mesh):
    tokens = P("ctx", "grp")
    return jax.shard_map(
        on_device,
        mesh=mesh,
        in_specs=(tokens,) * 6 + (P(),) + (P(None, "grp"),) * 3,
        out_specs=tokens,
        check_vma=False,
    )
```

time: 163 us -> 141 us (0.87)
  waiting for transfers between devices: 70 us -> 32.3 us
  blocking collectives: 27.1 us -> 0 us
  starting transfers between devices: 29.1 us -> 54.3 us
  local copies, waits for them, and re-layouts: 7.57 us -> 22.2 us
  matrix products: 0 us -> 6.56 us
  Pallas kernels: 25.4 us -> 23.4 us
    all_to_all x1 -> x0, blocking collectives: 27.1 us -> none  [on_device(): returned = lax.all_to_all(chosen_grad, 'ctx', 0, 0)]
    unnamed x24 -> x61, local copies, waits for them, and re-layouts: 3.3 us -> 22.2 us
    all_to_all x1 -> x2, starting transfers between devices: 4.09 us -> 16.8 us  [the longest x1 8.5 us: on_device(): returned = lax.all_to_all(chosen_grad, 'ctx', 0, 0)]
    ppermute x9 -> x17, starting transfers between devices: 10.6 us -> 22.2 us  [the longest x12 19 us: over_x(): lax.ppermute(value, 'grp', [(source, source ^ partner) for source in rang...]
    ppermute x9 -> x17, waiting for transfers between devices: 29 us -> 20.4 us  [the longest x12 12.3 us: over_x(): lax.ppermute(value, 'grp', [(source, source ^ partner) for source in rang...]
    ppermute x1, waiting for transfers between devices: 7.85 us -> 0.01 us  [on_device(): lax.ppermute(own, 'ctx', [(i, (i + 1) % count) for i in range(count)])]
    all_to_all x1, waiting for transfers between devices: 11.3 us -> 3.57 us  [on_device(): pieces = lax.all_to_all(own.reshape(BLOCKS, PIECE, 2 * HD), 'ctx', 0, 0)]
    all_to_all x1, waiting for transfers between devices: 9.88 us -> 3.15 us  [on_device(): chosen = lax.all_to_all(picked, 'ctx', 0, 0)]
  transfers between devices with their start and end apart: 14 -> 23, of which waited for: 9 -> 11; matrix products, arithmetic and copies ran while one was open for 0% -> 4% of each run, Pallas kernels for 0% -> 16%
where the time goes in v2:
time: 141 us; the launch traced here: 140 us
  starting transfers between devices  54.3 us (39%)
  waiting for transfers between devices  32.3 us (23%)
  Pallas kernels  23.4 us (17%)
  local copies, waits for them, and re-layouts  22.2 us (16%)
  matrix products  6.56 us (5%)
    unnamed x61, local copies, waits for them, and re-layouts  22.2 us
    ppermute x12, starting transfers between devices, over_x(): lax.ppermute(value, 'grp', [(source, source ^ partner) for source in rang...  19 us
    ppermute x12, waiting for transfers between devices, over_x(): lax.ppermute(value, 'grp', [(source, source ^ partner) for source in rang...  12.3 us
    all_to_all x1, starting transfers between devices, on_device(): pieces = lax.all_to_all(own.reshape(BLOCKS, PIECE, 2 * HD), 'ctx', 0, 0)  10.1 us
    all_to_all x1, starting transfers between devices, on_device(): returned = lax.all_to_all(chosen_grad, 'ctx', 0, 0)  8.5 us
    all_to_all x1, starting transfers between devices, on_device(): chosen_sum = lax.all_to_all(collected, 'ctx', 0, 0).reshape(rows)  8.27 us
    ppermute x2, waiting for transfers between devices, on_device(): got = lax.ppermute(sent, 'grp', pairs)  8.08 us
    dot_general x5, matrix products, product(): return lax.dot_general(left, right, NT, preferred_element_type=F32)  6.56 us
  transfers between devices with their start and end apart: 23, of which 11 were waited for; matrix products, arithmetic and copies ran while one was open for 4% of the time, Pallas kernels for 16%

profile of v2, /device:TPU:24, one launch (start us, length us, event | category | flops | bytes accessed | tf_op | source)
XLA Modules:
  0.0 140.1 jit_solution(12678508544673923306)
XLA Ops:
  2.6 10.1 %all-to-all-start = ((bf16[32,16,256]{2,1,0:T(8,128)(2,1)}), bf16[32,16,256]{2,1,0:T(8,128)(2,1)S(1)}, u32[]{:S(2)}, u32[]{:S(2)}) async-start(bf16[32,16,256]{2,1,0:T(8,128)(2,1)} %bitcast.4), calls=%async_computation | async-start | bytes 524288 | tf_op jit(solution)/shard_map/all_to_all | solution.py:294
  13.0 2.2 %copy-done = bf16[4096,512]{1,0:T(8,128)(2,1)S(1)} copy-done((bf16[4096,512]{1,0:T(8,128)(2,1)S(1)}, bf16[4096,512]{1,0:T(8,128)(2,1)}, u32[]{:S(2)}) %copy-start) | copy-done | bytes 4194328
  21.4 3.6 %all-to-all-done.pieces = bf16[32,16,256]{2,1,0:T(8,128)(2,1)S(1)} async-done(((bf16[32,16,256]{2,1,0:T(8,128)(2,1)}), bf16[32,16,256]{2,1,0:T(8,128)(2,1)S(1)}, u32[]{:S(2)}, u32[]{:S(2)}) %all-to-all-start) | async-done | bytes 262176 | tf_op jit(solution)/shard_map/all_to_all | solution.py:294
  26.9 4.9 %all-to-all-start.1 = ((bf16[32,2,16,256]{3,2,1,0:T(8,128)(2,1)}), bf16[32,2,16,256]{3,2,1,0:T(8,128)(2,1)S(1)}, u32[]{:S(2)}, u32[]{:S(2)}) async-start(bf16[32,2,16,256]{3,2,1,0:T(8,128)(2,1)} %shard_map.105), calls=%async_computation.1 | async-start | bytes 1048576 | tf_op jit(solution)/shard_map/all_to_all | solution.py:303
  33.4 2.7 %collective-permute-start.1 = (bf16[512,768]{1,0:T(8,128)(2,1)}, bf16[512,768]{1,0:T(8,128)(2,1)}, u32[]{:S(2)}, u32[]{:S(2)}) collective-permute-start(bf16[512,768]{1,0:T(8,128)(2,1)} %shard_map.101.refs_1_), channel_id=1, source_target_pairs={{0,2},{1,3},{2,0},{3,1},{4,6},{5,7},{6,4},{7,5},{8,10},{9,11},{10,... | collective-permute-start | bytes 2359304 | tf_op jit(solution)/shard_map/ppermute | solution.py:255
  38.3 6.2 %shard_map.104 = (f32[4,1,512]{2,1,0:T(1,128)S(1)}, f32[4,128,512]{2,1,0:T(8,128)S(1)}, f32[512,256]{1,0:T(8,128)S(1)}, bf16[512,256]{1,0:T(8,128)(2,1)S(1)}) custom-call(s32[1]{0:T(128)} %bitcast.2.place, bf16[512,512]{1,0:T(8,128)(2,1)S(1)} %copy-done.19, bf16[512,512]{1,0:T(8,128)(2,1)S(1)} %copy-done.21, bf16[512,512]{1,0:T(8,128)(2,1)S(1)} %copy-done.18, ...), custom_call_target="tpu_custom_call" | custom-call | flops 8053063680 | bytes 4194304 | tf_op jit(solution)/shard_map/pallas_call | solution.py:307
  46.3 3.1 %all-to-all-done.1.chosen = bf16[32,2,16,256]{3,2,1,0:T(8,128)(2,1)S(1)} async-done(((bf16[32,2,16,256]{3,2,1,0:T(8,128)(2,1)}), bf16[32,2,16,256]{3,2,1,0:T(8,128)(2,1)S(1)}, u32[]{:S(2)}, u32[]{:S(2)}) %all-to-all-start.1) | async-done | bytes 524320 | tf_op jit(solution)/shard_map/all_to_all | solution.py:303
  52.8 4.1 %shard_map.106 = (bf16[512,512]{1,0:T(8,128)(2,1)S(1)}, bf16[32,2,16,256]{3,2,1,0:T(8,128)(2,1)S(1)}) custom-call(s32[1]{0:T(128)} %bitcast.2.place, s32[32,3]{1,0:T(8,128)S(1)} %copy.12.selection, bf16[512,512]{1,0:T(8,128)(2,1)S(1)} %copy-done.20, bf16[512,512]{1,0:T(8,128)(2,1)S(1)} %copy-done.22, f32[4,1,512]{2,1,0:T(1,128)S(1)} %reshape.13.norm, ...), custom_call_target="tpu_custom_call" | custom-call | flops 8053063680 | bytes 4194304 | tf_op jit(solution)/shard_map/pallas_call | solution.py:325
  58.5 8.5 %all-to-all-start.2 = ((bf16[32,2,16,256]{3,2,1,0:T(8,128)(2,1)}), bf16[32,2,16,256]{3,2,1,0:T(8,128)(2,1)S(1)}, u32[]{:S(2)}, u32[]{:S(2)}) async-start(bf16[32,2,16,256]{3,2,1,0:T(8,128)(2,1)} %copy-done.10), calls=%async_computation.2 | async-start | bytes 1048576 | tf_op jit(solution)/shard_map/all_to_all | solution.py:339
  67.0 3.9 %collective-permute-done.1.refs_1_ = bf16[512,768]{1,0:T(8,128)(2,1)} collective-permute-done((bf16[512,768]{1,0:T(8,128)(2,1)}, bf16[512,768]{1,0:T(8,128)(2,1)}, u32[]{:S(2)}, u32[]{:S(2)}) %collective-permute-start.1) | collective-permute-done | bytes 786464 | tf_op jit(solution)/shard_map/ppermute | solution.py:255
  70.9 2.4 %collective-permute-done.2.refs_2_ = bf16[512,768]{1,0:T(8,128)(2,1)} collective-permute-done((bf16[512,768]{1,0:T(8,128)(2,1)S(1)}, bf16[512,768]{1,0:T(8,128)(2,1)}, u32[]{:S(2)}, u32[]{:S(2)}) %collective-permute-start.2) | collective-permute-done | bytes 786464 | tf_op jit(solution)/shard_map/ppermute | solution.py:255
  75.8 2.7 %collective-permute-start.6 = (bf16[512,512]{1,0:T(8,128)(2,1)}, bf16[512,512]{1,0:T(8,128)(2,1)}, u32[]{:S(2)}, u32[]{:S(2)}) collective-permute-start(bf16[512,512]{1,0:T(8,128)(2,1)} %copy-done.6), channel_id=1, source_target_pairs={{0,3},{1,2},{2,1},{3,0},{4,7},{5,6},{6,5},{7,4},{8,11},{9,10},{10,... | collective-permute-start | bytes 1572872 | tf_op jit(solution)/shard_map/ppermute | solution.py:255
  78.6 2.2 %copy-done.1 = bf16[4096,512]{1,0:T(8,128)(2,1)S(1)} copy-done((bf16[4096,512]{1,0:T(8,128)(2,1)S(1)}, bf16[4096,512]{1,0:T(8,128)(2,1)}, u32[]{:S(2)}) %copy-start.1) | copy-done | bytes 4194328
  80.7 2.8 %shard_map.107 = (bf16[1024,2048]{1,0:T(8,128)(2,1)S(1)}, bf16[512,1024]{1,0:T(8,128)(2,1)S(1)}, bf16[512,1024]{1,0:T(8,128)(2,1)S(1)}, bf16[16,128]{1,0:T(8,128)(2,1)S(1)}) custom-call(s32[2]{0:T(128)S(1)} %pad_add_fusion.place, bf16[512,768]{1,0:T(8,128)(2,1)} %collective-permute-done.refs_0_, bf16[512,768]{1,0:T(8,128)(2,1)} %collective-permute-done.1.refs_1_, ...), custom_call_target="tpu_custom_call" | custom-call | bytes 12591104 | tf_op jit(solution)/shard_map/pallas_call | solution.py:216
  83.6 2.0 %copy-done.13 = bf16[1024,2048]{1,0:T(8,128)(2,1)} copy-done((bf16[1024,2048]{1,0:T(8,128)(2,1)}, bf16[1024,2048]{1,0:T(8,128)(2,1)S(1)}, u32[]{:S(2)}) %copy-start.13) | copy-done | bytes 4194328
  87.6 2.4 %shard_map.108.refs_4_ = bf16[32,16,256]{2,1,0:T(8,128)(2,1)} custom-call(s32[32,3]{1,0:T(8,128)S(1)} %copy.12.selection, bf16[32,2,16,256]{3,2,1,0:T(8,128)(2,1)S(1)} %all-to-all-done.2.parts, bf16[16,128]{1,0:T(8,128)(2,1)S(1)} %get-tuple-element.27.refs_0_), custom_call_target="tpu_custom_call" | custom-call | bytes 786432 | tf_op jit(solution)/shard_map/pallas_call | solution.py:344
  89.9 8.3 %all-to-all-start.3 = ((bf16[32,16,256]{2,1,0:T(8,128)(2,1)}), bf16[32,16,256]{2,1,0:T(8,128)(2,1)S(1)}, u32[]{:S(2)}, u32[]{:S(2)}) async-start(bf16[32,16,256]{2,1,0:T(8,128)(2,1)} %shard_map.108.refs_4_), calls=%async_computation.3 | async-start | bytes 524288 | tf_op jit(solution)/shard_map/all_to_all | solution.py:355
  99.7 2.8 %collective-permute-done.6.refs_3_ = bf16[512,512]{1,0:T(8,128)(2,1)} collective-permute-done((bf16[512,512]{1,0:T(8,128)(2,1)}, bf16[512,512]{1,0:T(8,128)(2,1)}, u32[]{:S(2)}, u32[]{:S(2)}) %collective-permute-start.6) | collective-permute-done | bytes 524320 | tf_op jit(solution)/shard_map/ppermute | solution.py:255
  105.2 5.2 %all-to-all-done.3 = bf16[32,16,256]{2,1,0:T(8,128)(2,1)S(1)} async-done(((bf16[32,16,256]{2,1,0:T(8,128)(2,1)}), bf16[32,16,256]{2,1,0:T(8,128)(2,1)S(1)}, u32[]{:S(2)}, u32[]{:S(2)}) %all-to-all-start.3) | async-done | bytes 262176 | tf_op jit(solution)/shard_map/all_to_all | solution.py:355
  112.5 2.7 %collective-permute-start.13 = (bf16[256,256]{1,0:T(8,128)(2,1)S(1)}, bf16[256,256]{1,0:T(8,128)(2,1)S(1)}, u32[]{:S(2)}, u32[]{:S(2)}) collective-permute-start(bf16[256,256]{1,0:T(8,128)(2,1)S(1)} %get-tuple-element.33), channel_id=1, source_target_pairs={{0,3},{1,2},{2,1},{3,0},{4,7},{5,6},{6,5},{7,4},{8,11},{9,10},{10,... | collective-permute-start | bytes 393224 | tf_op jit(solution)/shard_map/ppermute | solution.py:255
  115.2 4.6 %fusion.17 = f32[512,1024]{1,0:T(8,128)S(1)} fusion(bf16[512,2048]{1,0:T(8,128)(2,1)S(1)} %shard_map.109, bf16[1024,2048]{1,0:T(8,128)(2,1)} %copy-done.13), kind=kOutput, calls=%fused_computation.27 | convolution fusion | flops 2147483648 | bytes 8388608 | tf_op jit(solution)/shard_map/dot_general | solution.py:263
  122.0 2.7 %collective-permute-start.17 = (bf16[256,256]{1,0:T(8,128)(2,1)S(1)}, bf16[256,256]{1,0:T(8,128)(2,1)S(1)}, u32[]{:S(2)}, u32[]{:S(2)}) collective-permute-start(bf16[256,256]{1,0:T(8,128)(2,1)S(1)} %get-tuple-element.34), channel_id=1, source_target_pairs={{0,3},{1,2},{2,1},{3,0},{4,7},{5,6},{6,5},{7,4},{8,11},{9,10},{10,... | collective-permute-start | bytes 393224 | tf_op jit(solution)/shard_map/ppermute | solution.py:255
  130.2 4.4 %collective-permute-done.14 = bf16[256,512]{1,0:T(8,128)(2,1)S(1)} collective-permute-done((bf16[256,512]{1,0:T(8,128)(2,1)S(1)}, bf16[256,512]{1,0:T(8,128)(2,1)S(1)}, u32[]{:S(2)}, u32[]{:S(2)}) %collective-permute-start.14) | collective-permute-done | bytes 262176 | tf_op jit(solution)/shard_map/ppermute | solution.py:366
  135.0 3.7 %collective-permute-done.18 = bf16[256,512]{1,0:T(8,128)(2,1)S(1)} collective-permute-done((bf16[256,512]{1,0:T(8,128)(2,1)S(1)}, bf16[256,512]{1,0:T(8,128)(2,1)S(1)}, u32[]{:S(2)}, u32[]{:S(2)}) %collective-permute-start.18) | collective-permute-done | bytes 262176 | tf_op jit(solution)/shard_map/ppermute | solution.py:366
  (104 shorter events, 41.7 us)
Async XLA Ops:
  2.6 22.4 %all-to-all-start = ((bf16[32,16,256]{2,1,0:T(8,128)(2,1)}), bf16[32,16,256]{2,1,0:T(8,128)(2,1)S(1)}, u32[]{:S(2)}, u32[]{:S(2)}) async-start(bf16[32,16,256]{2,1,0:T(8,128)(2,1)} %bitcast.4), calls=%async_computation | async-start | bytes 524288 | tf_op jit(solution)/shard_map/all_to_all | solution.py:294
  12.7 23.9 %collective-permute-start.3 = (bf16[512,256]{1,0:T(8,128)(2,1)}, bf16[512,256]{1,0:T(8,128)(2,1)S(1)}, u32[]{:S(2)}, u32[]{:S(2)}) collective-permute-start(bf16[512,256]{1,0:T(8,128)(2,1)} %shard_map.103.own), channel_id=1, source_target_pairs={{0,8},{8,16},{16,24},{24,32},{32,40},{40,48},{48,56},{56,64},{64,7... | collective-permute-start | bytes 786440 | tf_op jit(solution)/shard_map/ppermute | solution.py:293
  26.9 22.6 %all-to-all-start.1 = ((bf16[32,2,16,256]{3,2,1,0:T(8,128)(2,1)}), bf16[32,2,16,256]{3,2,1,0:T(8,128)(2,1)S(1)}, u32[]{:S(2)}, u32[]{:S(2)}) async-start(bf16[32,2,16,256]{3,2,1,0:T(8,128)(2,1)} %shard_map.105), calls=%async_computation.1 | async-start | bytes 1048576 | tf_op jit(solution)/shard_map/all_to_all | solution.py:303
  31.8 35.2 %collective-permute-start = (bf16[512,768]{1,0:T(8,128)(2,1)}, bf16[512,768]{1,0:T(8,128)(2,1)}, u32[]{:S(2)}, u32[]{:S(2)}) collective-permute-start(bf16[512,768]{1,0:T(8,128)(2,1)} %shard_map.100.refs_0_), channel_id=1, source_target_pairs={{0,1},{1,0},{2,3},{3,2},{4,5},{5,4},{6,7},{7,6},{8,9},{9,8},{10,11... | collective-permute-start | bytes 2359304 | tf_op jit(solution)/shard_map/ppermute | solution.py:255
  33.4 37.6 %collective-permute-start.1 = (bf16[512,768]{1,0:T(8,128)(2,1)}, bf16[512,768]{1,0:T(8,128)(2,1)}, u32[]{:S(2)}, u32[]{:S(2)}) collective-permute-start(bf16[512,768]{1,0:T(8,128)(2,1)} %shard_map.101.refs_1_), channel_id=1, source_target_pairs={{0,2},{1,3},{2,0},{3,1},{4,6},{5,7},{6,4},{7,5},{8,10},{9,11},{10,... | collective-permute-start | bytes 2359304 | tf_op jit(solution)/shard_map/ppermute | solution.py:255
  36.1 37.2 %collective-permute-start.2 = (bf16[512,768]{1,0:T(8,128)(2,1)S(1)}, bf16[512,768]{1,0:T(8,128)(2,1)}, u32[]{:S(2)}, u32[]{:S(2)}) collective-permute-start(bf16[512,768]{1,0:T(8,128)(2,1)S(1)} %shard_map.102.refs_2_), channel_id=1, source_target_pairs={{0,3},{1,2},{2,1},{3,0},{4,7},{5,6},{6,5},{7,4},{8,11},{9,10},{10,... | collective-permute-start | bytes 2359304 | tf_op jit(solution)/shard_map/ppermute | solution.py:255
  52.8 25.7 %copy-start.5 = (bf16[4096,128]{1,0:T(8,128)(2,1)S(1)}, bf16[4096,128]{1,0:T(8,128)(2,1)}, u32[]{:S(2)}) copy-start(bf16[4096,128]{1,0:T(8,128)(2,1)} %refs_11_.1) | copy-start | bytes 3145732
  58.5 29.1 %all-to-all-start.2 = ((bf16[32,2,16,256]{3,2,1,0:T(8,128)(2,1)}), bf16[32,2,16,256]{3,2,1,0:T(8,128)(2,1)S(1)}, u32[]{:S(2)}, u32[]{:S(2)}) async-start(bf16[32,2,16,256]{3,2,1,0:T(8,128)(2,1)} %copy-done.10), calls=%async_computation.2 | async-start | bytes 1048576 | tf_op jit(solution)/shard_map/all_to_all | solution.py:339
  73.3 2.5 %collective-permute-start.7 = (bf16[512,768]{1,0:T(8,128)(2,1)}, bf16[512,768]{1,0:T(8,128)(2,1)S(1)}, u32[]{:S(2)}, u32[]{:S(2)}) collective-permute-start(bf16[512,768]{1,0:T(8,128)(2,1)} %collective-permute-done.refs_0_), channel_id=1, source_target_pairs={{0,8},{8,0},{16,24},{24,16},{32,40},{40,32},{48,56},{56,48},{64,72... | collective-permute-start | bytes 2359304 | tf_op jit(solution)/shard_map/ppermute | solution.py:341
  73.3 5.2 %collective-permute-start.8 = (bf16[512,768]{1,0:T(8,128)(2,1)}, bf16[512,768]{1,0:T(8,128)(2,1)S(1)}, u32[]{:S(2)}, u32[]{:S(2)}) collective-permute-start(bf16[512,768]{1,0:T(8,128)(2,1)} %collective-permute-done.1.refs_1_), channel_id=1, source_target_pairs={{0,8},{8,0},{16,24},{24,16},{32,40},{40,32},{48,56},{56,48},{64,72... | collective-permute-start | bytes 2359304 | tf_op jit(solution)/shard_map/ppermute | solution.py:341
  73.8 4.7 %collective-permute-start.9 = (bf16[512,768]{1,0:T(8,128)(2,1)}, bf16[512,768]{1,0:T(8,128)(2,1)S(1)}, u32[]{:S(2)}, u32[]{:S(2)}) collective-permute-start(bf16[512,768]{1,0:T(8,128)(2,1)} %collective-permute-done.2.refs_2_), channel_id=1, source_target_pairs={{0,8},{8,0},{16,24},{24,16},{32,40},{40,32},{48,56},{56,48},{64,72... | collective-permute-start | bytes 2359304 | tf_op jit(solution)/shard_map/ppermute | solution.py:341
  73.8 24.6 %collective-permute-start.4 = (bf16[512,512]{1,0:T(8,128)(2,1)}, bf16[512,512]{1,0:T(8,128)(2,1)}, u32[]{:S(2)}, u32[]{:S(2)}) collective-permute-start(bf16[512,512]{1,0:T(8,128)(2,1)} %copy-done.6), channel_id=1, source_target_pairs={{0,1},{1,0},{2,3},{3,2},{4,5},{5,4},{6,7},{7,6},{8,9},{9,8},{10,11... | collective-permute-start | bytes 1572872 | tf_op jit(solution)/shard_map/ppermute | solution.py:255
  73.8 25.9 %collective-permute-start.5 = (bf16[512,512]{1,0:T(8,128)(2,1)}, bf16[512,512]{1,0:T(8,128)(2,1)}, u32[]{:S(2)}, u32[]{:S(2)}) collective-permute-start(bf16[512,512]{1,0:T(8,128)(2,1)} %copy-done.6), channel_id=1, source_target_pairs={{0,2},{1,3},{2,0},{3,1},{4,6},{5,7},{6,4},{7,5},{8,10},{9,11},{10,... | collective-permute-start | bytes 1572872 | tf_op jit(solution)/shard_map/ppermute | solution.py:255
  75.8 26.7 %collective-permute-start.6 = (bf16[512,512]{1,0:T(8,128)(2,1)}, bf16[512,512]{1,0:T(8,128)(2,1)}, u32[]{:S(2)}, u32[]{:S(2)}) collective-permute-start(bf16[512,512]{1,0:T(8,128)(2,1)} %copy-done.6), channel_id=1, source_target_pairs={{0,3},{1,2},{2,1},{3,0},{4,7},{5,6},{6,5},{7,4},{8,11},{9,10},{10,... | collective-permute-start | bytes 1572872 | tf_op jit(solution)/shard_map/ppermute | solution.py:255
  89.9 20.4 %all-to-all-start.3 = ((bf16[32,16,256]{2,1,0:T(8,128)(2,1)}), bf16[32,16,256]{2,1,0:T(8,128)(2,1)S(1)}, u32[]{:S(2)}, u32[]{:S(2)}) async-start(bf16[32,16,256]{2,1,0:T(8,128)(2,1)} %shard_map.108.refs_4_), calls=%async_computation.3 | async-start | bytes 524288 | tf_op jit(solution)/shard_map/all_to_all | solution.py:355
  98.2 6.9 %collective-permute-start.10 = (bf16[512,256]{1,0:T(8,128)(2,1)}, bf16[512,256]{1,0:T(8,128)(2,1)S(1)}, u32[]{:S(2)}, u32[]{:S(2)}) collective-permute-start(bf16[512,256]{1,0:T(8,128)(2,1)} %copy-done.23), channel_id=1, source_target_pairs={{0,248},{8,0},{16,8},{24,16},{32,24},{40,32},{48,40},{56,48},{64,5... | collective-permute-start | bytes 786440 | tf_op jit(solution)/shard_map/ppermute | solution.py:322
  110.5 11.5 %collective-permute-start.11 = (bf16[256,256]{1,0:T(8,128)(2,1)S(1)}, bf16[256,256]{1,0:T(8,128)(2,1)S(1)}, u32[]{:S(2)}, u32[]{:S(2)}) collective-permute-start(bf16[256,256]{1,0:T(8,128)(2,1)S(1)} %get-tuple-element.33), channel_id=1, source_target_pairs={{0,1},{1,0},{2,3},{3,2},{4,5},{5,4},{6,7},{7,6},{8,9},{9,8},{10,11... | collective-permute-start | bytes 393224 | tf_op jit(solution)/shard_map/ppermute | solution.py:255
  110.6 14.1 %collective-permute-start.12 = (bf16[256,256]{1,0:T(8,128)(2,1)S(1)}, bf16[256,256]{1,0:T(8,128)(2,1)S(1)}, u32[]{:S(2)}, u32[]{:S(2)}) collective-permute-start(bf16[256,256]{1,0:T(8,128)(2,1)S(1)} %get-tuple-element.33), channel_id=1, source_target_pairs={{0,2},{1,3},{2,0},{3,1},{4,6},{5,7},{6,4},{7,5},{8,10},{9,11},{10,... | collective-permute-start | bytes 393224 | tf_op jit(solution)/shard_map/ppermute | solution.py:255
  112.5 12.2 %collective-permute-start.13 = (bf16[256,256]{1,0:T(8,128)(2,1)S(1)}, bf16[256,256]{1,0:T(8,128)(2,1)S(1)}, u32[]{:S(2)}, u32[]{:S(2)}) collective-permute-start(bf16[256,256]{1,0:T(8,128)(2,1)S(1)} %get-tuple-element.33), channel_id=1, source_target_pairs={{0,3},{1,2},{2,1},{3,0},{4,7},{5,6},{6,5},{7,4},{8,11},{9,10},{10,... | collective-permute-start | bytes 393224 | tf_op jit(solution)/shard_map/ppermute | solution.py:255
  119.9 6.6 %collective-permute-start.15 = (bf16[256,256]{1,0:T(8,128)(2,1)S(1)}, bf16[256,256]{1,0:T(8,128)(2,1)S(1)}, u32[]{:S(2)}, u32[]{:S(2)}) collective-permute-start(bf16[256,256]{1,0:T(8,128)(2,1)S(1)} %get-tuple-element.34), channel_id=1, source_target_pairs={{0,1},{1,0},{2,3},{3,2},{4,5},{5,4},{6,7},{7,6},{8,9},{9,8},{10,11... | collective-permute-start | bytes 393224 | tf_op jit(solution)/shard_map/ppermute | solution.py:255
  120.0 7.0 %collective-permute-start.16 = (bf16[256,256]{1,0:T(8,128)(2,1)S(1)}, bf16[256,256]{1,0:T(8,128)(2,1)S(1)}, u32[]{:S(2)}, u32[]{:S(2)}) collective-permute-start(bf16[256,256]{1,0:T(8,128)(2,1)S(1)} %get-tuple-element.34), channel_id=1, source_target_pairs={{0,2},{1,3},{2,0},{3,1},{4,6},{5,7},{6,4},{7,5},{8,10},{9,11},{10,... | collective-permute-start | bytes 393224 | tf_op jit(solution)/shard_map/ppermute | solution.py:255
  122.0 6.4 %collective-permute-start.17 = (bf16[256,256]{1,0:T(8,128)(2,1)S(1)}, bf16[256,256]{1,0:T(8,128)(2,1)S(1)}, u32[]{:S(2)}, u32[]{:S(2)}) collective-permute-start(bf16[256,256]{1,0:T(8,128)(2,1)S(1)} %get-tuple-element.34), channel_id=1, source_target_pairs={{0,3},{1,2},{2,1},{3,0},{4,7},{5,6},{6,5},{7,4},{8,11},{9,10},{10,... | collective-permute-start | bytes 393224 | tf_op jit(solution)/shard_map/ppermute | solution.py:255
  125.2 9.4 %collective-permute-start.14 = (bf16[256,512]{1,0:T(8,128)(2,1)S(1)}, bf16[256,512]{1,0:T(8,128)(2,1)S(1)}, u32[]{:S(2)}, u32[]{:S(2)}) collective-permute-start(bf16[256,512]{1,0:T(8,128)(2,1)S(1)} %fusion.3), channel_id=1, source_target_pairs={{0,4},{1,5},{2,6},{3,7},{4,0},{5,1},{6,2},{7,3},{8,12},{9,13},{10,... | collective-permute-start | bytes 786440 | tf_op jit(solution)/shard_map/ppermute | solution.py:366
  128.9 9.9 %collective-permute-start.18 = (bf16[256,512]{1,0:T(8,128)(2,1)S(1)}, bf16[256,512]{1,0:T(8,128)(2,1)S(1)}, u32[]{:S(2)}, u32[]{:S(2)}) collective-permute-start(bf16[256,512]{1,0:T(8,128)(2,1)S(1)} %fusion), channel_id=1, source_target_pairs={{0,4},{1,5},{2,6},{3,7},{4,0},{5,1},{6,2},{7,3},{8,12},{9,13},{10,... | collective-permute-start | bytes 786440 | tf_op jit(solution)/shard_map/ppermute | solution.py:366
  (29 other events, 140.0 us)

commit v3 on v2

--- a/solution.py
+++ b/solution.py
@@ -16,10 +16,17 @@
 LOG2E = 1.4426950408889634
 BF = jnp.bfloat16
 F32 = jnp.float32
-MIB = 1024 * 1024
+VMEM_BYTES = 60 * 1024 * 1024
+PARAMS = pltpu.CompilerParams(vmem_limit_bytes=VMEM_BYTES)
+
+
+def params(mib):
+    return pltpu.CompilerParams(vmem_limit_bytes=mib * 1024 * 1024)
+
 
 PARTNERS = 3
 HALVES = 2
+TOKEN = (16, HD)
 OTHER = 4
 
 NT = (((1,), (1,)), ((), ()))
@@ -39,7 +46,7 @@
             out[block, slot] = pieces[chosen]
         return carry
 
-    lax.fori_loop(0, BLOCKS, step, 0)
+    lax.fori_loop(0, BLOCKS, step, 0, unroll=4)
 
 
 def collect_kernel(selection, parts, *refs):
@@ -55,7 +62,7 @@
 
         return carry
 
-    lax.fori_loop(0, BLOCKS, step, 0)
+    lax.fori_loop(0, BLOCKS, step, 0, unroll=4)
     out[...] = total[...].astype(BF)
 
 
@@ -120,8 +127,9 @@
 
 def far_kernel(
     place, selection, queries, output_grad, norm, delta, query_near, chosen,
-    query_out, chosen_out, keys, values, keys_t, query_total, key_total, value_total,
+    query_out, chosen_out, done, keys, values, keys_t, query_total, key_total, value_total,
 ):
+    done[...] = jnp.zeros_like(done)
     scratch = (keys, values, keys_t, query_total, key_total, value_total)
     block = place[0]
     query_total[...] = query_near[...]
@@ -157,33 +165,46 @@
     out[:, HD:] = value_rows[...]
 
 
-def pack_kernel(place, query_weight, key_weight, value_weight, out):
+def pack_kernel(place, *refs):
     wide = HEADS * HD
-    out[:, :wide] = query_weight[...]
-    out[:, wide : wide + HD] = key_weight[...]
-    out[:, wide + HD :] = value_weight[...]
-
-
-def pack_weights(place, partner, *weights):
-    rows = lambda step, place: (place[0] ^ (place[1] * OTHER) ^ partner, 0)
-    shape = (BLOCK, (HEADS + 2) * HD)
+    done = refs[-1]
+    done[...] = jnp.zeros_like(done)
+    for partner in range(PARTNERS):
+        query, key, value = refs[3 * partner : 3 * partner + 3]
+        out = refs[3 * PARTNERS + partner]
+        out[:, :wide] = query[...]
+        out[:, wide : wide + HD] = key[...]
+        out[:, wide + HD :] = value[...]
+
+
+def pack_weights(place, weights):
+    steps = 4
+    rows, width = BLOCK // steps, (HEADS + 2) * HD
+
+    def index(partner):
+        return lambda step, place: ((place[0] ^ (place[1] * OTHER) ^ partner) * steps + step, 0)
+
+    partners = range(1, PARTNERS + 1)
     return pl.pallas_call(
         pack_kernel,
         grid_spec=pltpu.PrefetchScalarGridSpec(
             num_scalar_prefetch=1,
-            grid=(1,),
-            in_specs=[pl.BlockSpec((BLOCK, weight.shape[1]), rows) for weight in weights],
-            out_specs=pl.BlockSpec(shape, lambda step, place: (0, 0)),
+            grid=(steps,),
+            in_specs=[
+                pl.BlockSpec((rows, weight.shape[1]), index(partner)) for partner in partners for weight in weights
+            ],
+            out_specs=[pl.BlockSpec((rows, width), lambda step, place: (step, 0))] * PARTNERS
+            + [pl.BlockSpec(TOKEN, lambda step, place: (0, 0))],
         ),
-        out_shape=jax.ShapeDtypeStruct(shape, BF),
-        cost_estimate=cost(0, 4 * shape[0] * shape[1]),
-        compiler_params=pltpu.CompilerParams(vmem_limit_bytes=8 * MIB),
-    )(place, *weights)
+        out_shape=[jax.ShapeDtypeStruct((BLOCK, width), BF)] * PARTNERS + [jax.ShapeDtypeStruct(TOKEN, BF)],
+        cost_estimate=cost(0, 4 * PARTNERS * BLOCK * width),
+        compiler_params=PARAMS,
+    )(place, *weights * PARTNERS)
 
 
 def unpack_kernel(place, *refs):
     direct, swapped, refs = refs[:PARTNERS], refs[PARTNERS : 2 * PARTNERS], refs[2 * PARTNERS :]
-    own, (query_out, kept, sent, done) = (refs[:3], refs[3:6]), refs[6:]
+    own, (query_out, kept, sent, done) = (refs[:3], refs[3:6]), refs[7:]
     done[...] = jnp.zeros_like(done)
     wide = HEADS * HD
 
@@ -207,24 +228,24 @@
         run(swapped, direct)
 
 
-def unpack_weights(place, weights, direct, swapped):
+def unpack_weights(place, weights, direct, swapped, after):
     part = pl.BlockSpec((BLOCK, (HEADS + 2) * HD), lambda step, place: (0, 0))
     kept = [pl.BlockSpec((BLOCK, weight.shape[1]), lambda step, place: (place[0], 0)) for weight in weights]
     sent = [pl.BlockSpec((BLOCK, weight.shape[1]), lambda step, place: (place[0] ^ OTHER, 0)) for weight in weights]
     near = (BLOCK, (PARTNERS + 1) * 2 * HD)
-    shapes = [(2 * BLOCK, (PARTNERS + 1) * HEADS * HD), near, near, (16, HD)]
+    shapes = [(2 * BLOCK, (PARTNERS + 1) * HEADS * HD), near, near, TOKEN]
     return pl.pallas_call(
         unpack_kernel,
         grid_spec=pltpu.PrefetchScalarGridSpec(
             num_scalar_prefetch=1,
             grid=(1,),
-            in_specs=[part] * (2 * PARTNERS) + kept + sent,
+            in_specs=[part] * (2 * PARTNERS) + kept + sent + [pl.BlockSpec(memory_space=pl.ANY)],
             out_specs=[pl.BlockSpec(shape, lambda step, place: (0, 0)) for shape in shapes],
         ),
         out_shape=[jax.ShapeDtypeStruct(shape, BF) for shape in shapes],
         cost_estimate=cost(0, 4 * sum(rows * cols for rows, cols in shapes)),
-        compiler_params=pltpu.CompilerParams(vmem_limit_bytes=32 * MIB),
-    )(place, *direct, *swapped, *weights, *weights)
+        compiler_params=PARAMS,
+    )(place, *direct, *swapped, *weights, *weights, after)
 
 
 def join_queries_kernel(*refs):
@@ -243,7 +264,7 @@
         out_specs=whole(shape),
         out_shape=jax.ShapeDtypeStruct(shape, BF),
         cost_estimate=cost(0, 4 * shape[0] * shape[1]),
-        compiler_params=pltpu.CompilerParams(vmem_limit_bytes=12 * MIB),
+        compiler_params=params(12),
     )(*parts, after)
 
 
@@ -268,9 +289,8 @@
     query_weight, key_weight, value_weight,
 ):
     smem = pl.BlockSpec(memory_space=pltpu.SMEM)
-    vmem = pl.BlockSpec(memory_space=pltpu.VMEM)
+    whole = lambda shape: pl.BlockSpec(shape, lambda step: (0,) * len(shape))
     hbm = pl.BlockSpec(memory_space=pl.ANY)
-    small, large = [pltpu.CompilerParams(vmem_limit_bytes=size * MIB) for size in (4, 24)]
     index = lax.axis_index("ctx").astype(jnp.int32)
     place = index.reshape(1)
     group = jnp.stack([lax.axis_index("grp").astype(jnp.int32), index % 2])
@@ -281,28 +301,29 @@
 
     own = pl.pallas_call(
         join_kernel,
-        in_specs=[vmem, vmem],
-        out_specs=vmem,
+        grid=(1,),
+        in_specs=[whole(key_rows.shape), whole(value_rows.shape)],
+        out_specs=whole(rows),
         out_shape=jax.ShapeDtypeStruct(rows, BF),
         cost_estimate=cost(0, 8 * BLOCK * HD),
-        compiler_params=small,
+        compiler_params=PARAMS,
     )(key_rows, value_rows)
     weights = (query_weight, key_weight, value_weight)
-    packed = [pack_weights(group, partner, *weights) for partner in range(1, PARTNERS + 1)]
+    *packed, pack_done = pack_weights(group, weights)
     direct = [over_x(part, index + 1) for index, part in enumerate(packed)]
     before = lax.ppermute(own, "ctx", [(i, (i + 1) % count) for i in range(count)])
     pieces = lax.all_to_all(own.reshape(BLOCKS, PIECE, 2 * HD), "ctx", 0, 0)
     picked = pl.pallas_call(
         pick_kernel,
-        in_specs=[smem, vmem] + [hbm] * PARTNERS,
-        out_specs=vmem,
+        grid=(1,),
+        in_specs=[smem, whole(pieces.shape), hbm],
+        out_specs=whole(pieces_shape),
         out_shape=jax.ShapeDtypeStruct(pieces_shape, BF),
         cost_estimate=cost(0, 12 * BLOCK * HD),
-        compiler_params=small,
-    )(selection, pieces, *packed)
+        compiler_params=params(8),
+    )(selection, pieces, pack_done)
     chosen = lax.all_to_all(picked, "ctx", 0, 0)
 
-    whole = lambda shape: pl.BlockSpec(shape, lambda step: (0,) * len(shape))
     near_in = (queries, output_grad, output_rows, norm, own, before)
     delta, query_near, own_grad, before_grad = pl.pallas_call(
         near_kernel,
@@ -316,56 +337,60 @@
             jax.ShapeDtypeStruct(rows, BF),
         ],
         scratch_shapes=tile_scratch(0),
-        cost_estimate=cost(6 * tile_flops, 1 << 22),
-        compiler_params=large,
+        cost_estimate=cost(600 * tile_flops, 1 << 22),
+        compiler_params=PARAMS,
     )(place, *near_in)
     before_sum = lax.ppermute(before_grad, "ctx", [(i, (i - 1) % count) for i in range(count)])
 
     far_in = (queries, output_grad, norm, delta, query_near, chosen)
-    query_grad, chosen_grad = pl.pallas_call(
+    query_grad, chosen_grad, far_done = pl.pallas_call(
         far_kernel,
         grid=(1,),
         in_specs=[smem, smem] + [whole(array.shape) for array in far_in],
-        out_specs=[whole((BLOCK, HEADS * HD)), whole(pieces_shape)],
+        out_specs=[whole((BLOCK, HEADS * HD)), whole(pieces_shape), whole(TOKEN)],
         out_shape=[
             jax.ShapeDtypeStruct((BLOCK, HEADS * HD), BF),
             jax.ShapeDtypeStruct(pieces_shape, BF),
+            jax.ShapeDtypeStruct(TOKEN, BF),
         ],
         scratch_shapes=tile_scratch(1),
         cost_estimate=cost(6 * tile_flops, 1 << 22),
-        compiler_params=large,
+        compiler_params=PARAMS,
     )(place, selection, *far_in)
 
     returned = lax.all_to_all(chosen_grad, "ctx", 0, 0)
-    *direct, query_grad = lax.optimization_barrier((*direct, query_grad))
+    *direct, far_done = lax.optimization_barrier((*direct, far_done))
     swapped = [lax.ppermute(part, "ctx", [(i, i ^ 1) for i in range(count)]) for part in direct]
-    query_all_weight, near_kept, near_sent, done = unpack_weights(group, weights, direct, swapped)
+    query_all_weight, near_kept, near_sent, done = unpack_weights(group, weights, direct, swapped, far_done)
     query_parts = gather_over_x(query_grad)
     collected = pl.pallas_call(
         collect_kernel,
-        in_specs=[smem, vmem, hbm],
-        out_specs=vmem,
+        grid=(1,),
+        in_specs=[smem, whole(pieces_shape), hbm],
+        out_specs=whole(pieces.shape),
         out_shape=jax.ShapeDtypeStruct((BLOCKS, PIECE, 2 * HD), BF),
         scratch_shapes=[pltpu.VMEM((BLOCKS, PIECE, 2 * HD), F32)],
         cost_estimate=cost(0, 12 * BLOCK * HD),
-        compiler_params=small,
+        compiler_params=params(8),
     )(selection, returned, done)
     part = product(join_queries(query_parts, collected), query_all_weight)
     kept_part, sent_part = part[:, :BLOCK], part[:, BLOCK:]
     chosen_sum = lax.all_to_all(collected, "ctx", 0, 0).reshape(rows)
+    chosen_sum, kept_part, sent_part = lax.optimization_barrier((chosen_sum, kept_part, sent_part))
     factor = jnp.where(lax.broadcasted_iota(jnp.int32, rows, 1) < HD, SCALE, 1.0)
     near_grad = ((own_grad + before_sum.astype(F32) + chosen_sum.astype(F32)) * factor).astype(BF)
     half = BLOCK // HALVES
     pairs = [(source, source ^ OTHER) for source in range(GROUPS)]
     near_parts = [gather_over_x(near_grad[i * half : (i + 1) * half]) for i in range(HALVES)]
-    outs = []
+    kept, got = [], []
     for i, near_all in enumerate(near_parts):
         some = slice(i * half, (i + 1) * half)
         near_all = jnp.concatenate(near_all, axis=1)
         sent = (sent_part[some] + product(near_all, near_sent)).astype(BF)
-        got = lax.ppermute(sent, "grp", pairs)
-        outs.append((kept_part[some] + product(near_all, near_kept) + got.astype(F32)).astype(BF))
-    return jnp.concatenate(outs, axis=0)
+        got.append(lax.ppermute(sent, "grp", pairs))
+        kept.append(kept_part[some] + product(near_all, near_kept))
+    kept = lax.optimization_barrier(kept)
+    return jnp.concatenate([(part + other.astype(F32)).astype(BF) for part, other in zip(kept, got)], axis=0)
 
 
 def solution(mesh):

time: 141 us -> 135 us (0.957)
  local copies, waits for them, and re-layouts: 22.2 us -> 3.94 us
  Pallas kernels: 23.4 us -> 31.4 us
  waiting for transfers between devices: 32.3 us -> 38.5 us
  starting transfers between devices: 54.3 us -> 52.3 us
  other arithmetic: 1.02 us -> 2.66 us
    unnamed x61 -> x29, local copies, waits for them, and re-layouts: 22.2 us -> 3.12 us
    all_to_all x1, waiting for transfers between devices: 3.15 us -> 8.98 us  [on_device(): chosen = lax.all_to_all(picked, 'ctx', 0, 0)]
    all_to_all x1, waiting for transfers between devices: 0.01 us -> 4.61 us  [on_device(): returned = lax.all_to_all(chosen_grad, 'ctx', 0, 0)]
    all_to_all x1, starting transfers between devices: 8.27 us -> 4.09 us  [on_device(): chosen_sum = lax.all_to_all(collected, 'ctx', 0, 0).reshape(rows)]
    pallas_call x1, Pallas kernels: 2.83 us -> 6.85 us  [unpack_weights(): pl.pallas_call(unpack_kernel, grid_spec=pltpu.PrefetchScalarGridSpec(num_...]
    all_to_all x1, waiting for transfers between devices: 3.57 us -> 1.13 us  [on_device(): pieces = lax.all_to_all(own.reshape(BLOCKS, PIECE, 2 * HD), 'ctx', 0, 0)]
    all_to_all x1, starting transfers between devices: 4.86 us -> 7.2 us  [on_device(): chosen = lax.all_to_all(picked, 'ctx', 0, 0)]
    pallas_call x1, Pallas kernels: 6.24 us -> 8.04 us  [on_device(): pl.pallas_call(near_kernel, grid=(1,), in_specs=[smem] + [whole(array.sha...]
  transfers between devices with their start and end apart: 23 -> 23, of which waited for: 11 -> 10; matrix products, arithmetic and copies ran while one was open for 4% -> 5% of each run, Pallas kernels for 16% -> 22%
where the time goes in v3:
time: 135 us
  starting transfers between devices  52.3 us (39%)
  waiting for transfers between devices  38.5 us (29%)
  Pallas kernels  31.4 us (23%)
  matrix products  5.48 us (4%)
  local copies, waits for them, and re-layouts  3.94 us (3%)
  other arithmetic  2.66 us (2%)
    ppermute x12, starting transfers between devices, over_x(): lax.ppermute(value, 'grp', [(source, source ^ partner) for source in rang...  18.9 us
    ppermute x12, waiting for transfers between devices, over_x(): lax.ppermute(value, 'grp', [(source, source ^ partner) for source in rang...  11.2 us
    all_to_all x1, starting transfers between devices, on_device(): pieces = lax.all_to_all(own.reshape(BLOCKS, PIECE, 2 * HD), 'ctx', 0, 0)  10.1 us
    all_to_all x1, waiting for transfers between devices, on_device(): chosen = lax.all_to_all(picked, 'ctx', 0, 0)  8.98 us
    pallas_call x1, Pallas kernels, on_device(): pl.pallas_call(near_kernel, grid=(1,), in_specs=[smem] + [whole(array.sha...  8.04 us
    all_to_all x1, starting transfers between devices, on_device(): returned = lax.all_to_all(chosen_grad, 'ctx', 0, 0)  7.48 us
    all_to_all x1, starting transfers between devices, on_device(): chosen = lax.all_to_all(picked, 'ctx', 0, 0)  7.2 us
    ppermute x2, waiting for transfers between devices, on_device(): got.append(lax.ppermute(sent, 'grp', pairs))  7.09 us
  transfers between devices with their start and end apart: 23, of which 10 were waited for; matrix products, arithmetic and copies ran while one was open for 5% of the time, Pallas kernels for 22%

profile of v3, /device:TPU:24, one launch (start us, length us, event | category | flops | bytes accessed | tf_op | source)
XLA Modules:
  0.0 134.6 jit_solution(6491625855451952278)
XLA Ops:
  1.7 10.1 %all-to-all-start = ((bf16[32,16,256]{2,1,0:T(8,128)(2,1)}), bf16[32,16,256]{2,1,0:T(8,128)(2,1)S(1)}, u32[]{:S(2)}, u32[]{:S(2)}) async-start(bf16[32,16,256]{2,1,0:T(8,128)(2,1)} %bitcast.12), calls=%async_computation | async-start | bytes 524288 | tf_op jit(solution)/shard_map/all_to_all | solution.py:315
  12.7 4.9 %shard_map.102 = (bf16[512,768]{1,0:T(8,128)(2,1)}, bf16[512,768]{1,0:T(8,128)(2,1)}, bf16[512,768]{1,0:T(8,128)(2,1)}, bf16[16,128]{1,0:T(8,128)(2,1)}) custom-call(s32[2]{0:T(128)} %pad_add_fusion.place, bf16[4096,512]{1,0:T(8,128)(2,1)} %refs_9_.1, bf16[4096,128]{1,0:T(8,128)(2,1)} %refs_10_.1, bf16[4096,128]{1,0:T(8,128)(2,1)} %refs_11_.1, ...), custom_call_target="tpu_custom_call" | custom-call | bytes 4718592 | tf_op jit(solution)/shard_map/pallas_call | solution.py:188
  19.1 2.7 %collective-permute-start.2 = (bf16[512,768]{1,0:T(8,128)(2,1)}, bf16[512,768]{1,0:T(8,128)(2,1)}, u32[]{:S(2)}, u32[]{:S(2)}) collective-permute-start(bf16[512,768]{1,0:T(8,128)(2,1)} %get-tuple-element.34), channel_id=1, source_target_pairs={{0,2},{1,3},{2,0},{3,1},{4,6},{5,7},{6,4},{7,5},{8,10},{9,11},{10,... | collective-permute-start | bytes 2359304 | tf_op jit(solution)/shard_map/ppermute | solution.py:276
  26.6 7.2 %all-to-all-start.1 = ((bf16[32,2,16,256]{3,2,1,0:T(8,128)(2,1)}), bf16[32,2,16,256]{3,2,1,0:T(8,128)(2,1)}, u32[]{:S(2)}, u32[]{:S(2)}) async-start(bf16[32,2,16,256]{3,2,1,0:T(8,128)(2,1)} %shard_map.103), calls=%async_computation.1 | async-start | bytes 1048576 | tf_op jit(solution)/shard_map/all_to_all | solution.py:325
  34.6 8.0 %shard_map.101 = (f32[4,1,512]{2,1,0:T(1,128)}, f32[4,128,512]{2,1,0:T(8,128)}, f32[512,256]{1,0:T(8,128)}, bf16[512,256]{1,0:T(8,128)(2,1)}) custom-call(s32[1]{0:T(128)} %bitcast.place, bf16[512,512]{1,0:T(8,128)(2,1)} %queries.3, bf16[512,512]{1,0:T(8,128)(2,1)} %output_grad.3, bf16[512,512]{1,0:T(8,128)(2,1)} %output_rows.1, f32[4,1,512]{2,1,0:T(1,128)} %reshape.13.norm, ...), custom_call_target="tpu_custom_call" | custom-call | flops 805306368000 | bytes 4194304 | tf_op jit(solution)/shard_map/pallas_call | solution.py:328
  42.6 9.0 %all-to-all-done.1.chosen = bf16[32,2,16,256]{3,2,1,0:T(8,128)(2,1)} async-done(((bf16[32,2,16,256]{3,2,1,0:T(8,128)(2,1)}), bf16[32,2,16,256]{3,2,1,0:T(8,128)(2,1)}, u32[]{:S(2)}, u32[]{:S(2)}) %all-to-all-start.1) | async-done | bytes 524320 | tf_op jit(solution)/shard_map/all_to_all | solution.py:325
  51.6 5.8 %shard_map.104 = (bf16[512,512]{1,0:T(8,128)(2,1)}, bf16[32,2,16,256]{3,2,1,0:T(8,128)(2,1)}, bf16[16,128]{1,0:T(8,128)(2,1)}) custom-call(s32[1]{0:T(128)} %bitcast.place, s32[32,3]{1,0:T(8,128)} %copy-done.1, bf16[512,512]{1,0:T(8,128)(2,1)} %queries.3, bf16[512,512]{1,0:T(8,128)(2,1)} %output_grad.3, f32[4,1,512]{2,1,0:T(1,128)} %reshape.13.norm, ...), custom_call_target="tpu_custom_call" | custom-call | flops 8053063680 | bytes 4194304 | tf_op jit(solution)/shard_map/pallas_call | solution.py:346
  57.4 3.2 %collective-permute-done.3.refs_2_ = bf16[512,768]{1,0:T(8,128)(2,1)} collective-permute-done((bf16[512,768]{1,0:T(8,128)(2,1)}, bf16[512,768]{1,0:T(8,128)(2,1)}, u32[]{:S(2)}, u32[]{:S(2)}) %collective-permute-start.3) | collective-permute-done | bytes 786464 | tf_op jit(solution)/shard_map/ppermute | solution.py:276
  60.6 7.5 %all-to-all-start.2 = ((bf16[32,2,16,256]{3,2,1,0:T(8,128)(2,1)}), bf16[32,2,16,256]{3,2,1,0:T(8,128)(2,1)S(1)}, u32[]{:S(2)}, u32[]{:S(2)}) async-start(bf16[32,2,16,256]{3,2,1,0:T(8,128)(2,1)} %get-tuple-element.32), calls=%async_computation.2 | async-start | bytes 1048576 | tf_op jit(solution)/shard_map/all_to_all | solution.py:361
  70.6 2.8 %collective-permute-start.9 = (bf16[512,512]{1,0:T(8,128)(2,1)}, bf16[512,512]{1,0:T(8,128)(2,1)S(1)}, u32[]{:S(2)}, u32[]{:S(2)}) collective-permute-start(bf16[512,512]{1,0:T(8,128)(2,1)} %get-tuple-element.42.refs_0_), channel_id=1, source_target_pairs={{0,3},{1,2},{2,1},{3,0},{4,7},{5,6},{6,5},{7,4},{8,11},{9,10},{10,... | collective-permute-start | bytes 1572872 | tf_op jit(solution)/shard_map/ppermute | solution.py:276
  74.3 6.9 %shard_map.105 = (bf16[1024,2048]{1,0:T(8,128)(2,1)}, bf16[512,1024]{1,0:T(8,128)(2,1)}, bf16[512,1024]{1,0:T(8,128)(2,1)}, bf16[16,128]{1,0:T(8,128)(2,1)}) custom-call(s32[2]{0:T(128)} %pad_add_fusion.place, bf16[512,768]{1,0:T(8,128)(2,1)} %collective-permute-done.1.refs_0_, bf16[512,768]{1,0:T(8,128)(2,1)} %collective-permute-done.2.refs_1_, ...), custom_call_target="tpu_custom_call" | custom-call | bytes 12591104 | tf_op jit(solution)/shard_map/pallas_call | solution.py:237
  81.2 4.6 %all-to-all-done.2.parts = bf16[32,2,16,256]{3,2,1,0:T(8,128)(2,1)S(1)} async-done(((bf16[32,2,16,256]{3,2,1,0:T(8,128)(2,1)}), bf16[32,2,16,256]{3,2,1,0:T(8,128)(2,1)S(1)}, u32[]{:S(2)}, u32[]{:S(2)}) %all-to-all-start.2) | async-done | bytes 524320 | tf_op jit(solution)/shard_map/all_to_all | solution.py:361
  86.5 2.2 %shard_map.106.refs_4_ = bf16[32,16,256]{2,1,0:T(8,128)(2,1)} custom-call(s32[32,3]{1,0:T(8,128)S(1)} %copy-done.2, bf16[32,2,16,256]{3,2,1,0:T(8,128)(2,1)S(1)} %all-to-all-done.2.parts, bf16[16,128]{1,0:T(8,128)(2,1)S(1)} %copy-done.4), custom_call_target="tpu_custom_call" | custom-call | bytes 786432 | tf_op jit(solution)/shard_map/pallas_call | solution.py:366
  88.7 4.1 %all-to-all-start.3 = ((bf16[32,16,256]{2,1,0:T(8,128)(2,1)}), bf16[32,16,256]{2,1,0:T(8,128)(2,1)S(1)}, u32[]{:S(2)}, u32[]{:S(2)}) async-start(bf16[32,16,256]{2,1,0:T(8,128)(2,1)} %shard_map.106.refs_4_), calls=%async_computation.3 | async-start | bytes 524288 | tf_op jit(solution)/shard_map/all_to_all | solution.py:378
  94.1 2.6 %collective-permute-done.9.refs_3_ = bf16[512,512]{1,0:T(8,128)(2,1)S(1)} collective-permute-done((bf16[512,512]{1,0:T(8,128)(2,1)}, bf16[512,512]{1,0:T(8,128)(2,1)S(1)}, u32[]{:S(2)}, u32[]{:S(2)}) %collective-permute-start.9) | collective-permute-done | bytes 524320 | tf_op jit(solution)/shard_map/ppermute | solution.py:276
  96.9 2.4 %fusion.8 = f32[512,1024]{1,0:T(8,128)S(1)} fusion(bf16[512,2048]{1,0:T(8,128)(2,1)S(1)} %shard_map.107, bf16[1024,2048]{1,0:T(8,128)(2,1)S(1)} %copy-done.10), kind=kOutput, calls=%fused_computation.20 | convolution fusion | flops 2147483648 | bytes 8388608 | tf_op jit(solution)/shard_map/dot_general | solution.py:284
  99.5 5.5 %all-to-all-done.3 = bf16[32,16,256]{2,1,0:T(8,128)(2,1)S(1)} async-done(((bf16[32,16,256]{2,1,0:T(8,128)(2,1)}), bf16[32,16,256]{2,1,0:T(8,128)(2,1)S(1)}, u32[]{:S(2)}, u32[]{:S(2)}) %all-to-all-start.3) | async-done | bytes 262176 | tf_op jit(solution)/shard_map/all_to_all | solution.py:378
  108.1 2.8 %collective-permute-start.13 = (bf16[256,256]{1,0:T(8,128)(2,1)S(1)}, bf16[256,256]{1,0:T(8,128)(2,1)S(1)}, u32[]{:S(2)}, u32[]{:S(2)}) collective-permute-start(bf16[256,256]{1,0:T(8,128)(2,1)S(1)} %get-tuple-element.56), channel_id=1, source_target_pairs={{0,3},{1,2},{2,1},{3,0},{4,7},{5,6},{6,5},{7,4},{8,11},{9,10},{10,... | collective-permute-start | bytes 393224 | tf_op jit(solution)/shard_map/ppermute | solution.py:276
  110.8 1.9 %collective-permute-start.15 = (bf16[256,256]{1,0:T(8,128)(2,1)S(1)}, bf16[256,256]{1,0:T(8,128)(2,1)S(1)}, u32[]{:S(2)}, u32[]{:S(2)}) collective-permute-start(bf16[256,256]{1,0:T(8,128)(2,1)S(1)} %get-tuple-element.55), channel_id=1, source_target_pairs={{0,2},{1,3},{2,0},{3,1},{4,6},{5,7},{6,4},{7,5},{8,10},{9,11},{10,... | collective-permute-start | bytes 393224 | tf_op jit(solution)/shard_map/ppermute | solution.py:276
  112.8 2.8 %collective-permute-start.16 = (bf16[256,256]{1,0:T(8,128)(2,1)S(1)}, bf16[256,256]{1,0:T(8,128)(2,1)S(1)}, u32[]{:S(2)}, u32[]{:S(2)}) collective-permute-start(bf16[256,256]{1,0:T(8,128)(2,1)S(1)} %get-tuple-element.55), channel_id=1, source_target_pairs={{0,3},{1,2},{2,1},{3,0},{4,7},{5,6},{6,5},{7,4},{8,11},{9,10},{10,... | collective-permute-start | bytes 393224 | tf_op jit(solution)/shard_map/ppermute | solution.py:276
  115.5 4.1 %collective-permute-done.13 = bf16[256,256]{1,0:T(8,128)(2,1)S(1)} collective-permute-done((bf16[256,256]{1,0:T(8,128)(2,1)S(1)}, bf16[256,256]{1,0:T(8,128)(2,1)S(1)}, u32[]{:S(2)}, u32[]{:S(2)}) %collective-permute-start.13) | collective-permute-done | bytes 131104 | tf_op jit(solution)/shard_map/ppermute | solution.py:276
  123.2 2.4 %collective-permute-start.18 = (bf16[256,512]{1,0:T(8,128)(2,1)S(1)}, bf16[256,512]{1,0:T(8,128)(2,1)S(1)}, u32[]{:S(2)}, u32[]{:S(2)}) collective-permute-start(bf16[256,512]{1,0:T(8,128)(2,1)S(1)} %fusion.1), channel_id=1, source_target_pairs={{0,4},{1,5},{2,6},{3,7},{4,0},{5,1},{6,2},{7,3},{8,12},{9,13},{10,... | collective-permute-start | bytes 786440 | tf_op jit(solution)/shard_map/ppermute | solution.py:390
  126.5 4.4 %collective-permute-done.17 = bf16[256,512]{1,0:T(8,128)(2,1)S(1)} collective-permute-done((bf16[256,512]{1,0:T(8,128)(2,1)S(1)}, bf16[256,512]{1,0:T(8,128)(2,1)S(1)}, u32[]{:S(2)}, u32[]{:S(2)}) %collective-permute-start.17) | collective-permute-done | bytes 262176 | tf_op jit(solution)/shard_map/ppermute | solution.py:390
  130.9 2.7 %collective-permute-done.18 = bf16[256,512]{1,0:T(8,128)(2,1)S(1)} collective-permute-done((bf16[256,512]{1,0:T(8,128)(2,1)S(1)}, bf16[256,512]{1,0:T(8,128)(2,1)S(1)}, u32[]{:S(2)}, u32[]{:S(2)}) %collective-permute-start.18) | collective-permute-done | bytes 262176 | tf_op jit(solution)/shard_map/ppermute | solution.py:390
  (73 shorter events, 24.0 us)
Async XLA Ops:
  1.7 22.4 %all-to-all-start = ((bf16[32,16,256]{2,1,0:T(8,128)(2,1)}), bf16[32,16,256]{2,1,0:T(8,128)(2,1)S(1)}, u32[]{:S(2)}, u32[]{:S(2)}) async-start(bf16[32,16,256]{2,1,0:T(8,128)(2,1)} %bitcast.12), calls=%async_computation | async-start | bytes 524288 | tf_op jit(solution)/shard_map/all_to_all | solution.py:315
  11.8 22.0 %collective-permute-start = (bf16[512,256]{1,0:T(8,128)(2,1)}, bf16[512,256]{1,0:T(8,128)(2,1)S(1)}, u32[]{:S(2)}, u32[]{:S(2)}) collective-permute-start(bf16[512,256]{1,0:T(8,128)(2,1)} %shard_map.100.own), channel_id=1, source_target_pairs={{0,8},{8,16},{16,24},{24,32},{32,40},{40,48},{48,56},{56,64},{64,7... | collective-permute-start | bytes 786440 | tf_op jit(solution)/shard_map/ppermute | solution.py:314
  17.6 39.8 %collective-permute-start.1 = (bf16[512,768]{1,0:T(8,128)(2,1)}, bf16[512,768]{1,0:T(8,128)(2,1)}, u32[]{:S(2)}, u32[]{:S(2)}) collective-permute-start(bf16[512,768]{1,0:T(8,128)(2,1)} %get-tuple-element.33), channel_id=1, source_target_pairs={{0,1},{1,0},{2,3},{3,2},{4,5},{5,4},{6,7},{7,6},{8,9},{9,8},{10,11... | collective-permute-start | bytes 2359304 | tf_op jit(solution)/shard_map/ppermute | solution.py:276
  19.1 38.2 %collective-permute-start.2 = (bf16[512,768]{1,0:T(8,128)(2,1)}, bf16[512,768]{1,0:T(8,128)(2,1)}, u32[]{:S(2)}, u32[]{:S(2)}) collective-permute-start(bf16[512,768]{1,0:T(8,128)(2,1)} %get-tuple-element.34), channel_id=1, source_target_pairs={{0,2},{1,3},{2,0},{3,1},{4,6},{5,7},{6,4},{7,5},{8,10},{9,11},{10,... | collective-permute-start | bytes 2359304 | tf_op jit(solution)/shard_map/ppermute | solution.py:276
  21.9 38.7 %collective-permute-start.3 = (bf16[512,768]{1,0:T(8,128)(2,1)}, bf16[512,768]{1,0:T(8,128)(2,1)}, u32[]{:S(2)}, u32[]{:S(2)}) collective-permute-start(bf16[512,768]{1,0:T(8,128)(2,1)} %get-tuple-element.35), channel_id=1, source_target_pairs={{0,3},{1,2},{2,1},{3,0},{4,7},{5,6},{6,5},{7,4},{8,11},{9,10},{10,... | collective-permute-start | bytes 2359304 | tf_op jit(solution)/shard_map/ppermute | solution.py:276
  26.6 25.0 %all-to-all-start.1 = ((bf16[32,2,16,256]{3,2,1,0:T(8,128)(2,1)}), bf16[32,2,16,256]{3,2,1,0:T(8,128)(2,1)}, u32[]{:S(2)}, u32[]{:S(2)}) async-start(bf16[32,2,16,256]{3,2,1,0:T(8,128)(2,1)} %shard_map.103), calls=%async_computation.1 | async-start | bytes 1048576 | tf_op jit(solution)/shard_map/all_to_all | solution.py:325
  60.6 10.0 %collective-permute-start.4 = (bf16[512,768]{1,0:T(8,128)(2,1)}, bf16[512,768]{1,0:T(8,128)(2,1)S(1)}, u32[]{:S(2)}, u32[]{:S(2)}) collective-permute-start(bf16[512,768]{1,0:T(8,128)(2,1)} %collective-permute-done.1.refs_0_), channel_id=1, source_target_pairs={{0,8},{8,0},{16,24},{24,16},{32,40},{40,32},{48,56},{56,48},{64,72... | collective-permute-start | bytes 2359304 | tf_op jit(solution)/shard_map/ppermute | solution.py:363
  60.6 25.2 %all-to-all-start.2 = ((bf16[32,2,16,256]{3,2,1,0:T(8,128)(2,1)}), bf16[32,2,16,256]{3,2,1,0:T(8,128)(2,1)S(1)}, u32[]{:S(2)}, u32[]{:S(2)}) async-start(bf16[32,2,16,256]{3,2,1,0:T(8,128)(2,1)} %get-tuple-element.32), calls=%async_computation.2 | async-start | bytes 1048576 | tf_op jit(solution)/shard_map/all_to_all | solution.py:361
  68.1 5.3 %collective-permute-start.5 = (bf16[512,768]{1,0:T(8,128)(2,1)}, bf16[512,768]{1,0:T(8,128)(2,1)S(1)}, u32[]{:S(2)}, u32[]{:S(2)}) collective-permute-start(bf16[512,768]{1,0:T(8,128)(2,1)} %collective-permute-done.2.refs_1_), channel_id=1, source_target_pairs={{0,8},{8,0},{16,24},{24,16},{32,40},{40,32},{48,56},{56,48},{64,72... | collective-permute-start | bytes 2359304 | tf_op jit(solution)/shard_map/ppermute | solution.py:363
  68.3 6.0 %collective-permute-start.6 = (bf16[512,768]{1,0:T(8,128)(2,1)}, bf16[512,768]{1,0:T(8,128)(2,1)}, u32[]{:S(2)}, u32[]{:S(2)}) collective-permute-start(bf16[512,768]{1,0:T(8,128)(2,1)} %collective-permute-done.3.refs_2_), channel_id=1, source_target_pairs={{0,8},{8,0},{16,24},{24,16},{32,40},{40,32},{48,56},{56,48},{64,72... | collective-permute-start | bytes 2359304 | tf_op jit(solution)/shard_map/ppermute | solution.py:363
  68.7 24.1 %collective-permute-start.7 = (bf16[512,512]{1,0:T(8,128)(2,1)}, bf16[512,512]{1,0:T(8,128)(2,1)S(1)}, u32[]{:S(2)}, u32[]{:S(2)}) collective-permute-start(bf16[512,512]{1,0:T(8,128)(2,1)} %get-tuple-element.42.refs_0_), channel_id=1, source_target_pairs={{0,1},{1,0},{2,3},{3,2},{4,5},{5,4},{6,7},{7,6},{8,9},{9,8},{10,11... | collective-permute-start | bytes 1572872 | tf_op jit(solution)/shard_map/ppermute | solution.py:276
  68.7 25.4 %collective-permute-start.8 = (bf16[512,512]{1,0:T(8,128)(2,1)}, bf16[512,512]{1,0:T(8,128)(2,1)S(1)}, u32[]{:S(2)}, u32[]{:S(2)}) collective-permute-start(bf16[512,512]{1,0:T(8,128)(2,1)} %get-tuple-element.42.refs_0_), channel_id=1, source_target_pairs={{0,2},{1,3},{2,0},{3,1},{4,6},{5,7},{6,4},{7,5},{8,10},{9,11},{10,... | collective-permute-start | bytes 1572872 | tf_op jit(solution)/shard_map/ppermute | solution.py:276
  70.6 26.1 %collective-permute-start.9 = (bf16[512,512]{1,0:T(8,128)(2,1)}, bf16[512,512]{1,0:T(8,128)(2,1)S(1)}, u32[]{:S(2)}, u32[]{:S(2)}) collective-permute-start(bf16[512,512]{1,0:T(8,128)(2,1)} %get-tuple-element.42.refs_0_), channel_id=1, source_target_pairs={{0,3},{1,2},{2,1},{3,0},{4,7},{5,6},{6,5},{7,4},{8,11},{9,10},{10,... | collective-permute-start | bytes 1572872 | tf_op jit(solution)/shard_map/ppermute | solution.py:276
  74.3 22.4 %copy-start = (bf16[512,512]{1,0:T(8,128)(2,1)S(1)}, bf16[512,512]{1,0:T(8,128)(2,1)}, u32[]{:S(2)}) copy-start(bf16[512,512]{1,0:T(8,128)(2,1)} %get-tuple-element.42.refs_0_) | copy-start | bytes 1572868
  74.3 30.7 %collective-permute-start.10 = (bf16[512,256]{1,0:T(8,128)(2,1)}, bf16[512,256]{1,0:T(8,128)(2,1)}, u32[]{:S(2)}, u32[]{:S(2)}) collective-permute-start(bf16[512,256]{1,0:T(8,128)(2,1)} %get-tuple-element.46), channel_id=1, source_target_pairs={{0,248},{8,0},{16,8},{24,16},{32,24},{40,32},{48,40},{56,48},{64,5... | collective-permute-start | bytes 786440 | tf_op jit(solution)/shard_map/ppermute | solution.py:343
  88.7 16.3 %all-to-all-start.3 = ((bf16[32,16,256]{2,1,0:T(8,128)(2,1)}), bf16[32,16,256]{2,1,0:T(8,128)(2,1)S(1)}, u32[]{:S(2)}, u32[]{:S(2)}) async-start(bf16[32,16,256]{2,1,0:T(8,128)(2,1)} %shard_map.106.refs_4_), calls=%async_computation.3 | async-start | bytes 524288 | tf_op jit(solution)/shard_map/all_to_all | solution.py:378
  106.1 6.7 %collective-permute-start.11 = (bf16[256,256]{1,0:T(8,128)(2,1)S(1)}, bf16[256,256]{1,0:T(8,128)(2,1)S(1)}, u32[]{:S(2)}, u32[]{:S(2)}) collective-permute-start(bf16[256,256]{1,0:T(8,128)(2,1)S(1)} %get-tuple-element.56), channel_id=1, source_target_pairs={{0,1},{1,0},{2,3},{3,2},{4,5},{5,4},{6,7},{7,6},{8,9},{9,8},{10,11... | collective-permute-start | bytes 393224 | tf_op jit(solution)/shard_map/ppermute | solution.py:276
  106.2 9.4 %collective-permute-start.12 = (bf16[256,256]{1,0:T(8,128)(2,1)S(1)}, bf16[256,256]{1,0:T(8,128)(2,1)S(1)}, u32[]{:S(2)}, u32[]{:S(2)}) collective-permute-start(bf16[256,256]{1,0:T(8,128)(2,1)S(1)} %get-tuple-element.56), channel_id=1, source_target_pairs={{0,2},{1,3},{2,0},{3,1},{4,6},{5,7},{6,4},{7,5},{8,10},{9,11},{10,... | collective-permute-start | bytes 393224 | tf_op jit(solution)/shard_map/ppermute | solution.py:276
  108.1 11.5 %collective-permute-start.13 = (bf16[256,256]{1,0:T(8,128)(2,1)S(1)}, bf16[256,256]{1,0:T(8,128)(2,1)S(1)}, u32[]{:S(2)}, u32[]{:S(2)}) collective-permute-start(bf16[256,256]{1,0:T(8,128)(2,1)S(1)} %get-tuple-element.56), channel_id=1, source_target_pairs={{0,3},{1,2},{2,1},{3,0},{4,7},{5,6},{6,5},{7,4},{8,11},{9,10},{10,... | collective-permute-start | bytes 393224 | tf_op jit(solution)/shard_map/ppermute | solution.py:276
  110.8 11.8 %collective-permute-start.14 = (bf16[256,256]{1,0:T(8,128)(2,1)S(1)}, bf16[256,256]{1,0:T(8,128)(2,1)S(1)}, u32[]{:S(2)}, u32[]{:S(2)}) collective-permute-start(bf16[256,256]{1,0:T(8,128)(2,1)S(1)} %get-tuple-element.55), channel_id=1, source_target_pairs={{0,1},{1,0},{2,3},{3,2},{4,5},{5,4},{6,7},{7,6},{8,9},{9,8},{10,11... | collective-permute-start | bytes 393224 | tf_op jit(solution)/shard_map/ppermute | solution.py:276
  110.8 11.8 %collective-permute-start.15 = (bf16[256,256]{1,0:T(8,128)(2,1)S(1)}, bf16[256,256]{1,0:T(8,128)(2,1)S(1)}, u32[]{:S(2)}, u32[]{:S(2)}) collective-permute-start(bf16[256,256]{1,0:T(8,128)(2,1)S(1)} %get-tuple-element.55), channel_id=1, source_target_pairs={{0,2},{1,3},{2,0},{3,1},{4,6},{5,7},{6,4},{7,5},{8,10},{9,11},{10,... | collective-permute-start | bytes 393224 | tf_op jit(solution)/shard_map/ppermute | solution.py:276
  112.8 9.9 %collective-permute-start.16 = (bf16[256,256]{1,0:T(8,128)(2,1)S(1)}, bf16[256,256]{1,0:T(8,128)(2,1)S(1)}, u32[]{:S(2)}, u32[]{:S(2)}) collective-permute-start(bf16[256,256]{1,0:T(8,128)(2,1)S(1)} %get-tuple-element.55), channel_id=1, source_target_pairs={{0,3},{1,2},{2,1},{3,0},{4,7},{5,6},{6,5},{7,4},{8,11},{9,10},{10,... | collective-permute-start | bytes 393224 | tf_op jit(solution)/shard_map/ppermute | solution.py:276
  121.3 9.5 %collective-permute-start.17 = (bf16[256,512]{1,0:T(8,128)(2,1)S(1)}, bf16[256,512]{1,0:T(8,128)(2,1)S(1)}, u32[]{:S(2)}, u32[]{:S(2)}) collective-permute-start(bf16[256,512]{1,0:T(8,128)(2,1)S(1)} %fusion), channel_id=1, source_target_pairs={{0,4},{1,5},{2,6},{3,7},{4,0},{5,1},{6,2},{7,3},{8,12},{9,13},{10,... | collective-permute-start | bytes 786440 | tf_op jit(solution)/shard_map/ppermute | solution.py:390
  123.2 10.5 %collective-permute-start.18 = (bf16[256,512]{1,0:T(8,128)(2,1)S(1)}, bf16[256,512]{1,0:T(8,128)(2,1)S(1)}, u32[]{:S(2)}, u32[]{:S(2)}) collective-permute-start(bf16[256,512]{1,0:T(8,128)(2,1)S(1)} %fusion.1), channel_id=1, source_target_pairs={{0,4},{1,5},{2,6},{3,7},{4,0},{5,1},{6,2},{7,3},{8,12},{9,13},{10,... | collective-permute-start | bytes 786440 | tf_op jit(solution)/shard_map/ppermute | solution.py:390
  (13 other events, 88.5 us)

commit v4 on v3

--- a/solution.py
+++ b/solution.py
@@ -316,12 +316,12 @@
     picked = pl.pallas_call(
         pick_kernel,
         grid=(1,),
-        in_specs=[smem, whole(pieces.shape), hbm],
+        in_specs=[smem, whole(pieces.shape)],
         out_specs=whole(pieces_shape),
         out_shape=jax.ShapeDtypeStruct(pieces_shape, BF),
         cost_estimate=cost(0, 12 * BLOCK * HD),
         compiler_params=params(8),
-    )(selection, pieces, pack_done)
+    )(selection, pieces)
     chosen = lax.all_to_all(picked, "ctx", 0, 0)
 
     near_in = (queries, output_grad, output_rows, norm, own, before)
@@ -366,13 +366,13 @@
     collected = pl.pallas_call(
         collect_kernel,
         grid=(1,),
-        in_specs=[smem, whole(pieces_shape), hbm],
+        in_specs=[smem, whole(pieces_shape)],
         out_specs=whole(pieces.shape),
         out_shape=jax.ShapeDtypeStruct((BLOCKS, PIECE, 2 * HD), BF),
         scratch_shapes=[pltpu.VMEM((BLOCKS, PIECE, 2 * HD), F32)],
         cost_estimate=cost(0, 12 * BLOCK * HD),
         compiler_params=params(8),
-    )(selection, returned, done)
+    )(selection, returned)
     part = product(join_queries(query_parts, collected), query_all_weight)
     kept_part, sent_part = part[:, :BLOCK], part[:, BLOCK:]
     chosen_sum = lax.all_to_all(collected, "ctx", 0, 0).reshape(rows)

time: 135 us -> 133 us (0.985)
  starting transfers between devices: 52.3 us -> 48.1 us
  waiting for transfers between devices: 38.5 us -> 42.2 us
  local copies, waits for them, and re-layouts: 3.94 us -> 2.56 us
    ppermute x12, waiting for transfers between devices: 11.2 us -> 15.1 us  [over_x(): lax.ppermute(value, 'grp', [(source, source ^ partner) for source in rang...]
    ppermute x12, starting transfers between devices: 18.9 us -> 15.7 us  [over_x(): lax.ppermute(value, 'grp', [(source, source ^ partner) for source in rang...]
    unnamed x29 -> x25, local copies, waits for them, and re-layouts: 3.12 us -> 1.74 us
  transfers between devices with their start and end apart: 23 -> 23, of which waited for: 10 -> 13; matrix products, arithmetic and copies ran while one was open for 5% -> 5% of each run, Pallas kernels for 22% -> 22%
where the time goes in v4:
time: 133 us
  starting transfers between devices  48.1 us (36%)
  waiting for transfers between devices  42.2 us (32%)
  Pallas kernels  31.4 us (24%)
  matrix products  5.48 us (4%)
  other arithmetic  2.67 us (2%)
  local copies, waits for them, and re-layouts  2.56 us (2%)
    ppermute x12, starting transfers between devices, over_x(): lax.ppermute(value, 'grp', [(source, source ^ partner) for source in rang...  15.7 us
    ppermute x12, waiting for transfers between devices, over_x(): lax.ppermute(value, 'grp', [(source, source ^ partner) for source in rang...  15.1 us
    all_to_all x1, starting transfers between devices, on_device(): pieces = lax.all_to_all(own.reshape(BLOCKS, PIECE, 2 * HD), 'ctx', 0, 0)  10.1 us
    all_to_all x1, waiting for transfers between devices, on_device(): chosen = lax.all_to_all(picked, 'ctx', 0, 0)  8.98 us
    pallas_call x1, Pallas kernels, on_device(): pl.pallas_call(near_kernel, grid=(1,), in_specs=[smem] + [whole(array.sha...  8.03 us
    ppermute x2, waiting for transfers between devices, on_device(): got.append(lax.ppermute(sent, 'grp', pairs))  7.55 us
    all_to_all x1, starting transfers between devices, on_device(): returned = lax.all_to_all(chosen_grad, 'ctx', 0, 0)  7.48 us
    all_to_all x1, starting transfers between devices, on_device(): chosen = lax.all_to_all(picked, 'ctx', 0, 0)  7.21 us
  transfers between devices with their start and end apart: 23, of which 13 were waited for; matrix products, arithmetic and copies ran while one was open for 5% of the time, Pallas kernels for 22%

profile of v4, /device:TPU:24, one launch (start us, length us, event | category | flops | bytes accessed | tf_op | source)
XLA Modules:
  0.0 132.6 jit_solution(10449569492287729276)
XLA Ops:
  1.7 10.1 %all-to-all-start = ((bf16[32,16,256]{2,1,0:T(8,128)(2,1)}), bf16[32,16,256]{2,1,0:T(8,128)(2,1)S(1)}, u32[]{:S(2)}, u32[]{:S(2)}) async-start(bf16[32,16,256]{2,1,0:T(8,128)(2,1)} %bitcast.12), calls=%async_computation | async-start | bytes 524288 | tf_op jit(solution)/shard_map/all_to_all | solution.py:315
  12.7 4.9 %shard_map.106 = (bf16[512,768]{1,0:T(8,128)(2,1)}, bf16[512,768]{1,0:T(8,128)(2,1)}, bf16[512,768]{1,0:T(8,128)(2,1)}, bf16[16,128]{1,0:T(8,128)(2,1)}) custom-call(s32[2]{0:T(128)} %pad_add_fusion.place, bf16[4096,512]{1,0:T(8,128)(2,1)} %refs_9_.1, bf16[4096,128]{1,0:T(8,128)(2,1)} %refs_10_.1, bf16[4096,128]{1,0:T(8,128)(2,1)} %refs_11_.1, ...), custom_call_target="tpu_custom_call" | custom-call | bytes 4718592 | tf_op jit(solution)/shard_map/pallas_call | solution.py:188
  19.1 2.7 %collective-permute-start.5 = (bf16[512,768]{1,0:T(8,128)(2,1)}, bf16[512,768]{1,0:T(8,128)(2,1)}, u32[]{:S(2)}, u32[]{:S(2)}) collective-permute-start(bf16[512,768]{1,0:T(8,128)(2,1)} %get-tuple-element.32), channel_id=1, source_target_pairs={{0,2},{1,3},{2,0},{3,1},{4,6},{5,7},{6,4},{7,5},{8,10},{9,11},{10,... | collective-permute-start | bytes 2359304 | tf_op jit(solution)/shard_map/ppermute | solution.py:276
  24.2 1.8 %shard_map.102 = bf16[32,2,16,256]{3,2,1,0:T(8,128)(2,1)} custom-call(s32[32,3]{1,0:T(8,128)S(1)} %copy.13.selection, bf16[32,16,256]{2,1,0:T(8,128)(2,1)S(1)} %all-to-all-done.pieces), custom_call_target="tpu_custom_call" | custom-call | bytes 786432 | tf_op jit(solution)/shard_map/pallas_call | solution.py:316
  25.9 7.2 %all-to-all-start.1 = ((bf16[32,2,16,256]{3,2,1,0:T(8,128)(2,1)}), bf16[32,2,16,256]{3,2,1,0:T(8,128)(2,1)}, u32[]{:S(2)}, u32[]{:S(2)}) async-start(bf16[32,2,16,256]{3,2,1,0:T(8,128)(2,1)} %shard_map.102), calls=%async_computation.1 | async-start | bytes 1048576 | tf_op jit(solution)/shard_map/all_to_all | solution.py:325
  33.9 8.0 %shard_map.101 = (f32[4,1,512]{2,1,0:T(1,128)}, f32[4,128,512]{2,1,0:T(8,128)}, f32[512,256]{1,0:T(8,128)}, bf16[512,256]{1,0:T(8,128)(2,1)}) custom-call(s32[1]{0:T(128)} %bitcast.place, bf16[512,512]{1,0:T(8,128)(2,1)} %queries.3, bf16[512,512]{1,0:T(8,128)(2,1)} %output_grad.3, bf16[512,512]{1,0:T(8,128)(2,1)} %output_rows.1, f32[4,1,512]{2,1,0:T(1,128)} %reshape.13.norm, ...), custom_call_target="tpu_custom_call" | custom-call | flops 805306368000 | bytes 4194304 | tf_op jit(solution)/shard_map/pallas_call | solution.py:328
  41.9 9.0 %all-to-all-done.1.chosen = bf16[32,2,16,256]{3,2,1,0:T(8,128)(2,1)} async-done(((bf16[32,2,16,256]{3,2,1,0:T(8,128)(2,1)}), bf16[32,2,16,256]{3,2,1,0:T(8,128)(2,1)}, u32[]{:S(2)}, u32[]{:S(2)}) %all-to-all-start.1) | async-done | bytes 524320 | tf_op jit(solution)/shard_map/all_to_all | solution.py:325
  50.9 5.8 %shard_map.103 = (bf16[512,512]{1,0:T(8,128)(2,1)}, bf16[32,2,16,256]{3,2,1,0:T(8,128)(2,1)}, bf16[16,128]{1,0:T(8,128)(2,1)}) custom-call(s32[1]{0:T(128)} %bitcast.place, s32[32,3]{1,0:T(8,128)} %copy-done.1, bf16[512,512]{1,0:T(8,128)(2,1)} %queries.3, bf16[512,512]{1,0:T(8,128)(2,1)} %output_grad.3, f32[4,1,512]{2,1,0:T(1,128)} %reshape.13.norm, ...), custom_call_target="tpu_custom_call" | custom-call | flops 8053063680 | bytes 4194304 | tf_op jit(solution)/shard_map/pallas_call | solution.py:346
  57.2 3.4 %collective-permute-done.6.refs_2_ = bf16[512,768]{1,0:T(8,128)(2,1)} collective-permute-done((bf16[512,768]{1,0:T(8,128)(2,1)}, bf16[512,768]{1,0:T(8,128)(2,1)}, u32[]{:S(2)}, u32[]{:S(2)}) %collective-permute-start.6) | collective-permute-done | bytes 786464 | tf_op jit(solution)/shard_map/ppermute | solution.py:276
  60.6 7.5 %all-to-all-start.2 = ((bf16[32,2,16,256]{3,2,1,0:T(8,128)(2,1)}), bf16[32,2,16,256]{3,2,1,0:T(8,128)(2,1)S(1)}, u32[]{:S(2)}, u32[]{:S(2)}) async-start(bf16[32,2,16,256]{3,2,1,0:T(8,128)(2,1)} %get-tuple-element.29), calls=%async_computation.2 | async-start | bytes 1048576 | tf_op jit(solution)/shard_map/all_to_all | solution.py:361
  68.7 1.9 %collective-permute-start.2 = (bf16[512,512]{1,0:T(8,128)(2,1)}, bf16[512,512]{1,0:T(8,128)(2,1)S(1)}, u32[]{:S(2)}, u32[]{:S(2)}) collective-permute-start(bf16[512,512]{1,0:T(8,128)(2,1)} %get-tuple-element.30.refs_0_), channel_id=1, source_target_pairs={{0,2},{1,3},{2,0},{3,1},{4,6},{5,7},{6,4},{7,5},{8,10},{9,11},{10,... | collective-permute-start | bytes 1572872 | tf_op jit(solution)/shard_map/ppermute | solution.py:276
  70.6 2.8 %collective-permute-start.3 = (bf16[512,512]{1,0:T(8,128)(2,1)}, bf16[512,512]{1,0:T(8,128)(2,1)S(1)}, u32[]{:S(2)}, u32[]{:S(2)}) collective-permute-start(bf16[512,512]{1,0:T(8,128)(2,1)} %get-tuple-element.30.refs_0_), channel_id=1, source_target_pairs={{0,3},{1,2},{2,1},{3,0},{4,7},{5,6},{6,5},{7,4},{8,11},{9,10},{10,... | collective-permute-start | bytes 1572872 | tf_op jit(solution)/shard_map/ppermute | solution.py:276
  74.3 6.9 %shard_map.107 = (bf16[1024,2048]{1,0:T(8,128)(2,1)}, bf16[512,1024]{1,0:T(8,128)(2,1)}, bf16[512,1024]{1,0:T(8,128)(2,1)}, bf16[16,128]{1,0:T(8,128)(2,1)}) custom-call(s32[2]{0:T(128)} %pad_add_fusion.place, bf16[512,768]{1,0:T(8,128)(2,1)} %collective-permute-done.4.refs_0_, bf16[512,768]{1,0:T(8,128)(2,1)} %collective-permute-done.5.refs_1_, ...), custom_call_target="tpu_custom_call" | custom-call | bytes 12591104 | tf_op jit(solution)/shard_map/pallas_call | solution.py:237
  81.2 4.6 %all-to-all-done.2.parts = bf16[32,2,16,256]{3,2,1,0:T(8,128)(2,1)S(1)} async-done(((bf16[32,2,16,256]{3,2,1,0:T(8,128)(2,1)}), bf16[32,2,16,256]{3,2,1,0:T(8,128)(2,1)S(1)}, u32[]{:S(2)}, u32[]{:S(2)}) %all-to-all-start.2) | async-done | bytes 524320 | tf_op jit(solution)/shard_map/all_to_all | solution.py:361
  85.8 2.2 %shard_map.104.refs_4_ = bf16[32,16,256]{2,1,0:T(8,128)(2,1)} custom-call(s32[32,3]{1,0:T(8,128)S(1)} %copy-done.2, bf16[32,2,16,256]{3,2,1,0:T(8,128)(2,1)S(1)} %all-to-all-done.2.parts), custom_call_target="tpu_custom_call" | custom-call | bytes 786432 | tf_op jit(solution)/shard_map/pallas_call | solution.py:366
  88.0 4.1 %all-to-all-start.3 = ((bf16[32,16,256]{2,1,0:T(8,128)(2,1)}), bf16[32,16,256]{2,1,0:T(8,128)(2,1)S(1)}, u32[]{:S(2)}, u32[]{:S(2)}) async-start(bf16[32,16,256]{2,1,0:T(8,128)(2,1)} %shard_map.104.refs_4_), calls=%async_computation.3 | async-start | bytes 524288 | tf_op jit(solution)/shard_map/all_to_all | solution.py:378
  92.1 2.0 %collective-permute-done.2.refs_2_ = bf16[512,512]{1,0:T(8,128)(2,1)S(1)} collective-permute-done((bf16[512,512]{1,0:T(8,128)(2,1)}, bf16[512,512]{1,0:T(8,128)(2,1)S(1)}, u32[]{:S(2)}, u32[]{:S(2)}) %collective-permute-start.2) | collective-permute-done | bytes 524320 | tf_op jit(solution)/shard_map/ppermute | solution.py:276
  94.1 2.6 %collective-permute-done.3.refs_3_ = bf16[512,512]{1,0:T(8,128)(2,1)S(1)} collective-permute-done((bf16[512,512]{1,0:T(8,128)(2,1)}, bf16[512,512]{1,0:T(8,128)(2,1)S(1)}, u32[]{:S(2)}, u32[]{:S(2)}) %collective-permute-start.3) | collective-permute-done | bytes 524320 | tf_op jit(solution)/shard_map/ppermute | solution.py:276
  96.9 2.4 %fusion.8 = f32[512,1024]{1,0:T(8,128)S(1)} fusion(bf16[512,2048]{1,0:T(8,128)(2,1)S(1)} %shard_map.105, bf16[1024,2048]{1,0:T(8,128)(2,1)S(1)} %copy-done.8), kind=kOutput, calls=%fused_computation.20 | convolution fusion | flops 2147483648 | bytes 8388608 | tf_op jit(solution)/shard_map/dot_general | solution.py:284
  99.5 4.8 %all-to-all-done.3 = bf16[32,16,256]{2,1,0:T(8,128)(2,1)S(1)} async-done(((bf16[32,16,256]{2,1,0:T(8,128)(2,1)}), bf16[32,16,256]{2,1,0:T(8,128)(2,1)S(1)}, u32[]{:S(2)}, u32[]{:S(2)}) %all-to-all-start.3) | async-done | bytes 262176 | tf_op jit(solution)/shard_map/all_to_all | solution.py:378
  106.5 3.0 %collective-permute-start.14 = (bf16[256,256]{1,0:T(8,128)(2,1)S(1)}, bf16[256,256]{1,0:T(8,128)(2,1)S(1)}, u32[]{:S(2)}, u32[]{:S(2)}) collective-permute-start(bf16[256,256]{1,0:T(8,128)(2,1)S(1)} %get-tuple-element.51), channel_id=1, source_target_pairs={{0,1},{1,0},{2,3},{3,2},{4,5},{5,4},{6,7},{7,6},{8,9},{9,8},{10,11... | collective-permute-start | bytes 393224 | tf_op jit(solution)/shard_map/ppermute | solution.py:276
  111.6 4.7 %collective-permute-done.16 = bf16[256,256]{1,0:T(8,128)(2,1)S(1)} collective-permute-done((bf16[256,256]{1,0:T(8,128)(2,1)S(1)}, bf16[256,256]{1,0:T(8,128)(2,1)S(1)}, u32[]{:S(2)}, u32[]{:S(2)}) %collective-permute-start.16) | collective-permute-done | bytes 131104 | tf_op jit(solution)/shard_map/ppermute | solution.py:276
  124.1 4.8 %collective-permute-done.18 = bf16[256,512]{1,0:T(8,128)(2,1)S(1)} collective-permute-done((bf16[256,512]{1,0:T(8,128)(2,1)S(1)}, bf16[256,512]{1,0:T(8,128)(2,1)S(1)}, u32[]{:S(2)}, u32[]{:S(2)}) %collective-permute-start.18) | collective-permute-done | bytes 262176 | tf_op jit(solution)/shard_map/ppermute | solution.py:390
  129.0 2.7 %collective-permute-done.17 = bf16[256,512]{1,0:T(8,128)(2,1)S(1)} collective-permute-done((bf16[256,512]{1,0:T(8,128)(2,1)S(1)}, bf16[256,512]{1,0:T(8,128)(2,1)S(1)}, u32[]{:S(2)}, u32[]{:S(2)}) %collective-permute-start.17) | collective-permute-done | bytes 262176 | tf_op jit(solution)/shard_map/ppermute | solution.py:390
  (69 shorter events, 22.5 us)
Async XLA Ops:
  1.7 22.4 %all-to-all-start = ((bf16[32,16,256]{2,1,0:T(8,128)(2,1)}), bf16[32,16,256]{2,1,0:T(8,128)(2,1)S(1)}, u32[]{:S(2)}, u32[]{:S(2)}) async-start(bf16[32,16,256]{2,1,0:T(8,128)(2,1)} %bitcast.12), calls=%async_computation | async-start | bytes 524288 | tf_op jit(solution)/shard_map/all_to_all | solution.py:315
  11.8 21.3 %collective-permute-start = (bf16[512,256]{1,0:T(8,128)(2,1)}, bf16[512,256]{1,0:T(8,128)(2,1)S(1)}, u32[]{:S(2)}, u32[]{:S(2)}) collective-permute-start(bf16[512,256]{1,0:T(8,128)(2,1)} %shard_map.100.own), channel_id=1, source_target_pairs={{0,8},{8,16},{16,24},{24,32},{32,40},{40,48},{48,56},{56,64},{64,7... | collective-permute-start | bytes 786440 | tf_op jit(solution)/shard_map/ppermute | solution.py:314
  17.6 39.1 %collective-permute-start.4 = (bf16[512,768]{1,0:T(8,128)(2,1)}, bf16[512,768]{1,0:T(8,128)(2,1)}, u32[]{:S(2)}, u32[]{:S(2)}) collective-permute-start(bf16[512,768]{1,0:T(8,128)(2,1)} %get-tuple-element.31), channel_id=1, source_target_pairs={{0,1},{1,0},{2,3},{3,2},{4,5},{5,4},{6,7},{7,6},{8,9},{9,8},{10,11... | collective-permute-start | bytes 2359304 | tf_op jit(solution)/shard_map/ppermute | solution.py:276
  19.1 38.0 %collective-permute-start.5 = (bf16[512,768]{1,0:T(8,128)(2,1)}, bf16[512,768]{1,0:T(8,128)(2,1)}, u32[]{:S(2)}, u32[]{:S(2)}) collective-permute-start(bf16[512,768]{1,0:T(8,128)(2,1)} %get-tuple-element.32), channel_id=1, source_target_pairs={{0,2},{1,3},{2,0},{3,1},{4,6},{5,7},{6,4},{7,5},{8,10},{9,11},{10,... | collective-permute-start | bytes 2359304 | tf_op jit(solution)/shard_map/ppermute | solution.py:276
  21.9 38.7 %collective-permute-start.6 = (bf16[512,768]{1,0:T(8,128)(2,1)}, bf16[512,768]{1,0:T(8,128)(2,1)}, u32[]{:S(2)}, u32[]{:S(2)}) collective-permute-start(bf16[512,768]{1,0:T(8,128)(2,1)} %get-tuple-element.33), channel_id=1, source_target_pairs={{0,3},{1,2},{2,1},{3,0},{4,7},{5,6},{6,5},{7,4},{8,11},{9,10},{10,... | collective-permute-start | bytes 2359304 | tf_op jit(solution)/shard_map/ppermute | solution.py:276
  25.9 25.0 %all-to-all-start.1 = ((bf16[32,2,16,256]{3,2,1,0:T(8,128)(2,1)}), bf16[32,2,16,256]{3,2,1,0:T(8,128)(2,1)}, u32[]{:S(2)}, u32[]{:S(2)}) async-start(bf16[32,2,16,256]{3,2,1,0:T(8,128)(2,1)} %shard_map.102), calls=%async_computation.1 | async-start | bytes 1048576 | tf_op jit(solution)/shard_map/all_to_all | solution.py:325
  60.6 10.0 %collective-permute-start.7 = (bf16[512,768]{1,0:T(8,128)(2,1)}, bf16[512,768]{1,0:T(8,128)(2,1)S(1)}, u32[]{:S(2)}, u32[]{:S(2)}) collective-permute-start(bf16[512,768]{1,0:T(8,128)(2,1)} %collective-permute-done.4.refs_0_), channel_id=1, source_target_pairs={{0,8},{8,0},{16,24},{24,16},{32,40},{40,32},{48,56},{56,48},{64,72... | collective-permute-start | bytes 2359304 | tf_op jit(solution)/shard_map/ppermute | solution.py:363
  60.6 25.2 %all-to-all-start.2 = ((bf16[32,2,16,256]{3,2,1,0:T(8,128)(2,1)}), bf16[32,2,16,256]{3,2,1,0:T(8,128)(2,1)S(1)}, u32[]{:S(2)}, u32[]{:S(2)}) async-start(bf16[32,2,16,256]{3,2,1,0:T(8,128)(2,1)} %get-tuple-element.29), calls=%async_computation.2 | async-start | bytes 1048576 | tf_op jit(solution)/shard_map/all_to_all | solution.py:361
  68.1 5.3 %collective-permute-start.8 = (bf16[512,768]{1,0:T(8,128)(2,1)}, bf16[512,768]{1,0:T(8,128)(2,1)S(1)}, u32[]{:S(2)}, u32[]{:S(2)}) collective-permute-start(bf16[512,768]{1,0:T(8,128)(2,1)} %collective-permute-done.5.refs_1_), channel_id=1, source_target_pairs={{0,8},{8,0},{16,24},{24,16},{32,40},{40,32},{48,56},{56,48},{64,72... | collective-permute-start | bytes 2359304 | tf_op jit(solution)/shard_map/ppermute | solution.py:363
  68.3 6.0 %collective-permute-start.9 = (bf16[512,768]{1,0:T(8,128)(2,1)}, bf16[512,768]{1,0:T(8,128)(2,1)}, u32[]{:S(2)}, u32[]{:S(2)}) collective-permute-start(bf16[512,768]{1,0:T(8,128)(2,1)} %collective-permute-done.6.refs_2_), channel_id=1, source_target_pairs={{0,8},{8,0},{16,24},{24,16},{32,40},{40,32},{48,56},{56,48},{64,72... | collective-permute-start | bytes 2359304 | tf_op jit(solution)/shard_map/ppermute | solution.py:363
  68.7 23.4 %collective-permute-start.1 = (bf16[512,512]{1,0:T(8,128)(2,1)}, bf16[512,512]{1,0:T(8,128)(2,1)S(1)}, u32[]{:S(2)}, u32[]{:S(2)}) collective-permute-start(bf16[512,512]{1,0:T(8,128)(2,1)} %get-tuple-element.30.refs_0_), channel_id=1, source_target_pairs={{0,1},{1,0},{2,3},{3,2},{4,5},{5,4},{6,7},{7,6},{8,9},{9,8},{10,11... | collective-permute-start | bytes 1572872 | tf_op jit(solution)/shard_map/ppermute | solution.py:276
  68.7 25.4 %collective-permute-start.2 = (bf16[512,512]{1,0:T(8,128)(2,1)}, bf16[512,512]{1,0:T(8,128)(2,1)S(1)}, u32[]{:S(2)}, u32[]{:S(2)}) collective-permute-start(bf16[512,512]{1,0:T(8,128)(2,1)} %get-tuple-element.30.refs_0_), channel_id=1, source_target_pairs={{0,2},{1,3},{2,0},{3,1},{4,6},{5,7},{6,4},{7,5},{8,10},{9,11},{10,... | collective-permute-start | bytes 1572872 | tf_op jit(solution)/shard_map/ppermute | solution.py:276
  70.6 26.1 %collective-permute-start.3 = (bf16[512,512]{1,0:T(8,128)(2,1)}, bf16[512,512]{1,0:T(8,128)(2,1)S(1)}, u32[]{:S(2)}, u32[]{:S(2)}) collective-permute-start(bf16[512,512]{1,0:T(8,128)(2,1)} %get-tuple-element.30.refs_0_), channel_id=1, source_target_pairs={{0,3},{1,2},{2,1},{3,0},{4,7},{5,6},{6,5},{7,4},{8,11},{9,10},{10,... | collective-permute-start | bytes 1572872 | tf_op jit(solution)/shard_map/ppermute | solution.py:276
  74.3 22.4 %copy-start = (bf16[512,512]{1,0:T(8,128)(2,1)S(1)}, bf16[512,512]{1,0:T(8,128)(2,1)}, u32[]{:S(2)}) copy-start(bf16[512,512]{1,0:T(8,128)(2,1)} %get-tuple-element.30.refs_0_) | copy-start | bytes 1572868
  74.3 30.0 %collective-permute-start.10 = (bf16[512,256]{1,0:T(8,128)(2,1)}, bf16[512,256]{1,0:T(8,128)(2,1)}, u32[]{:S(2)}, u32[]{:S(2)}) collective-permute-start(bf16[512,256]{1,0:T(8,128)(2,1)} %get-tuple-element.42), channel_id=1, source_target_pairs={{0,248},{8,0},{16,8},{24,16},{32,24},{40,32},{48,40},{56,48},{64,5... | collective-permute-start | bytes 786440 | tf_op jit(solution)/shard_map/ppermute | solution.py:343
  88.0 16.3 %all-to-all-start.3 = ((bf16[32,16,256]{2,1,0:T(8,128)(2,1)}), bf16[32,16,256]{2,1,0:T(8,128)(2,1)S(1)}, u32[]{:S(2)}, u32[]{:S(2)}) async-start(bf16[32,16,256]{2,1,0:T(8,128)(2,1)} %shard_map.104.refs_4_), calls=%async_computation.3 | async-start | bytes 524288 | tf_op jit(solution)/shard_map/all_to_all | solution.py:378
  105.4 11.0 %collective-permute-start.16 = (bf16[256,256]{1,0:T(8,128)(2,1)S(1)}, bf16[256,256]{1,0:T(8,128)(2,1)S(1)}, u32[]{:S(2)}, u32[]{:S(2)}) collective-permute-start(bf16[256,256]{1,0:T(8,128)(2,1)S(1)} %get-tuple-element.51), channel_id=1, source_target_pairs={{0,3},{1,2},{2,1},{3,0},{4,7},{5,6},{6,5},{7,4},{8,11},{9,10},{10,... | collective-permute-start | bytes 393224 | tf_op jit(solution)/shard_map/ppermute | solution.py:276
  105.9 10.4 %collective-permute-start.15 = (bf16[256,256]{1,0:T(8,128)(2,1)S(1)}, bf16[256,256]{1,0:T(8,128)(2,1)S(1)}, u32[]{:S(2)}, u32[]{:S(2)}) collective-permute-start(bf16[256,256]{1,0:T(8,128)(2,1)S(1)} %get-tuple-element.51), channel_id=1, source_target_pairs={{0,2},{1,3},{2,0},{3,1},{4,6},{5,7},{6,4},{7,5},{8,10},{9,11},{10,... | collective-permute-start | bytes 393224 | tf_op jit(solution)/shard_map/ppermute | solution.py:276
  106.5 10.2 %collective-permute-start.14 = (bf16[256,256]{1,0:T(8,128)(2,1)S(1)}, bf16[256,256]{1,0:T(8,128)(2,1)S(1)}, u32[]{:S(2)}, u32[]{:S(2)}) collective-permute-start(bf16[256,256]{1,0:T(8,128)(2,1)S(1)} %get-tuple-element.51), channel_id=1, source_target_pairs={{0,1},{1,0},{2,3},{3,2},{4,5},{5,4},{6,7},{7,6},{8,9},{9,8},{10,11... | collective-permute-start | bytes 393224 | tf_op jit(solution)/shard_map/ppermute | solution.py:276
  109.5 10.3 %collective-permute-start.13 = (bf16[256,256]{1,0:T(8,128)(2,1)S(1)}, bf16[256,256]{1,0:T(8,128)(2,1)S(1)}, u32[]{:S(2)}, u32[]{:S(2)}) collective-permute-start(bf16[256,256]{1,0:T(8,128)(2,1)S(1)} %get-tuple-element.52), channel_id=1, source_target_pairs={{0,3},{1,2},{2,1},{3,0},{4,7},{5,6},{6,5},{7,4},{8,11},{9,10},{10,... | collective-permute-start | bytes 393224 | tf_op jit(solution)/shard_map/ppermute | solution.py:276
  110.0 9.8 %collective-permute-start.12 = (bf16[256,256]{1,0:T(8,128)(2,1)S(1)}, bf16[256,256]{1,0:T(8,128)(2,1)S(1)}, u32[]{:S(2)}, u32[]{:S(2)}) collective-permute-start(bf16[256,256]{1,0:T(8,128)(2,1)S(1)} %get-tuple-element.52), channel_id=1, source_target_pairs={{0,2},{1,3},{2,0},{3,1},{4,6},{5,7},{6,4},{7,5},{8,10},{9,11},{10,... | collective-permute-start | bytes 393224 | tf_op jit(solution)/shard_map/ppermute | solution.py:276
  116.3 5.0 %collective-permute-start.11 = (bf16[256,256]{1,0:T(8,128)(2,1)S(1)}, bf16[256,256]{1,0:T(8,128)(2,1)S(1)}, u32[]{:S(2)}, u32[]{:S(2)}) collective-permute-start(bf16[256,256]{1,0:T(8,128)(2,1)S(1)} %get-tuple-element.52), channel_id=1, source_target_pairs={{0,1},{1,0},{2,3},{3,2},{4,5},{5,4},{6,7},{7,6},{8,9},{9,8},{10,11... | collective-permute-start | bytes 393224 | tf_op jit(solution)/shard_map/ppermute | solution.py:276
  118.5 10.4 %collective-permute-start.18 = (bf16[256,512]{1,0:T(8,128)(2,1)S(1)}, bf16[256,512]{1,0:T(8,128)(2,1)S(1)}, u32[]{:S(2)}, u32[]{:S(2)}) collective-permute-start(bf16[256,512]{1,0:T(8,128)(2,1)S(1)} %fusion.1), channel_id=1, source_target_pairs={{0,4},{1,5},{2,6},{3,7},{4,0},{5,1},{6,2},{7,3},{8,12},{9,13},{10,... | collective-permute-start | bytes 786440 | tf_op jit(solution)/shard_map/ppermute | solution.py:390
  121.8 9.9 %collective-permute-start.17 = (bf16[256,512]{1,0:T(8,128)(2,1)S(1)}, bf16[256,512]{1,0:T(8,128)(2,1)S(1)}, u32[]{:S(2)}, u32[]{:S(2)}) collective-permute-start(bf16[256,512]{1,0:T(8,128)(2,1)S(1)} %fusion), channel_id=1, source_target_pairs={{0,4},{1,5},{2,6},{3,7},{4,0},{5,1},{6,2},{7,3},{8,12},{9,13},{10,... | collective-permute-start | bytes 786440 | tf_op jit(solution)/shard_map/ppermute | solution.py:390
  (11 other events, 86.1 us)

commit v5 on v4

--- a/solution.py
+++ b/solution.py
@@ -46,7 +46,7 @@
             out[block, slot] = pieces[chosen]
         return carry
 
-    lax.fori_loop(0, BLOCKS, step, 0, unroll=4)
+    lax.fori_loop(0, BLOCKS, step, 0, unroll=True)
 
 
 def collect_kernel(selection, parts, *refs):
@@ -55,14 +55,11 @@
 
     def step(block, carry):
         for slot, chosen in enumerate(others(selection, block)):
-
-            @pl.when(chosen < block)
-            def _():
-                total[chosen] += parts[block, slot].astype(F32)
+            total[chosen] += jnp.where(chosen < block, parts[block, slot].astype(F32), 0.0)
 
         return carry
 
-    lax.fori_loop(0, BLOCKS, step, 0, unroll=4)
+    lax.fori_loop(0, BLOCKS, step, 0, unroll=8)
     out[...] = total[...].astype(BF)
 
 
@@ -178,7 +175,7 @@
 
 
 def pack_weights(place, weights):
-    steps = 4
+    steps = 2
     rows, width = BLOCK // steps, (HEADS + 2) * HD
 
     def index(partner):

time: 133 us -> 132 us (level)
  Pallas kernels: 31.4 us -> 29.8 us
  transfers between devices with their start and end apart: 23 -> 23, of which waited for: 13 -> 13; matrix products, arithmetic and copies ran while one was open for 5% -> 5% of each run, Pallas kernels for 22% -> 21%
where the time goes in v5:
time: 132 us; the launch traced here: 131 us
  starting transfers between devices  46.8 us (35%)
  waiting for transfers between devices  43.5 us (33%)
  Pallas kernels  29.8 us (23%)
  matrix products  5.47 us (4%)
  other arithmetic  2.67 us (2%)
  local copies, waits for them, and re-layouts  2.56 us (2%)
    ppermute x12, starting transfers between devices, over_x(): lax.ppermute(value, 'grp', [(source, source ^ partner) for source in rang...  15.7 us
    ppermute x12, waiting for transfers between devices, over_x(): lax.ppermute(value, 'grp', [(source, source ^ partner) for source in rang...  15.5 us
    all_to_all x1, starting transfers between devices, on_device(): pieces = lax.all_to_all(own.reshape(BLOCKS, PIECE, 2 * HD), 'ctx', 0, 0)  10.1 us
    all_to_all x1, waiting for transfers between devices, on_device(): chosen = lax.all_to_all(picked, 'ctx', 0, 0)  8.98 us
    pallas_call x1, Pallas kernels, on_device(): pl.pallas_call(near_kernel, grid=(1,), in_specs=[smem] + [whole(array.sha...  8.03 us
    ppermute x2, waiting for transfers between devices, on_device(): got.append(lax.ppermute(sent, 'grp', pairs))  7.56 us
    all_to_all x1, starting transfers between devices, on_device(): returned = lax.all_to_all(chosen_grad, 'ctx', 0, 0)  7.48 us
    pallas_call x1, Pallas kernels, unpack_weights(): pl.pallas_call(unpack_kernel, grid_spec=pltpu.PrefetchScalarGridSpec(num_...  6.86 us
  transfers between devices with their start and end apart: 23, of which 13 were waited for; matrix products, arithmetic and copies ran while one was open for 5% of the time, Pallas kernels for 21%

profile of v5, /device:TPU:24, one launch (start us, length us, event | category | flops | bytes accessed | tf_op | source)
XLA Modules:
  0.0 131.0 jit_solution(15353583849840145330)
XLA Ops:
  1.7 10.1 %all-to-all-start = ((bf16[32,16,256]{2,1,0:T(8,128)(2,1)}), bf16[32,16,256]{2,1,0:T(8,128)(2,1)S(1)}, u32[]{:S(2)}, u32[]{:S(2)}) async-start(bf16[32,16,256]{2,1,0:T(8,128)(2,1)} %bitcast.12), calls=%async_computation | async-start | bytes 524288 | tf_op jit(solution)/shard_map/all_to_all | solution.py:312
  12.7 3.6 %shard_map.106 = (bf16[512,768]{1,0:T(8,128)(2,1)}, bf16[512,768]{1,0:T(8,128)(2,1)}, bf16[512,768]{1,0:T(8,128)(2,1)}, bf16[16,128]{1,0:T(8,128)(2,1)}) custom-call(s32[2]{0:T(128)} %pad_add_fusion.place, bf16[4096,512]{1,0:T(8,128)(2,1)} %refs_9_.1, bf16[4096,128]{1,0:T(8,128)(2,1)} %refs_10_.1, bf16[4096,128]{1,0:T(8,128)(2,1)} %refs_11_.1, ...), custom_call_target="tpu_custom_call" | custom-call | bytes 4718592 | tf_op jit(solution)/shard_map/pallas_call | solution.py:185
  17.9 2.7 %collective-permute-start.5 = (bf16[512,768]{1,0:T(8,128)(2,1)}, bf16[512,768]{1,0:T(8,128)(2,1)}, u32[]{:S(2)}, u32[]{:S(2)}) collective-permute-start(bf16[512,768]{1,0:T(8,128)(2,1)} %get-tuple-element.32), channel_id=1, source_target_pairs={{0,2},{1,3},{2,0},{3,1},{4,6},{5,7},{6,4},{7,5},{8,10},{9,11},{10,... | collective-permute-start | bytes 2359304 | tf_op jit(solution)/shard_map/ppermute | solution.py:273
  21.8 2.4 %all-to-all-done.pieces = bf16[32,16,256]{2,1,0:T(8,128)(2,1)S(1)} async-done(((bf16[32,16,256]{2,1,0:T(8,128)(2,1)}), bf16[32,16,256]{2,1,0:T(8,128)(2,1)S(1)}, u32[]{:S(2)}, u32[]{:S(2)}) %all-to-all-start) | async-done | bytes 262176 | tf_op jit(solution)/shard_map/all_to_all | solution.py:312
  25.9 6.0 %all-to-all-start.1 = ((bf16[32,2,16,256]{3,2,1,0:T(8,128)(2,1)}), bf16[32,2,16,256]{3,2,1,0:T(8,128)(2,1)}, u32[]{:S(2)}, u32[]{:S(2)}) async-start(bf16[32,2,16,256]{3,2,1,0:T(8,128)(2,1)} %shard_map.102), calls=%async_computation.1 | async-start | bytes 1048576 | tf_op jit(solution)/shard_map/all_to_all | solution.py:322
  32.6 8.0 %shard_map.101 = (f32[4,1,512]{2,1,0:T(1,128)}, f32[4,128,512]{2,1,0:T(8,128)}, f32[512,256]{1,0:T(8,128)}, bf16[512,256]{1,0:T(8,128)(2,1)}) custom-call(s32[1]{0:T(128)} %bitcast.place, bf16[512,512]{1,0:T(8,128)(2,1)} %queries.3, bf16[512,512]{1,0:T(8,128)(2,1)} %output_grad.3, bf16[512,512]{1,0:T(8,128)(2,1)} %output_rows.1, f32[4,1,512]{2,1,0:T(1,128)} %reshape.13.norm, ...), custom_call_target="tpu_custom_call" | custom-call | flops 805306368000 | bytes 4194304 | tf_op jit(solution)/shard_map/pallas_call | solution.py:325
  40.6 9.0 %all-to-all-done.1.chosen = bf16[32,2,16,256]{3,2,1,0:T(8,128)(2,1)} async-done(((bf16[32,2,16,256]{3,2,1,0:T(8,128)(2,1)}), bf16[32,2,16,256]{3,2,1,0:T(8,128)(2,1)}, u32[]{:S(2)}, u32[]{:S(2)}) %all-to-all-start.1) | async-done | bytes 524320 | tf_op jit(solution)/shard_map/all_to_all | solution.py:322
  49.6 5.8 %shard_map.103 = (bf16[512,512]{1,0:T(8,128)(2,1)}, bf16[32,2,16,256]{3,2,1,0:T(8,128)(2,1)}, bf16[16,128]{1,0:T(8,128)(2,1)}) custom-call(s32[1]{0:T(128)} %bitcast.place, s32[32,3]{1,0:T(8,128)} %copy-done.1, bf16[512,512]{1,0:T(8,128)(2,1)} %queries.3, bf16[512,512]{1,0:T(8,128)(2,1)} %output_grad.3, f32[4,1,512]{2,1,0:T(1,128)} %reshape.13.norm, ...), custom_call_target="tpu_custom_call" | custom-call | flops 8053063680 | bytes 4194304 | tf_op jit(solution)/shard_map/pallas_call | solution.py:343
  55.9 3.4 %collective-permute-done.6.refs_2_ = bf16[512,768]{1,0:T(8,128)(2,1)} collective-permute-done((bf16[512,768]{1,0:T(8,128)(2,1)}, bf16[512,768]{1,0:T(8,128)(2,1)}, u32[]{:S(2)}, u32[]{:S(2)}) %collective-permute-start.6) | collective-permute-done | bytes 786464 | tf_op jit(solution)/shard_map/ppermute | solution.py:273
  59.3 7.5 %all-to-all-start.2 = ((bf16[32,2,16,256]{3,2,1,0:T(8,128)(2,1)}), bf16[32,2,16,256]{3,2,1,0:T(8,128)(2,1)S(1)}, u32[]{:S(2)}, u32[]{:S(2)}) async-start(bf16[32,2,16,256]{3,2,1,0:T(8,128)(2,1)} %get-tuple-element.29), calls=%async_computation.2 | async-start | bytes 1048576 | tf_op jit(solution)/shard_map/all_to_all | solution.py:358
  67.4 1.9 %collective-permute-start.2 = (bf16[512,512]{1,0:T(8,128)(2,1)}, bf16[512,512]{1,0:T(8,128)(2,1)S(1)}, u32[]{:S(2)}, u32[]{:S(2)}) collective-permute-start(bf16[512,512]{1,0:T(8,128)(2,1)} %get-tuple-element.30.refs_0_), channel_id=1, source_target_pairs={{0,2},{1,3},{2,0},{3,1},{4,6},{5,7},{6,4},{7,5},{8,10},{9,11},{10,... | collective-permute-start | bytes 1572872 | tf_op jit(solution)/shard_map/ppermute | solution.py:273
  69.4 2.8 %collective-permute-start.3 = (bf16[512,512]{1,0:T(8,128)(2,1)}, bf16[512,512]{1,0:T(8,128)(2,1)S(1)}, u32[]{:S(2)}, u32[]{:S(2)}) collective-permute-start(bf16[512,512]{1,0:T(8,128)(2,1)} %get-tuple-element.30.refs_0_), channel_id=1, source_target_pairs={{0,3},{1,2},{2,1},{3,0},{4,7},{5,6},{6,5},{7,4},{8,11},{9,10},{10,... | collective-permute-start | bytes 1572872 | tf_op jit(solution)/shard_map/ppermute | solution.py:273
  73.1 6.9 %shard_map.107 = (bf16[1024,2048]{1,0:T(8,128)(2,1)}, bf16[512,1024]{1,0:T(8,128)(2,1)}, bf16[512,1024]{1,0:T(8,128)(2,1)}, bf16[16,128]{1,0:T(8,128)(2,1)}) custom-call(s32[2]{0:T(128)} %pad_add_fusion.place, bf16[512,768]{1,0:T(8,128)(2,1)} %collective-permute-done.4.refs_0_, bf16[512,768]{1,0:T(8,128)(2,1)} %collective-permute-done.5.refs_1_, ...), custom_call_target="tpu_custom_call" | custom-call | bytes 12591104 | tf_op jit(solution)/shard_map/pallas_call | solution.py:234
  79.9 4.6 %all-to-all-done.2.parts = bf16[32,2,16,256]{3,2,1,0:T(8,128)(2,1)S(1)} async-done(((bf16[32,2,16,256]{3,2,1,0:T(8,128)(2,1)}), bf16[32,2,16,256]{3,2,1,0:T(8,128)(2,1)S(1)}, u32[]{:S(2)}, u32[]{:S(2)}) %all-to-all-start.2) | async-done | bytes 524320 | tf_op jit(solution)/shard_map/all_to_all | solution.py:358
  84.5 1.9 %shard_map.104.refs_4_ = bf16[32,16,256]{2,1,0:T(8,128)(2,1)} custom-call(s32[32,3]{1,0:T(8,128)S(1)} %copy-done.2, bf16[32,2,16,256]{3,2,1,0:T(8,128)(2,1)S(1)} %all-to-all-done.2.parts), custom_call_target="tpu_custom_call" | custom-call | bytes 786432 | tf_op jit(solution)/shard_map/pallas_call | solution.py:363
  86.4 4.1 %all-to-all-start.3 = ((bf16[32,16,256]{2,1,0:T(8,128)(2,1)}), bf16[32,16,256]{2,1,0:T(8,128)(2,1)S(1)}, u32[]{:S(2)}, u32[]{:S(2)}) async-start(bf16[32,16,256]{2,1,0:T(8,128)(2,1)} %shard_map.104.refs_4_), calls=%async_computation.3 | async-start | bytes 524288 | tf_op jit(solution)/shard_map/all_to_all | solution.py:375
  90.6 2.3 %collective-permute-done.2.refs_2_ = bf16[512,512]{1,0:T(8,128)(2,1)S(1)} collective-permute-done((bf16[512,512]{1,0:T(8,128)(2,1)}, bf16[512,512]{1,0:T(8,128)(2,1)S(1)}, u32[]{:S(2)}, u32[]{:S(2)}) %collective-permute-start.2) | collective-permute-done | bytes 524320 | tf_op jit(solution)/shard_map/ppermute | solution.py:273
  92.9 2.6 %collective-permute-done.3.refs_3_ = bf16[512,512]{1,0:T(8,128)(2,1)S(1)} collective-permute-done((bf16[512,512]{1,0:T(8,128)(2,1)}, bf16[512,512]{1,0:T(8,128)(2,1)S(1)}, u32[]{:S(2)}, u32[]{:S(2)}) %collective-permute-start.3) | collective-permute-done | bytes 524320 | tf_op jit(solution)/shard_map/ppermute | solution.py:273
  95.6 2.4 %fusion.8 = f32[512,1024]{1,0:T(8,128)S(1)} fusion(bf16[512,2048]{1,0:T(8,128)(2,1)S(1)} %shard_map.105, bf16[1024,2048]{1,0:T(8,128)(2,1)S(1)} %copy-done.8), kind=kOutput, calls=%fused_computation.20 | convolution fusion | flops 2147483648 | bytes 8388608 | tf_op jit(solution)/shard_map/dot_general | solution.py:281
  98.2 4.5 %all-to-all-done.3 = bf16[32,16,256]{2,1,0:T(8,128)(2,1)S(1)} async-done(((bf16[32,16,256]{2,1,0:T(8,128)(2,1)}), bf16[32,16,256]{2,1,0:T(8,128)(2,1)S(1)}, u32[]{:S(2)}, u32[]{:S(2)}) %all-to-all-start.3) | async-done | bytes 262176 | tf_op jit(solution)/shard_map/all_to_all | solution.py:375
  105.0 3.0 %collective-permute-start.14 = (bf16[256,256]{1,0:T(8,128)(2,1)S(1)}, bf16[256,256]{1,0:T(8,128)(2,1)S(1)}, u32[]{:S(2)}, u32[]{:S(2)}) collective-permute-start(bf16[256,256]{1,0:T(8,128)(2,1)S(1)} %get-tuple-element.51), channel_id=1, source_target_pairs={{0,1},{1,0},{2,3},{3,2},{4,5},{5,4},{6,7},{7,6},{8,9},{9,8},{10,11... | collective-permute-start | bytes 393224 | tf_op jit(solution)/shard_map/ppermute | solution.py:273
  110.1 4.7 %collective-permute-done.16 = bf16[256,256]{1,0:T(8,128)(2,1)S(1)} collective-permute-done((bf16[256,256]{1,0:T(8,128)(2,1)S(1)}, bf16[256,256]{1,0:T(8,128)(2,1)S(1)}, u32[]{:S(2)}, u32[]{:S(2)}) %collective-permute-start.16) | collective-permute-done | bytes 131104 | tf_op jit(solution)/shard_map/ppermute | solution.py:273
  122.5 4.8 %collective-permute-done.18 = bf16[256,512]{1,0:T(8,128)(2,1)S(1)} collective-permute-done((bf16[256,512]{1,0:T(8,128)(2,1)S(1)}, bf16[256,512]{1,0:T(8,128)(2,1)S(1)}, u32[]{:S(2)}, u32[]{:S(2)}) %collective-permute-start.18) | collective-permute-done | bytes 262176 | tf_op jit(solution)/shard_map/ppermute | solution.py:387
  127.4 2.7 %collective-permute-done.17 = bf16[256,512]{1,0:T(8,128)(2,1)S(1)} collective-permute-done((bf16[256,512]{1,0:T(8,128)(2,1)S(1)}, bf16[256,512]{1,0:T(8,128)(2,1)S(1)}, u32[]{:S(2)}, u32[]{:S(2)}) %collective-permute-start.17) | collective-permute-done | bytes 262176 | tf_op jit(solution)/shard_map/ppermute | solution.py:387
  (69 shorter events, 23.2 us)
Async XLA Ops:
  1.7 22.4 %all-to-all-start = ((bf16[32,16,256]{2,1,0:T(8,128)(2,1)}), bf16[32,16,256]{2,1,0:T(8,128)(2,1)S(1)}, u32[]{:S(2)}, u32[]{:S(2)}) async-start(bf16[32,16,256]{2,1,0:T(8,128)(2,1)} %bitcast.12), calls=%async_computation | async-start | bytes 524288 | tf_op jit(solution)/shard_map/all_to_all | solution.py:312
  11.8 20.0 %collective-permute-start = (bf16[512,256]{1,0:T(8,128)(2,1)}, bf16[512,256]{1,0:T(8,128)(2,1)S(1)}, u32[]{:S(2)}, u32[]{:S(2)}) collective-permute-start(bf16[512,256]{1,0:T(8,128)(2,1)} %shard_map.100.own), channel_id=1, source_target_pairs={{0,8},{8,16},{16,24},{24,32},{32,40},{40,48},{48,56},{56,64},{64,7... | collective-permute-start | bytes 786440 | tf_op jit(solution)/shard_map/ppermute | solution.py:311
  16.3 39.0 %collective-permute-start.4 = (bf16[512,768]{1,0:T(8,128)(2,1)}, bf16[512,768]{1,0:T(8,128)(2,1)}, u32[]{:S(2)}, u32[]{:S(2)}) collective-permute-start(bf16[512,768]{1,0:T(8,128)(2,1)} %get-tuple-element.31), channel_id=1, source_target_pairs={{0,1},{1,0},{2,3},{3,2},{4,5},{5,4},{6,7},{7,6},{8,9},{9,8},{10,11... | collective-permute-start | bytes 2359304 | tf_op jit(solution)/shard_map/ppermute | solution.py:273
  17.9 38.0 %collective-permute-start.5 = (bf16[512,768]{1,0:T(8,128)(2,1)}, bf16[512,768]{1,0:T(8,128)(2,1)}, u32[]{:S(2)}, u32[]{:S(2)}) collective-permute-start(bf16[512,768]{1,0:T(8,128)(2,1)} %get-tuple-element.32), channel_id=1, source_target_pairs={{0,2},{1,3},{2,0},{3,1},{4,6},{5,7},{6,4},{7,5},{8,10},{9,11},{10,... | collective-permute-start | bytes 2359304 | tf_op jit(solution)/shard_map/ppermute | solution.py:273
  20.6 38.7 %collective-permute-start.6 = (bf16[512,768]{1,0:T(8,128)(2,1)}, bf16[512,768]{1,0:T(8,128)(2,1)}, u32[]{:S(2)}, u32[]{:S(2)}) collective-permute-start(bf16[512,768]{1,0:T(8,128)(2,1)} %get-tuple-element.33), channel_id=1, source_target_pairs={{0,3},{1,2},{2,1},{3,0},{4,7},{5,6},{6,5},{7,4},{8,11},{9,10},{10,... | collective-permute-start | bytes 2359304 | tf_op jit(solution)/shard_map/ppermute | solution.py:273
  25.9 23.7 %all-to-all-start.1 = ((bf16[32,2,16,256]{3,2,1,0:T(8,128)(2,1)}), bf16[32,2,16,256]{3,2,1,0:T(8,128)(2,1)}, u32[]{:S(2)}, u32[]{:S(2)}) async-start(bf16[32,2,16,256]{3,2,1,0:T(8,128)(2,1)} %shard_map.102), calls=%async_computation.1 | async-start | bytes 1048576 | tf_op jit(solution)/shard_map/all_to_all | solution.py:322
  59.3 10.0 %collective-permute-start.7 = (bf16[512,768]{1,0:T(8,128)(2,1)}, bf16[512,768]{1,0:T(8,128)(2,1)S(1)}, u32[]{:S(2)}, u32[]{:S(2)}) collective-permute-start(bf16[512,768]{1,0:T(8,128)(2,1)} %collective-permute-done.4.refs_0_), channel_id=1, source_target_pairs={{0,8},{8,0},{16,24},{24,16},{32,40},{40,32},{48,56},{56,48},{64,72... | collective-permute-start | bytes 2359304 | tf_op jit(solution)/shard_map/ppermute | solution.py:360
  59.3 25.2 %all-to-all-start.2 = ((bf16[32,2,16,256]{3,2,1,0:T(8,128)(2,1)}), bf16[32,2,16,256]{3,2,1,0:T(8,128)(2,1)S(1)}, u32[]{:S(2)}, u32[]{:S(2)}) async-start(bf16[32,2,16,256]{3,2,1,0:T(8,128)(2,1)} %get-tuple-element.29), calls=%async_computation.2 | async-start | bytes 1048576 | tf_op jit(solution)/shard_map/all_to_all | solution.py:358
  66.8 5.3 %collective-permute-start.8 = (bf16[512,768]{1,0:T(8,128)(2,1)}, bf16[512,768]{1,0:T(8,128)(2,1)S(1)}, u32[]{:S(2)}, u32[]{:S(2)}) collective-permute-start(bf16[512,768]{1,0:T(8,128)(2,1)} %collective-permute-done.5.refs_1_), channel_id=1, source_target_pairs={{0,8},{8,0},{16,24},{24,16},{32,40},{40,32},{48,56},{56,48},{64,72... | collective-permute-start | bytes 2359304 | tf_op jit(solution)/shard_map/ppermute | solution.py:360
  67.1 6.0 %collective-permute-start.9 = (bf16[512,768]{1,0:T(8,128)(2,1)}, bf16[512,768]{1,0:T(8,128)(2,1)}, u32[]{:S(2)}, u32[]{:S(2)}) collective-permute-start(bf16[512,768]{1,0:T(8,128)(2,1)} %collective-permute-done.6.refs_2_), channel_id=1, source_target_pairs={{0,8},{8,0},{16,24},{24,16},{32,40},{40,32},{48,56},{56,48},{64,72... | collective-permute-start | bytes 2359304 | tf_op jit(solution)/shard_map/ppermute | solution.py:360
  67.4 23.1 %collective-permute-start.1 = (bf16[512,512]{1,0:T(8,128)(2,1)}, bf16[512,512]{1,0:T(8,128)(2,1)S(1)}, u32[]{:S(2)}, u32[]{:S(2)}) collective-permute-start(bf16[512,512]{1,0:T(8,128)(2,1)} %get-tuple-element.30.refs_0_), channel_id=1, source_target_pairs={{0,1},{1,0},{2,3},{3,2},{4,5},{5,4},{6,7},{7,6},{8,9},{9,8},{10,11... | collective-permute-start | bytes 1572872 | tf_op jit(solution)/shard_map/ppermute | solution.py:273
  67.4 25.4 %collective-permute-start.2 = (bf16[512,512]{1,0:T(8,128)(2,1)}, bf16[512,512]{1,0:T(8,128)(2,1)S(1)}, u32[]{:S(2)}, u32[]{:S(2)}) collective-permute-start(bf16[512,512]{1,0:T(8,128)(2,1)} %get-tuple-element.30.refs_0_), channel_id=1, source_target_pairs={{0,2},{1,3},{2,0},{3,1},{4,6},{5,7},{6,4},{7,5},{8,10},{9,11},{10,... | collective-permute-start | bytes 1572872 | tf_op jit(solution)/shard_map/ppermute | solution.py:273
  69.4 26.1 %collective-permute-start.3 = (bf16[512,512]{1,0:T(8,128)(2,1)}, bf16[512,512]{1,0:T(8,128)(2,1)S(1)}, u32[]{:S(2)}, u32[]{:S(2)}) collective-permute-start(bf16[512,512]{1,0:T(8,128)(2,1)} %get-tuple-element.30.refs_0_), channel_id=1, source_target_pairs={{0,3},{1,2},{2,1},{3,0},{4,7},{5,6},{6,5},{7,4},{8,11},{9,10},{10,... | collective-permute-start | bytes 1572872 | tf_op jit(solution)/shard_map/ppermute | solution.py:273
  73.0 22.4 %copy-start = (bf16[512,512]{1,0:T(8,128)(2,1)S(1)}, bf16[512,512]{1,0:T(8,128)(2,1)}, u32[]{:S(2)}) copy-start(bf16[512,512]{1,0:T(8,128)(2,1)} %get-tuple-element.30.refs_0_) | copy-start | bytes 1572868
  73.0 29.7 %collective-permute-start.10 = (bf16[512,256]{1,0:T(8,128)(2,1)}, bf16[512,256]{1,0:T(8,128)(2,1)}, u32[]{:S(2)}, u32[]{:S(2)}) collective-permute-start(bf16[512,256]{1,0:T(8,128)(2,1)} %get-tuple-element.42), channel_id=1, source_target_pairs={{0,248},{8,0},{16,8},{24,16},{32,24},{40,32},{48,40},{56,48},{64,5... | collective-permute-start | bytes 786440 | tf_op jit(solution)/shard_map/ppermute | solution.py:340
  86.4 16.3 %all-to-all-start.3 = ((bf16[32,16,256]{2,1,0:T(8,128)(2,1)}), bf16[32,16,256]{2,1,0:T(8,128)(2,1)S(1)}, u32[]{:S(2)}, u32[]{:S(2)}) async-start(bf16[32,16,256]{2,1,0:T(8,128)(2,1)} %shard_map.104.refs_4_), calls=%async_computation.3 | async-start | bytes 524288 | tf_op jit(solution)/shard_map/all_to_all | solution.py:375
  103.8 11.0 %collective-permute-start.16 = (bf16[256,256]{1,0:T(8,128)(2,1)S(1)}, bf16[256,256]{1,0:T(8,128)(2,1)S(1)}, u32[]{:S(2)}, u32[]{:S(2)}) collective-permute-start(bf16[256,256]{1,0:T(8,128)(2,1)S(1)} %get-tuple-element.51), channel_id=1, source_target_pairs={{0,3},{1,2},{2,1},{3,0},{4,7},{5,6},{6,5},{7,4},{8,11},{9,10},{10,... | collective-permute-start | bytes 393224 | tf_op jit(solution)/shard_map/ppermute | solution.py:273
  104.4 10.4 %collective-permute-start.15 = (bf16[256,256]{1,0:T(8,128)(2,1)S(1)}, bf16[256,256]{1,0:T(8,128)(2,1)S(1)}, u32[]{:S(2)}, u32[]{:S(2)}) collective-permute-start(bf16[256,256]{1,0:T(8,128)(2,1)S(1)} %get-tuple-element.51), channel_id=1, source_target_pairs={{0,2},{1,3},{2,0},{3,1},{4,6},{5,7},{6,4},{7,5},{8,10},{9,11},{10,... | collective-permute-start | bytes 393224 | tf_op jit(solution)/shard_map/ppermute | solution.py:273
  105.0 10.2 %collective-permute-start.14 = (bf16[256,256]{1,0:T(8,128)(2,1)S(1)}, bf16[256,256]{1,0:T(8,128)(2,1)S(1)}, u32[]{:S(2)}, u32[]{:S(2)}) collective-permute-start(bf16[256,256]{1,0:T(8,128)(2,1)S(1)} %get-tuple-element.51), channel_id=1, source_target_pairs={{0,1},{1,0},{2,3},{3,2},{4,5},{5,4},{6,7},{7,6},{8,9},{9,8},{10,11... | collective-permute-start | bytes 393224 | tf_op jit(solution)/shard_map/ppermute | solution.py:273
  108.0 10.3 %collective-permute-start.13 = (bf16[256,256]{1,0:T(8,128)(2,1)S(1)}, bf16[256,256]{1,0:T(8,128)(2,1)S(1)}, u32[]{:S(2)}, u32[]{:S(2)}) collective-permute-start(bf16[256,256]{1,0:T(8,128)(2,1)S(1)} %get-tuple-element.52), channel_id=1, source_target_pairs={{0,3},{1,2},{2,1},{3,0},{4,7},{5,6},{6,5},{7,4},{8,11},{9,10},{10,... | collective-permute-start | bytes 393224 | tf_op jit(solution)/shard_map/ppermute | solution.py:273
  108.5 9.8 %collective-permute-start.12 = (bf16[256,256]{1,0:T(8,128)(2,1)S(1)}, bf16[256,256]{1,0:T(8,128)(2,1)S(1)}, u32[]{:S(2)}, u32[]{:S(2)}) collective-permute-start(bf16[256,256]{1,0:T(8,128)(2,1)S(1)} %get-tuple-element.52), channel_id=1, source_target_pairs={{0,2},{1,3},{2,0},{3,1},{4,6},{5,7},{6,4},{7,5},{8,10},{9,11},{10,... | collective-permute-start | bytes 393224 | tf_op jit(solution)/shard_map/ppermute | solution.py:273
  114.8 5.0 %collective-permute-start.11 = (bf16[256,256]{1,0:T(8,128)(2,1)S(1)}, bf16[256,256]{1,0:T(8,128)(2,1)S(1)}, u32[]{:S(2)}, u32[]{:S(2)}) collective-permute-start(bf16[256,256]{1,0:T(8,128)(2,1)S(1)} %get-tuple-element.52), channel_id=1, source_target_pairs={{0,1},{1,0},{2,3},{3,2},{4,5},{5,4},{6,7},{7,6},{8,9},{9,8},{10,11... | collective-permute-start | bytes 393224 | tf_op jit(solution)/shard_map/ppermute | solution.py:273
  116.9 10.4 %collective-permute-start.18 = (bf16[256,512]{1,0:T(8,128)(2,1)S(1)}, bf16[256,512]{1,0:T(8,128)(2,1)S(1)}, u32[]{:S(2)}, u32[]{:S(2)}) collective-permute-start(bf16[256,512]{1,0:T(8,128)(2,1)S(1)} %fusion.1), channel_id=1, source_target_pairs={{0,4},{1,5},{2,6},{3,7},{4,0},{5,1},{6,2},{7,3},{8,12},{9,13},{10,... | collective-permute-start | bytes 786440 | tf_op jit(solution)/shard_map/ppermute | solution.py:387
  120.2 9.9 %collective-permute-start.17 = (bf16[256,512]{1,0:T(8,128)(2,1)S(1)}, bf16[256,512]{1,0:T(8,128)(2,1)S(1)}, u32[]{:S(2)}, u32[]{:S(2)}) collective-permute-start(bf16[256,512]{1,0:T(8,128)(2,1)S(1)} %fusion), channel_id=1, source_target_pairs={{0,4},{1,5},{2,6},{3,7},{4,0},{5,1},{6,2},{7,3},{8,12},{9,13},{10,... | collective-permute-start | bytes 786440 | tf_op jit(solution)/shard_map/ppermute | solution.py:387
  (11 other events, 83.6 us)

commit v6 on v5

--- a/solution.py
+++ b/solution.py
@@ -59,7 +59,7 @@
 
         return carry
 
-    lax.fori_loop(0, BLOCKS, step, 0, unroll=8)
+    lax.fori_loop(0, BLOCKS, step, 0, unroll=True)
     out[...] = total[...].astype(BF)
 
 
@@ -175,7 +175,7 @@
 
 
 def pack_weights(place, weights):
-    steps = 2
+    steps = 1
     rows, width = BLOCK // steps, (HEADS + 2) * HD
 
     def index(partner):

time: 132 us -> 133 us (level)
  transfers between devices with their start and end apart: 23 -> 23, of which waited for: 13 -> 13; matrix products, arithmetic and copies ran while one was open for 5% -> 5% of each run, Pallas kernels for 21% -> 22%
where the time goes in v6:
time: 133 us; the launch traced here: 131 us
  starting transfers between devices  47.2 us (35%)
  waiting for transfers between devices  43.2 us (32%)
  Pallas kernels  30 us (23%)
  matrix products  5.48 us (4%)
  other arithmetic  2.67 us (2%)
  local copies, waits for them, and re-layouts  2.56 us (2%)
    ppermute x12, starting transfers between devices, over_x(): lax.ppermute(value, 'grp', [(source, source ^ partner) for source in rang...  15.9 us
    ppermute x12, waiting for transfers between devices, over_x(): lax.ppermute(value, 'grp', [(source, source ^ partner) for source in rang...  15.4 us
    all_to_all x1, starting transfers between devices, on_device(): pieces = lax.all_to_all(own.reshape(BLOCKS, PIECE, 2 * HD), 'ctx', 0, 0)  10.1 us
    all_to_all x1, waiting for transfers between devices, on_device(): chosen = lax.all_to_all(picked, 'ctx', 0, 0)  8.98 us
    pallas_call x1, Pallas kernels, on_device(): pl.pallas_call(near_kernel, grid=(1,), in_specs=[smem] + [whole(array.sha...  8.03 us
    ppermute x2, waiting for transfers between devices, on_device(): got.append(lax.ppermute(sent, 'grp', pairs))  7.54 us
    all_to_all x1, starting transfers between devices, on_device(): returned = lax.all_to_all(chosen_grad, 'ctx', 0, 0)  7.48 us
    pallas_call x1, Pallas kernels, unpack_weights(): pl.pallas_call(unpack_kernel, grid_spec=pltpu.PrefetchScalarGridSpec(num_...  6.86 us
  transfers between devices with their start and end apart: 23, of which 13 were waited for; matrix products, arithmetic and copies ran while one was open for 5% of the time, Pallas kernels for 22%

profile of v6, /device:TPU:24, one launch (start us, length us, event | category | flops | bytes accessed | tf_op | source)
XLA Modules:
  0.0 131.3 jit_solution(187621363577594269)
XLA Ops:
  1.7 10.1 %all-to-all-start = ((bf16[32,16,256]{2,1,0:T(8,128)(2,1)}), bf16[32,16,256]{2,1,0:T(8,128)(2,1)S(1)}, u32[]{:S(2)}, u32[]{:S(2)}) async-start(bf16[32,16,256]{2,1,0:T(8,128)(2,1)} %bitcast.12), calls=%async_computation | async-start | bytes 524288 | tf_op jit(solution)/shard_map/all_to_all | solution.py:312
  12.7 3.9 %shard_map.106 = (bf16[512,768]{1,0:T(8,128)(2,1)}, bf16[512,768]{1,0:T(8,128)(2,1)}, bf16[512,768]{1,0:T(8,128)(2,1)}, bf16[16,128]{1,0:T(8,128)(2,1)}) custom-call(s32[2]{0:T(128)} %pad_add_fusion.place, bf16[4096,512]{1,0:T(8,128)(2,1)} %refs_9_.1, bf16[4096,128]{1,0:T(8,128)(2,1)} %refs_10_.1, bf16[4096,128]{1,0:T(8,128)(2,1)} %refs_11_.1, ...), custom_call_target="tpu_custom_call" | custom-call | bytes 4718592 | tf_op jit(solution)/shard_map/pallas_call | solution.py:185
  18.1 2.7 %collective-permute-start.5 = (bf16[512,768]{1,0:T(8,128)(2,1)}, bf16[512,768]{1,0:T(8,128)(2,1)}, u32[]{:S(2)}, u32[]{:S(2)}) collective-permute-start(bf16[512,768]{1,0:T(8,128)(2,1)} %get-tuple-element.32), channel_id=1, source_target_pairs={{0,2},{1,3},{2,0},{3,1},{4,6},{5,7},{6,4},{7,5},{8,10},{9,11},{10,... | collective-permute-start | bytes 2359304 | tf_op jit(solution)/shard_map/ppermute | solution.py:273
  22.0 2.2 %all-to-all-done.pieces = bf16[32,16,256]{2,1,0:T(8,128)(2,1)S(1)} async-done(((bf16[32,16,256]{2,1,0:T(8,128)(2,1)}), bf16[32,16,256]{2,1,0:T(8,128)(2,1)S(1)}, u32[]{:S(2)}, u32[]{:S(2)}) %all-to-all-start) | async-done | bytes 262176 | tf_op jit(solution)/shard_map/all_to_all | solution.py:312
  25.9 6.2 %all-to-all-start.1 = ((bf16[32,2,16,256]{3,2,1,0:T(8,128)(2,1)}), bf16[32,2,16,256]{3,2,1,0:T(8,128)(2,1)}, u32[]{:S(2)}, u32[]{:S(2)}) async-start(bf16[32,2,16,256]{3,2,1,0:T(8,128)(2,1)} %shard_map.102), calls=%async_computation.1 | async-start | bytes 1048576 | tf_op jit(solution)/shard_map/all_to_all | solution.py:322
  32.8 8.0 %shard_map.101 = (f32[4,1,512]{2,1,0:T(1,128)}, f32[4,128,512]{2,1,0:T(8,128)}, f32[512,256]{1,0:T(8,128)}, bf16[512,256]{1,0:T(8,128)(2,1)}) custom-call(s32[1]{0:T(128)} %bitcast.place, bf16[512,512]{1,0:T(8,128)(2,1)} %queries.3, bf16[512,512]{1,0:T(8,128)(2,1)} %output_grad.3, bf16[512,512]{1,0:T(8,128)(2,1)} %output_rows.1, f32[4,1,512]{2,1,0:T(1,128)} %reshape.13.norm, ...), custom_call_target="tpu_custom_call" | custom-call | flops 805306368000 | bytes 4194304 | tf_op jit(solution)/shard_map/pallas_call | solution.py:325
  40.8 9.0 %all-to-all-done.1.chosen = bf16[32,2,16,256]{3,2,1,0:T(8,128)(2,1)} async-done(((bf16[32,2,16,256]{3,2,1,0:T(8,128)(2,1)}), bf16[32,2,16,256]{3,2,1,0:T(8,128)(2,1)}, u32[]{:S(2)}, u32[]{:S(2)}) %all-to-all-start.1) | async-done | bytes 524320 | tf_op jit(solution)/shard_map/all_to_all | solution.py:322
  49.8 5.8 %shard_map.103 = (bf16[512,512]{1,0:T(8,128)(2,1)}, bf16[32,2,16,256]{3,2,1,0:T(8,128)(2,1)}, bf16[16,128]{1,0:T(8,128)(2,1)}) custom-call(s32[1]{0:T(128)} %bitcast.place, s32[32,3]{1,0:T(8,128)} %copy-done.1, bf16[512,512]{1,0:T(8,128)(2,1)} %queries.3, bf16[512,512]{1,0:T(8,128)(2,1)} %output_grad.3, f32[4,1,512]{2,1,0:T(1,128)} %reshape.13.norm, ...), custom_call_target="tpu_custom_call" | custom-call | flops 8053063680 | bytes 4194304 | tf_op jit(solution)/shard_map/pallas_call | solution.py:343
  56.1 3.4 %collective-permute-done.6.refs_2_ = bf16[512,768]{1,0:T(8,128)(2,1)} collective-permute-done((bf16[512,768]{1,0:T(8,128)(2,1)}, bf16[512,768]{1,0:T(8,128)(2,1)}, u32[]{:S(2)}, u32[]{:S(2)}) %collective-permute-start.6) | collective-permute-done | bytes 786464 | tf_op jit(solution)/shard_map/ppermute | solution.py:273
  59.5 7.5 %all-to-all-start.2 = ((bf16[32,2,16,256]{3,2,1,0:T(8,128)(2,1)}), bf16[32,2,16,256]{3,2,1,0:T(8,128)(2,1)S(1)}, u32[]{:S(2)}, u32[]{:S(2)}) async-start(bf16[32,2,16,256]{3,2,1,0:T(8,128)(2,1)} %get-tuple-element.29), calls=%async_computation.2 | async-start | bytes 1048576 | tf_op jit(solution)/shard_map/all_to_all | solution.py:358
  67.6 1.9 %collective-permute-start.2 = (bf16[512,512]{1,0:T(8,128)(2,1)}, bf16[512,512]{1,0:T(8,128)(2,1)S(1)}, u32[]{:S(2)}, u32[]{:S(2)}) collective-permute-start(bf16[512,512]{1,0:T(8,128)(2,1)} %get-tuple-element.30.refs_0_), channel_id=1, source_target_pairs={{0,2},{1,3},{2,0},{3,1},{4,6},{5,7},{6,4},{7,5},{8,10},{9,11},{10,... | collective-permute-start | bytes 1572872 | tf_op jit(solution)/shard_map/ppermute | solution.py:273
  69.6 2.8 %collective-permute-start.3 = (bf16[512,512]{1,0:T(8,128)(2,1)}, bf16[512,512]{1,0:T(8,128)(2,1)S(1)}, u32[]{:S(2)}, u32[]{:S(2)}) collective-permute-start(bf16[512,512]{1,0:T(8,128)(2,1)} %get-tuple-element.30.refs_0_), channel_id=1, source_target_pairs={{0,3},{1,2},{2,1},{3,0},{4,7},{5,6},{6,5},{7,4},{8,11},{9,10},{10,... | collective-permute-start | bytes 1572872 | tf_op jit(solution)/shard_map/ppermute | solution.py:273
  73.3 6.9 %shard_map.107 = (bf16[1024,2048]{1,0:T(8,128)(2,1)}, bf16[512,1024]{1,0:T(8,128)(2,1)}, bf16[512,1024]{1,0:T(8,128)(2,1)}, bf16[16,128]{1,0:T(8,128)(2,1)}) custom-call(s32[2]{0:T(128)} %pad_add_fusion.place, bf16[512,768]{1,0:T(8,128)(2,1)} %collective-permute-done.4.refs_0_, bf16[512,768]{1,0:T(8,128)(2,1)} %collective-permute-done.5.refs_1_, ...), custom_call_target="tpu_custom_call" | custom-call | bytes 12591104 | tf_op jit(solution)/shard_map/pallas_call | solution.py:234
  80.1 4.6 %all-to-all-done.2.parts = bf16[32,2,16,256]{3,2,1,0:T(8,128)(2,1)S(1)} async-done(((bf16[32,2,16,256]{3,2,1,0:T(8,128)(2,1)}), bf16[32,2,16,256]{3,2,1,0:T(8,128)(2,1)S(1)}, u32[]{:S(2)}, u32[]{:S(2)}) %all-to-all-start.2) | async-done | bytes 524320 | tf_op jit(solution)/shard_map/all_to_all | solution.py:358
  84.7 1.9 %shard_map.104.refs_4_ = bf16[32,16,256]{2,1,0:T(8,128)(2,1)} custom-call(s32[32,3]{1,0:T(8,128)S(1)} %copy-done.2, bf16[32,2,16,256]{3,2,1,0:T(8,128)(2,1)S(1)} %all-to-all-done.2.parts), custom_call_target="tpu_custom_call" | custom-call | bytes 786432 | tf_op jit(solution)/shard_map/pallas_call | solution.py:363
  86.6 4.1 %all-to-all-start.3 = ((bf16[32,16,256]{2,1,0:T(8,128)(2,1)}), bf16[32,16,256]{2,1,0:T(8,128)(2,1)S(1)}, u32[]{:S(2)}, u32[]{:S(2)}) async-start(bf16[32,16,256]{2,1,0:T(8,128)(2,1)} %shard_map.104.refs_4_), calls=%async_computation.3 | async-start | bytes 524288 | tf_op jit(solution)/shard_map/all_to_all | solution.py:375
  90.7 2.3 %collective-permute-done.2.refs_2_ = bf16[512,512]{1,0:T(8,128)(2,1)S(1)} collective-permute-done((bf16[512,512]{1,0:T(8,128)(2,1)}, bf16[512,512]{1,0:T(8,128)(2,1)S(1)}, u32[]{:S(2)}, u32[]{:S(2)}) %collective-permute-start.2) | collective-permute-done | bytes 524320 | tf_op jit(solution)/shard_map/ppermute | solution.py:273
  93.1 2.6 %collective-permute-done.3.refs_3_ = bf16[512,512]{1,0:T(8,128)(2,1)S(1)} collective-permute-done((bf16[512,512]{1,0:T(8,128)(2,1)}, bf16[512,512]{1,0:T(8,128)(2,1)S(1)}, u32[]{:S(2)}, u32[]{:S(2)}) %collective-permute-start.3) | collective-permute-done | bytes 524320 | tf_op jit(solution)/shard_map/ppermute | solution.py:273
  95.8 2.4 %fusion.8 = f32[512,1024]{1,0:T(8,128)S(1)} fusion(bf16[512,2048]{1,0:T(8,128)(2,1)S(1)} %shard_map.105, bf16[1024,2048]{1,0:T(8,128)(2,1)S(1)} %copy-done.8), kind=kOutput, calls=%fused_computation.20 | convolution fusion | flops 2147483648 | bytes 8388608 | tf_op jit(solution)/shard_map/dot_general | solution.py:281
  98.4 4.5 %all-to-all-done.3 = bf16[32,16,256]{2,1,0:T(8,128)(2,1)S(1)} async-done(((bf16[32,16,256]{2,1,0:T(8,128)(2,1)}), bf16[32,16,256]{2,1,0:T(8,128)(2,1)S(1)}, u32[]{:S(2)}, u32[]{:S(2)}) %all-to-all-start.3) | async-done | bytes 262176 | tf_op jit(solution)/shard_map/all_to_all | solution.py:375
  105.4 3.0 %collective-permute-start.14 = (bf16[256,256]{1,0:T(8,128)(2,1)S(1)}, bf16[256,256]{1,0:T(8,128)(2,1)S(1)}, u32[]{:S(2)}, u32[]{:S(2)}) collective-permute-start(bf16[256,256]{1,0:T(8,128)(2,1)S(1)} %get-tuple-element.51), channel_id=1, source_target_pairs={{0,1},{1,0},{2,3},{3,2},{4,5},{5,4},{6,7},{7,6},{8,9},{9,8},{10,11... | collective-permute-start | bytes 393224 | tf_op jit(solution)/shard_map/ppermute | solution.py:273
  110.4 4.6 %collective-permute-done.16 = bf16[256,256]{1,0:T(8,128)(2,1)S(1)} collective-permute-done((bf16[256,256]{1,0:T(8,128)(2,1)S(1)}, bf16[256,256]{1,0:T(8,128)(2,1)S(1)}, u32[]{:S(2)}, u32[]{:S(2)}) %collective-permute-start.16) | collective-permute-done | bytes 131104 | tf_op jit(solution)/shard_map/ppermute | solution.py:273
  122.8 4.1 %collective-permute-done.18 = bf16[256,512]{1,0:T(8,128)(2,1)S(1)} collective-permute-done((bf16[256,512]{1,0:T(8,128)(2,1)S(1)}, bf16[256,512]{1,0:T(8,128)(2,1)S(1)}, u32[]{:S(2)}, u32[]{:S(2)}) %collective-permute-start.18) | collective-permute-done | bytes 262176 | tf_op jit(solution)/shard_map/ppermute | solution.py:387
  126.9 3.5 %collective-permute-done.17 = bf16[256,512]{1,0:T(8,128)(2,1)S(1)} collective-permute-done((bf16[256,512]{1,0:T(8,128)(2,1)S(1)}, bf16[256,512]{1,0:T(8,128)(2,1)S(1)}, u32[]{:S(2)}, u32[]{:S(2)}) %collective-permute-start.17) | collective-permute-done | bytes 262176 | tf_op jit(solution)/shard_map/ppermute | solution.py:387
  (69 shorter events, 23.3 us)
Async XLA Ops:
  1.7 22.4 %all-to-all-start = ((bf16[32,16,256]{2,1,0:T(8,128)(2,1)}), bf16[32,16,256]{2,1,0:T(8,128)(2,1)S(1)}, u32[]{:S(2)}, u32[]{:S(2)}) async-start(bf16[32,16,256]{2,1,0:T(8,128)(2,1)} %bitcast.12), calls=%async_computation | async-start | bytes 524288 | tf_op jit(solution)/shard_map/all_to_all | solution.py:312
  11.8 20.2 %collective-permute-start = (bf16[512,256]{1,0:T(8,128)(2,1)}, bf16[512,256]{1,0:T(8,128)(2,1)S(1)}, u32[]{:S(2)}, u32[]{:S(2)}) collective-permute-start(bf16[512,256]{1,0:T(8,128)(2,1)} %shard_map.100.own), channel_id=1, source_target_pairs={{0,8},{8,16},{16,24},{24,32},{32,40},{40,48},{48,56},{56,64},{64,7... | collective-permute-start | bytes 786440 | tf_op jit(solution)/shard_map/ppermute | solution.py:311
  16.6 38.9 %collective-permute-start.4 = (bf16[512,768]{1,0:T(8,128)(2,1)}, bf16[512,768]{1,0:T(8,128)(2,1)}, u32[]{:S(2)}, u32[]{:S(2)}) collective-permute-start(bf16[512,768]{1,0:T(8,128)(2,1)} %get-tuple-element.31), channel_id=1, source_target_pairs={{0,1},{1,0},{2,3},{3,2},{4,5},{5,4},{6,7},{7,6},{8,9},{9,8},{10,11... | collective-permute-start | bytes 2359304 | tf_op jit(solution)/shard_map/ppermute | solution.py:273
  18.1 38.0 %collective-permute-start.5 = (bf16[512,768]{1,0:T(8,128)(2,1)}, bf16[512,768]{1,0:T(8,128)(2,1)}, u32[]{:S(2)}, u32[]{:S(2)}) collective-permute-start(bf16[512,768]{1,0:T(8,128)(2,1)} %get-tuple-element.32), channel_id=1, source_target_pairs={{0,2},{1,3},{2,0},{3,1},{4,6},{5,7},{6,4},{7,5},{8,10},{9,11},{10,... | collective-permute-start | bytes 2359304 | tf_op jit(solution)/shard_map/ppermute | solution.py:273
  20.8 38.7 %collective-permute-start.6 = (bf16[512,768]{1,0:T(8,128)(2,1)}, bf16[512,768]{1,0:T(8,128)(2,1)}, u32[]{:S(2)}, u32[]{:S(2)}) collective-permute-start(bf16[512,768]{1,0:T(8,128)(2,1)} %get-tuple-element.33), channel_id=1, source_target_pairs={{0,3},{1,2},{2,1},{3,0},{4,7},{5,6},{6,5},{7,4},{8,11},{9,10},{10,... | collective-permute-start | bytes 2359304 | tf_op jit(solution)/shard_map/ppermute | solution.py:273
  25.9 23.9 %all-to-all-start.1 = ((bf16[32,2,16,256]{3,2,1,0:T(8,128)(2,1)}), bf16[32,2,16,256]{3,2,1,0:T(8,128)(2,1)}, u32[]{:S(2)}, u32[]{:S(2)}) async-start(bf16[32,2,16,256]{3,2,1,0:T(8,128)(2,1)} %shard_map.102), calls=%async_computation.1 | async-start | bytes 1048576 | tf_op jit(solution)/shard_map/all_to_all | solution.py:322
  59.5 10.0 %collective-permute-start.7 = (bf16[512,768]{1,0:T(8,128)(2,1)}, bf16[512,768]{1,0:T(8,128)(2,1)S(1)}, u32[]{:S(2)}, u32[]{:S(2)}) collective-permute-start(bf16[512,768]{1,0:T(8,128)(2,1)} %collective-permute-done.4.refs_0_), channel_id=1, source_target_pairs={{0,8},{8,0},{16,24},{24,16},{32,40},{40,32},{48,56},{56,48},{64,72... | collective-permute-start | bytes 2359304 | tf_op jit(solution)/shard_map/ppermute | solution.py:360
  59.5 25.2 %all-to-all-start.2 = ((bf16[32,2,16,256]{3,2,1,0:T(8,128)(2,1)}), bf16[32,2,16,256]{3,2,1,0:T(8,128)(2,1)S(1)}, u32[]{:S(2)}, u32[]{:S(2)}) async-start(bf16[32,2,16,256]{3,2,1,0:T(8,128)(2,1)} %get-tuple-element.29), calls=%async_computation.2 | async-start | bytes 1048576 | tf_op jit(solution)/shard_map/all_to_all | solution.py:358
  67.0 5.3 %collective-permute-start.8 = (bf16[512,768]{1,0:T(8,128)(2,1)}, bf16[512,768]{1,0:T(8,128)(2,1)S(1)}, u32[]{:S(2)}, u32[]{:S(2)}) collective-permute-start(bf16[512,768]{1,0:T(8,128)(2,1)} %collective-permute-done.5.refs_1_), channel_id=1, source_target_pairs={{0,8},{8,0},{16,24},{24,16},{32,40},{40,32},{48,56},{56,48},{64,72... | collective-permute-start | bytes 2359304 | tf_op jit(solution)/shard_map/ppermute | solution.py:360
  67.3 6.0 %collective-permute-start.9 = (bf16[512,768]{1,0:T(8,128)(2,1)}, bf16[512,768]{1,0:T(8,128)(2,1)}, u32[]{:S(2)}, u32[]{:S(2)}) collective-permute-start(bf16[512,768]{1,0:T(8,128)(2,1)} %collective-permute-done.6.refs_2_), channel_id=1, source_target_pairs={{0,8},{8,0},{16,24},{24,16},{32,40},{40,32},{48,56},{56,48},{64,72... | collective-permute-start | bytes 2359304 | tf_op jit(solution)/shard_map/ppermute | solution.py:360
  67.6 23.1 %collective-permute-start.1 = (bf16[512,512]{1,0:T(8,128)(2,1)}, bf16[512,512]{1,0:T(8,128)(2,1)S(1)}, u32[]{:S(2)}, u32[]{:S(2)}) collective-permute-start(bf16[512,512]{1,0:T(8,128)(2,1)} %get-tuple-element.30.refs_0_), channel_id=1, source_target_pairs={{0,1},{1,0},{2,3},{3,2},{4,5},{5,4},{6,7},{7,6},{8,9},{9,8},{10,11... | collective-permute-start | bytes 1572872 | tf_op jit(solution)/shard_map/ppermute | solution.py:273
  67.6 25.4 %collective-permute-start.2 = (bf16[512,512]{1,0:T(8,128)(2,1)}, bf16[512,512]{1,0:T(8,128)(2,1)S(1)}, u32[]{:S(2)}, u32[]{:S(2)}) collective-permute-start(bf16[512,512]{1,0:T(8,128)(2,1)} %get-tuple-element.30.refs_0_), channel_id=1, source_target_pairs={{0,2},{1,3},{2,0},{3,1},{4,6},{5,7},{6,4},{7,5},{8,10},{9,11},{10,... | collective-permute-start | bytes 1572872 | tf_op jit(solution)/shard_map/ppermute | solution.py:273
  69.6 26.1 %collective-permute-start.3 = (bf16[512,512]{1,0:T(8,128)(2,1)}, bf16[512,512]{1,0:T(8,128)(2,1)S(1)}, u32[]{:S(2)}, u32[]{:S(2)}) collective-permute-start(bf16[512,512]{1,0:T(8,128)(2,1)} %get-tuple-element.30.refs_0_), channel_id=1, source_target_pairs={{0,3},{1,2},{2,1},{3,0},{4,7},{5,6},{6,5},{7,4},{8,11},{9,10},{10,... | collective-permute-start | bytes 1572872 | tf_op jit(solution)/shard_map/ppermute | solution.py:273
  73.2 22.4 %copy-start = (bf16[512,512]{1,0:T(8,128)(2,1)S(1)}, bf16[512,512]{1,0:T(8,128)(2,1)}, u32[]{:S(2)}) copy-start(bf16[512,512]{1,0:T(8,128)(2,1)} %get-tuple-element.30.refs_0_) | copy-start | bytes 1572868
  73.2 29.6 %collective-permute-start.10 = (bf16[512,256]{1,0:T(8,128)(2,1)}, bf16[512,256]{1,0:T(8,128)(2,1)}, u32[]{:S(2)}, u32[]{:S(2)}) collective-permute-start(bf16[512,256]{1,0:T(8,128)(2,1)} %get-tuple-element.42), channel_id=1, source_target_pairs={{0,248},{8,0},{16,8},{24,16},{32,24},{40,32},{48,40},{56,48},{64,5... | collective-permute-start | bytes 786440 | tf_op jit(solution)/shard_map/ppermute | solution.py:340
  86.6 16.3 %all-to-all-start.3 = ((bf16[32,16,256]{2,1,0:T(8,128)(2,1)}), bf16[32,16,256]{2,1,0:T(8,128)(2,1)S(1)}, u32[]{:S(2)}, u32[]{:S(2)}) async-start(bf16[32,16,256]{2,1,0:T(8,128)(2,1)} %shard_map.104.refs_4_), calls=%async_computation.3 | async-start | bytes 524288 | tf_op jit(solution)/shard_map/all_to_all | solution.py:375
  104.0 11.1 %collective-permute-start.16 = (bf16[256,256]{1,0:T(8,128)(2,1)S(1)}, bf16[256,256]{1,0:T(8,128)(2,1)S(1)}, u32[]{:S(2)}, u32[]{:S(2)}) collective-permute-start(bf16[256,256]{1,0:T(8,128)(2,1)S(1)} %get-tuple-element.51), channel_id=1, source_target_pairs={{0,3},{1,2},{2,1},{3,0},{4,7},{5,6},{6,5},{7,4},{8,11},{9,10},{10,... | collective-permute-start | bytes 393224 | tf_op jit(solution)/shard_map/ppermute | solution.py:273
  104.8 10.3 %collective-permute-start.15 = (bf16[256,256]{1,0:T(8,128)(2,1)S(1)}, bf16[256,256]{1,0:T(8,128)(2,1)S(1)}, u32[]{:S(2)}, u32[]{:S(2)}) collective-permute-start(bf16[256,256]{1,0:T(8,128)(2,1)S(1)} %get-tuple-element.51), channel_id=1, source_target_pairs={{0,2},{1,3},{2,0},{3,1},{4,6},{5,7},{6,4},{7,5},{8,10},{9,11},{10,... | collective-permute-start | bytes 393224 | tf_op jit(solution)/shard_map/ppermute | solution.py:273
  105.4 9.7 %collective-permute-start.14 = (bf16[256,256]{1,0:T(8,128)(2,1)S(1)}, bf16[256,256]{1,0:T(8,128)(2,1)S(1)}, u32[]{:S(2)}, u32[]{:S(2)}) collective-permute-start(bf16[256,256]{1,0:T(8,128)(2,1)S(1)} %get-tuple-element.51), channel_id=1, source_target_pairs={{0,1},{1,0},{2,3},{3,2},{4,5},{5,4},{6,7},{7,6},{8,9},{9,8},{10,11... | collective-permute-start | bytes 393224 | tf_op jit(solution)/shard_map/ppermute | solution.py:273
  108.4 10.2 %collective-permute-start.13 = (bf16[256,256]{1,0:T(8,128)(2,1)S(1)}, bf16[256,256]{1,0:T(8,128)(2,1)S(1)}, u32[]{:S(2)}, u32[]{:S(2)}) collective-permute-start(bf16[256,256]{1,0:T(8,128)(2,1)S(1)} %get-tuple-element.52), channel_id=1, source_target_pairs={{0,3},{1,2},{2,1},{3,0},{4,7},{5,6},{6,5},{7,4},{8,11},{9,10},{10,... | collective-permute-start | bytes 393224 | tf_op jit(solution)/shard_map/ppermute | solution.py:273
  108.8 9.7 %collective-permute-start.12 = (bf16[256,256]{1,0:T(8,128)(2,1)S(1)}, bf16[256,256]{1,0:T(8,128)(2,1)S(1)}, u32[]{:S(2)}, u32[]{:S(2)}) collective-permute-start(bf16[256,256]{1,0:T(8,128)(2,1)S(1)} %get-tuple-element.52), channel_id=1, source_target_pairs={{0,2},{1,3},{2,0},{3,1},{4,6},{5,7},{6,4},{7,5},{8,10},{9,11},{10,... | collective-permute-start | bytes 393224 | tf_op jit(solution)/shard_map/ppermute | solution.py:273
  115.0 5.0 %collective-permute-start.11 = (bf16[256,256]{1,0:T(8,128)(2,1)S(1)}, bf16[256,256]{1,0:T(8,128)(2,1)S(1)}, u32[]{:S(2)}, u32[]{:S(2)}) collective-permute-start(bf16[256,256]{1,0:T(8,128)(2,1)S(1)} %get-tuple-element.52), channel_id=1, source_target_pairs={{0,1},{1,0},{2,3},{3,2},{4,5},{5,4},{6,7},{7,6},{8,9},{9,8},{10,11... | collective-permute-start | bytes 393224 | tf_op jit(solution)/shard_map/ppermute | solution.py:273
  116.8 10.1 %collective-permute-start.18 = (bf16[256,512]{1,0:T(8,128)(2,1)S(1)}, bf16[256,512]{1,0:T(8,128)(2,1)S(1)}, u32[]{:S(2)}, u32[]{:S(2)}) collective-permute-start(bf16[256,512]{1,0:T(8,128)(2,1)S(1)} %fusion.1), channel_id=1, source_target_pairs={{0,4},{1,5},{2,6},{3,7},{4,0},{5,1},{6,2},{7,3},{8,12},{9,13},{10,... | collective-permute-start | bytes 786440 | tf_op jit(solution)/shard_map/ppermute | solution.py:387
  120.5 9.9 %collective-permute-start.17 = (bf16[256,512]{1,0:T(8,128)(2,1)S(1)}, bf16[256,512]{1,0:T(8,128)(2,1)S(1)}, u32[]{:S(2)}, u32[]{:S(2)}) collective-permute-start(bf16[256,512]{1,0:T(8,128)(2,1)S(1)} %fusion), channel_id=1, source_target_pairs={{0,4},{1,5},{2,6},{3,7},{4,0},{5,1},{6,2},{7,3},{8,12},{9,13},{10,... | collective-permute-start | bytes 786440 | tf_op jit(solution)/shard_map/ppermute | solution.py:387
  (11 other events, 84.4 us)
